TPU v7x, 256 devices: a whole 4x4x8 slice. The times are simulated.
256 devices in a mesh: row: 16 (over z_hi, x), col: 16 (over z_lo, y, core).
Axes of the slice: x: 4, y: 4, z: 8 (z_hi: 4, z_lo: 2; z = z_hi * 2 + z_lo), core: 2. Of those that a mesh axis runs over, the one named last changes fastest.
Arguments:
- embeddings: float32 [32768, 512], P(('row', 'col')), may hold values from -6 to 6
- margin: int32 [32768], P(('row', 'col')), may hold values from 0 to 99
- group: int32 [32768], P(('row', 'col')), may hold values from 0 to 7
Outputs:
- updated: float32 [32768, 512], P(('row', 'col'))
All inputs are finite; a program needn't handle non-finite values.
Results may differ from a plain program's by a relative error of at most 0.005.
Values may be sent and summed in bfloat16 or wider, within the bound.
No kernel may reach another device: no remote copies, remote signals or barrier semaphores. Data moves between devices by JAX's collectives and lax.ppermute only.
A program may use at most 64 MiB of HBM per device.

v0:
```python
import math

import jax
import jax.numpy as jnp
from jax import lax
from jax.sharding import PartitionSpec as P


def per_device(embeddings, margin, group):
    width = embeddings.shape[1]
    classes = embeddings.shape[0] * lax.axis_size("row") * lax.axis_size("col")
    lengths = jnp.sqrt(jnp.sum(embeddings * embeddings, axis=1) + 1e-06)
    unit_rows = embeddings / lengths[:, None]
    unit_half = unit_rows.astype(jnp.bfloat16)
    col_units, col_margin, col_group = (
        lax.all_gather(unit_half, "row", axis=0, tiled=True),
        lax.all_gather(margin, "row", axis=0, tiled=True),
        lax.all_gather(group, "row", axis=0, tiled=True),
    )
    cosine = lax.dot_general(
        lax.all_gather(unit_half, "col", axis=0, tiled=True),
        col_units,
        (((1,), (1,)), ((), ())),
        preferred_element_type=jnp.float32,
    )
    pair_margin = (
        lax.all_gather(margin, "col", axis=0, tiled=True)[:, None] + col_margin[None, :]
    ).astype(jnp.float32) * 0.0005
    slopes = jnp.where(
        lax.all_gather(group, "col", axis=0, tiled=True)[:, None] != col_group[None, :],
        2.0 * jax.nn.relu(cosine - pair_margin),
        0.0,
    ).astype(jnp.bfloat16)
    row_part = 2.0 * jnp.dot(slopes, col_units, preferred_element_type=jnp.float32)
    grad_units = lax.psum_scatter(row_part, "col", scatter_dimension=0, tiled=True)
    radial = jnp.sum(unit_rows * grad_units, axis=1, keepdims=True)
    grad_rows = (grad_units - unit_rows * radial) / lengths[:, None]
    step_rate = width * math.sqrt(width) / (3.0 * math.sqrt(classes))
    return embeddings - step_rate * grad_rows


def solution(mesh):
    in_specs = (P(("row", "col"), None), P(("row", "col")), P(("row", "col")))
    out_specs = P(("row", "col"), None)
    return jax.shard_map(
        per_device, mesh=mesh, in_specs=in_specs, out_specs=out_specs, check_vma=False
    )
```

profile of v0, /device:TPU:1, one launch (start us, length us, event | category | flops | bytes accessed | tf_op | source)
XLA Modules:
  0.0 215.9 jit_solution(10801326573991116214)
XLA Ops:
  6.5 0.0 all-gather.7.cloned.1.call-start
  6.5 1.1 multiply_reduce_fusion.1
  7.6 1.7 fusion.7
  9.3 0.0 all-gather.7.cloned.1.call-update
  9.3 0.0 all-gather.9.cloned.1.call-start
  9.4 0.7 all-gather.9.cloned.1.call-update
  10.1 0.0 reduce-scatter.2.cloned.1.call-start
  10.1 40.0 %all-gather.3 = s32[16,1,128]{2,1,0:T(1,128)S(1)} all-gather(s32[1,1,128]{2,1,0:T(1,128)} %bitcast.13), channel_id=1, replica_groups=mesh['row'=16,'col'=16] {'row'}, dimensions={0}, use_global_device_ids=true | all-gather | bytes 8704 | tf_op jit(solution)/shard_map/all_gather | solution.py:17
  50.1 27.1 %all-gather.2 = s32[16,1,128]{2,1,0:T(1,128)S(1)} all-gather(s32[1,1,128]{2,1,0:T(1,128)} %bitcast.14), channel_id=1, replica_groups=mesh['row'=16,'col'=16] {'col'}, dimensions={0}, use_global_device_ids=true | all-gather | bytes 8704 | tf_op jit(solution)/shard_map/all_gather | solution.py:27
  77.3 32.3 %all-gather.1 = s32[16,1,128]{2,1,0:T(1,128)S(1)} all-gather(s32[1,1,128]{2,1,0:T(1,128)} %bitcast.15), channel_id=1, replica_groups=mesh['row'=16,'col'=16] {'row'}, dimensions={0}, use_global_device_ids=true | all-gather | bytes 8704 | tf_op jit(solution)/shard_map/all_gather | solution.py:18
  109.6 21.8 %all-gather = s32[16,1,128]{2,1,0:T(1,128)S(1)} all-gather(s32[1,1,128]{2,1,0:T(1,128)} %bitcast.16), channel_id=1, replica_groups=mesh['row'=16,'col'=16] {'col'}, dimensions={0}, use_global_device_ids=true | all-gather | bytes 8704 | tf_op jit(solution)/shard_map/all_gather | solution.py:30
  131.5 0.0 all-gather.7.cloned.1.call-done
  131.5 0.0 all-gather.9.cloned.1.call-done
  131.5 14.5 %fusion.3 = f32[2048,512]{1,0:T(8,128)} fusion(bf16[2048,512]{1,0:T(8,128)(2,1)} %all-gather.9.cloned.1.call-done, s32[2048]{0:T(1024)S(1)} %bitcast.9, s32[2048]{0:T(1024)S(1)} %bitcast.10, s32[2048]{0:T(1024)S(1)} %bitcast.11, s32[2048]{0:T(1024)S(1)} %bitcast.12, bf16[2048,512]{1,0:T(8,128)(2,1)} %all-gather.7.cloned.1.call-done), kind=kOutput, calls=%fused_computation.3 | convolution fusion | flops 8628731904 | bytes 8421376 | tf_op jit(solution)/shard_map/dot_general | solution.py:34
  145.9 0.0 copy-start
  145.9 0.0 reduce-scatter.2.cloned.1.call-update
  146.0 60.5 %reduce-scatter.2.cloned.1.call-done = f32[128,512]{1,0:T(8,128)} async-done(((f32[2048,512]{1,0:T(8,128)}), f32[128,512]{1,0:T(8,128)}) %reduce-scatter.2.cloned.1.call-update) | async-done | bytes 262160 | tf_op jit(solution)/shard_map/reduce_scatter | solution.py:35
  206.4 0.0 copy-done
  206.4 1.1 multiply_reduce_fusion
  207.6 1.8 multiply_subtract_fusion
  (1 shorter events, 0.0 us)
Async XLA Ops:
  6.5 124.9 %all-gather.7.cloned.1.call-start = ((), (), s32[]{:S(2)}) async-start(), calls=%async_computation.1 | async-start | bytes 2228224 | tf_op jit(solution)/shard_map/all_gather | solution.py:21
  9.3 122.1 %all-gather.9.cloned.1.call-start = ((), (), s32[]{:S(2)}) async-start(), calls=%async_computation.2 | async-start | bytes 2228224 | tf_op jit(solution)/shard_map/all_gather | solution.py:16
  10.1 196.3 %reduce-scatter.2.cloned.1.call-start = ((), (), s32[]{:S(2)}) async-start(), calls=%async_computation.3 | async-start | bytes 4456448 | tf_op jit(solution)/shard_map/reduce_scatter | solution.py:35
  145.9 60.5 %copy-start = (f32[128,512]{1,0:T(8,128)S(1)}, f32[128,512]{1,0:T(8,128)}, u32[]{:S(2)}) copy-start(f32[128,512]{1,0:T(8,128)} %param.3) | copy-start | bytes 786436
Sparse Core Ops, SparseCore 0:
  9.5 40.7 all-gather.6
  52.6 58.1 all-gather.8
  146.1 60.2 reduce-scatter.1
where the time goes:
time: 219 us; the launch traced here: 216 us
  blocking collectives  121 us (55%)
  waiting for transfers between devices  61.2 us (28%)
  matrix products  14.5 us (7%)
  between operations  13.1 us (6%)
  other arithmetic  5.69 us (3%)
    reduce_scatter x1, waiting for transfers between devices, per_device(): lax.psum_scatter(row_part, 'col', scatter_dimension=0, tiled=True)  60.5 us
    all_gather x1, blocking collectives, per_device(): lax.all_gather(margin, 'row', axis=0, tiled=True)  40 us
    all_gather x1, blocking collectives, per_device(): lax.all_gather(group, 'row', axis=0, tiled=True)  32.3 us
    all_gather x1, blocking collectives, per_device(): lax.all_gather(margin, 'col', axis=0, tiled=True)[:, None]  27.1 us
    all_gather x1, blocking collectives, per_device(): lax.all_gather(group, 'col', axis=0, tiled=True)[:, None]  21.8 us
    dot_general x1, matrix products, per_device(): jnp.dot(slopes, col_units, preferred_element_type=jnp.float32)  14.5 us
  transfers between devices with their start and end apart: 3, of which 1 were waited for; matrix products, arithmetic and copies ran while one was open for 0% of the time, Pallas kernels for 0%

commit v1 on v0

v1 whole, which is shorter than its diff:
```python
import functools
import itertools
import math

import jax
import jax.numpy as jnp
from jax import lax
from jax.experimental import pallas as pl
from jax.experimental.pallas import tpu as pltpu
from jax.sharding import PartitionSpec as P

BF = jnp.bfloat16
F32 = jnp.float32
D = 512
CPD = 128
HALF = CPD // 2
META = 16
LANES = 128
CHUNKS = D // LANES
ROWS_R = CHUNKS * CPD + META
ROWS_C = CHUNKS * HALF + META
AXES = ("row", "col")
VMEM = pl.BlockSpec(memory_space=pltpu.VMEM)
ANY = pl.BlockSpec(memory_space=pl.ANY)


def _flat(x, y, z, core):
    return ((((z // 2) * 4 + x) * 2 + z % 2) * 4 + y) * 2 + core


LINKS = {
    "xa": lambda x, y, z: (x ^ 1, y, z),
    "xb": lambda x, y, z: (3 - x, y, z),
    "ya": lambda x, y, z: (x, y ^ 1, z),
    "yb": lambda x, y, z: (x, 3 - y, z),
    "za": lambda x, y, z: (x, y, z ^ 1),
    "zb": lambda x, y, z: (x, y, (z - 1) % 8 if z % 2 == 0 else (z + 1) % 8),
}
RING = ("xa", "ya", "xb", "yb")


def swap(block, link0, link1):
    pairs = []
    for x, y, z, core in itertools.product(range(4), range(4), range(8), range(2)):
        pairs.append((_flat(x, y, z, core), _flat(*LINKS[(link0, link1)[core]](x, y, z), core)))
    return lax.ppermute(block, AXES, pairs)


def swap_cores(block):
    return lax.ppermute(block, AXES, [(i, i ^ 1) for i in range(256)])


def pack_kernel(emb, margin, group, whole, first, second):
    e = emb[...]
    unit = (e / jnp.sqrt(jnp.sum(e * e, axis=1, keepdims=True) + 1e-06)).astype(BF)
    row = lax.broadcasted_iota(jnp.int32, (META, LANES), 0)
    meta = jnp.where(row == 0, margin[...], jnp.where(row == 1, group[...], 0)).astype(F32).astype(BF)
    for f in range(CHUNKS):
        part = unit[:, f * LANES : (f + 1) * LANES]
        whole[f * CPD : (f + 1) * CPD, :] = part
        first[f * HALF : (f + 1) * HALF, :] = part[:HALF]
        second[f * HALF : (f + 1) * HALF, :] = part[HALF:]
    whole[CHUNKS * CPD :, :] = meta
    first[CHUNKS * HALF :, :] = meta
    second[CHUNKS * HALF :, :] = meta


def pack(embeddings, margin, group):
    shapes = [jax.ShapeDtypeStruct((r, LANES), BF) for r in (ROWS_R, ROWS_C, ROWS_C)]
    return pl.pallas_call(
        pack_kernel,
        out_shape=shapes,
        in_specs=[VMEM] * 3,
        out_specs=[VMEM] * 3,
        name="pack",
    )(embeddings, margin.reshape(1, CPD), group.reshape(1, CPD))


TILE = 1024


def pair_kernel(n_r, n_c, *refs):
    r_in, c_in, rest = refs[:n_r], refs[n_r : n_r + n_c], refs[n_r + n_c :]
    outs = rest[:n_r]
    rbuf, rmeta, cbuf, cmeta, rm, rg, acc, r_sem, c_sem = rest[n_r:]
    tiles = n_c // 2
    r_copies, c_copies = [], []
    at = 0
    for i, ref in enumerate(r_in):
        n = ref.shape[0]
        own = [
            pltpu.make_async_copy(
                ref.at[:, f * CPD : (f + 1) * CPD, :],
                rbuf.at[at : at + n, :, f * LANES : (f + 1) * LANES],
                r_sem.at[i, f],
            )
            for f in range(CHUNKS)
        ]
        own.append(pltpu.make_async_copy(ref.at[:, CHUNKS * CPD :, :], rmeta.at[at : at + n], r_sem.at[i, CHUNKS]))
        r_copies += own
        at += n

    def c_copy(ref, t, h):
        own = [
            pltpu.make_async_copy(
                ref.at[:, f * HALF : (f + 1) * HALF, :],
                cbuf.at[pl.ds(t * 8, 8), h * HALF : (h + 1) * HALF, f * LANES : (f + 1) * LANES],
                c_sem.at[t, h, f],
            )
            for f in range(CHUNKS)
        ]
        own.append(
            pltpu.make_async_copy(ref.at[:, CHUNKS * HALF :, :], cmeta.at[h, pl.ds(t * 8, 8)], c_sem.at[t, h, CHUNKS])
        )
        return own

    for c in r_copies:
        c.start()
    for t in range(tiles):
        for h in range(2):
            for c in c_copy(c_in[2 * t + h], t, h):
                c.start()
    for c in r_copies:
        c.wait()
    for k in range(at):
        m = rmeta[k].astype(F32)
        rm[k * CPD : (k + 1) * CPD, :] = jnp.broadcast_to(m[0:1] * 0.0005, (CPD, CPD)).T
        rg[k * CPD : (k + 1) * CPD, :] = jnp.broadcast_to(m[1:2], (CPD, CPD)).T
    acc[...] = jnp.zeros_like(acc)
    lane = lax.broadcasted_iota(jnp.int32, (1, LANES), 1)

    def body(t, carry):
        for h in range(2):
            for c in c_copy(c_in[h], t, h):
                c.wait()
        ct = cbuf[pl.ds(t * 8, 8)].reshape(TILE, D)
        margins, groups = [], []
        for k in range(8):
            m0 = cmeta[0, t * 8 + k].astype(F32)
            m1 = cmeta[1, t * 8 + k].astype(F32)
            margins.append(jnp.where(lane < HALF, m0[0:1], m1[0:1]) * 0.0005)
            groups.append(jnp.where(lane < HALF, m0[1:2], m1[1:2]))
        for r0 in range(0, at * CPD, 256):
            rt = rbuf[r0 // CPD : r0 // CPD + 2].reshape(256, D)
            cos = lax.dot_general(rt, ct, (((1,), (1,)), ((), ())), preferred_element_type=F32)
            parts = []
            for k in range(8):
                over = jnp.maximum(cos[:, k * LANES : (k + 1) * LANES] - rm[r0 : r0 + 256, :] - margins[k], 0.0)
                parts.append(jnp.where(rg[r0 : r0 + 256, :] != groups[k], over, 0.0).astype(BF))
            s = jnp.concatenate(parts, axis=1)
            acc[r0 : r0 + 256, :] += jnp.dot(s, ct, preferred_element_type=F32)
        return carry

    lax.fori_loop(0, tiles, body, 0)
    o = 0
    for out in outs:
        n = out.shape[0]
        out[...] = acc[o : o + n, :].astype(out.dtype)
        o += n


def pair(r_in, c_in, out_dtype):
    blocks = sum(a.shape[0] for a in r_in)
    rows, n_c = blocks * CPD, len(c_in)
    tiles = n_c // 2
    return pl.pallas_call(
        functools.partial(pair_kernel, len(r_in), n_c),
        out_shape=[jax.ShapeDtypeStruct((a.shape[0] * CPD, D), out_dtype) for a in r_in],
        in_specs=[ANY] * (len(r_in) + n_c),
        out_specs=[VMEM] * len(r_in),
        scratch_shapes=[
            pltpu.VMEM((blocks, CPD, D), BF),
            pltpu.VMEM((blocks, META, LANES), BF),
            pltpu.VMEM((tiles * 8, CPD, D), BF),
            pltpu.VMEM((2, tiles * 8, META, LANES), BF),
            pltpu.VMEM((rows, CPD), F32),
            pltpu.VMEM((rows, CPD), F32),
            pltpu.VMEM((rows, D), F32),
            pltpu.SemaphoreType.DMA((len(r_in), CHUNKS + 1)),
            pltpu.SemaphoreType.DMA((tiles, 2, CHUNKS + 1)),
        ],
        compiler_params=pltpu.CompilerParams(vmem_limit_bytes=40 << 20),
        cost_estimate=pl.CostEstimate(
            flops=4 * rows * tiles * TILE * D, bytes_accessed=(tiles * TILE + rows) * D * 2, transcendentals=0
        ),
        name="pair",
    )(*r_in, *c_in)


def final_kernel(rate, emb, own, arrived, out):
    e = emb[...]
    lengths = jnp.sqrt(jnp.sum(e * e, axis=1, keepdims=True) + 1e-06)
    unit = e / lengths
    grad = 4.0 * (own[...] + arrived[...].astype(F32))
    radial = jnp.sum(unit * grad, axis=1, keepdims=True)
    out[...] = e - rate * ((grad - unit * radial) / lengths)


def per_device(embeddings, margin, group):
    classes = embeddings.shape[0] * lax.axis_size("row") * lax.axis_size("col")
    whole, first, second = pack(embeddings, margin, group)

    def cat(a, b):
        return jnp.concatenate([a, b], axis=0)

    z1 = cat(whole, swap(whole, "za", "zb"))
    z2 = swap(z1, "zb", "za")
    z3 = swap(z2, "za", "zb")
    z4 = swap(z3, "zb", "za")
    held = []
    for start, block in ((0, first), (2, second)):
        for s in range(3):
            block = cat(block, swap(block, RING[(start + s) % 4], RING[(start + s + 1) % 4]))
        held.append((block, swap(block, RING[(start + 3) % 4], RING[start])))
    (a0, a1), (b0, b1) = held
    c_in = [a0, b0, swap_cores(a0), swap_cores(b0), a1, b1, swap_cores(a1), swap_cores(b1)]
    c_in = [a.reshape(-1, ROWS_C, LANES) for a in c_in]
    z1, z2, z3, z4 = (a.reshape(-1, ROWS_R, LANES) for a in (z1, z2, z3, z4))

    (p4,) = pair([z4], c_in, BF)
    q = swap(p4, "zb", "za")
    p1, p2, p3 = pair([z1, z2, z3], c_in, F32)
    q = swap((p3 + q).astype(BF), "za", "zb")
    q = swap((p2 + q).astype(BF), "zb", "za")
    own = p1 + q
    q = swap(own[CPD:].astype(BF), "za", "zb")

    rate = D * math.sqrt(D) / (3.0 * math.sqrt(classes))
    return pl.pallas_call(
        functools.partial(final_kernel, rate),
        out_shape=jax.ShapeDtypeStruct((CPD, D), F32),
        in_specs=[VMEM] * 3,
        out_specs=VMEM,
        name="final",
    )(embeddings, own[:CPD], q)


def solution(mesh):
    in_specs = (P(("row", "col"), None), P(("row", "col")), P(("row", "col")))
    out_specs = P(("row", "col"), None)
    return jax.shard_map(per_device, mesh=mesh, in_specs=in_specs, out_specs=out_specs, check_vma=False)
```

time: 219 us -> 99.9 us (0.46)
  the two profiles are of different devices: /device:TPU:1 before, /device:TPU:18 now
where the time goes in v1:
time: 99.9 us; the launch traced here: 99.8 us
  waiting for transfers between devices  48.2 us (48%)
  starting transfers between devices  31.1 us (31%)
  Pallas kernels  17.5 us (18%)
  local copies, waits for them, and re-layouts  2.49 us (2%)
    ppermute x16, waiting for transfers between devices, swap(): return lax.ppermute(block, AXES, pairs)  48.2 us
    ppermute x16, starting transfers between devices, swap(): return lax.ppermute(block, AXES, pairs)  30.1 us
    pallas_call x2, Pallas kernels, pair(): pl.pallas_call(functools.partial(pair_kernel, len(r_in), n_c), out_shape=...  13.7 us
    pallas_call x1, Pallas kernels, per_device(): pl.pallas_call(functools.partial(final_kernel, rate), out_shape=jax.Shape...  2 us
  transfers between devices with their start and end apart: 20, of which 12 were waited for; matrix products, arithmetic and copies ran while one was open for 2% of the time, Pallas kernels for 9%

profile of v1, /device:TPU:18, one launch (start us, length us, event | category | flops | bytes accessed | tf_op | source)
XLA Modules:
  0.0 99.8 jit_solution(18263990283122612909)
XLA Ops:
  0.0 1.8 %pack.1 = (bf16[528,128]{1,0:T(8,128)(2,1)}, bf16[272,128]{1,0:T(8,128)(2,1)}, bf16[272,128]{1,0:T(8,128)(2,1)}) custom-call(f32[128,512]{1,0:T(8,128)} %emb.3, s32[1,128]{1,0:T(1,128)} %bitcast.34, s32[1,128]{1,0:T(1,128)} %bitcast.35), custom_call_target="tpu_custom_call" | custom-call | tf_op jit(solution)/shard_map/pack/pallas_call | solution.py:70
  1.8 0.5 collective-permute-start.3
  2.3 0.0 copy-start.1
  2.3 2.2 %collective-permute-start.6 = (bf16[272,128]{1,0:T(8,128)(2,1)}, bf16[272,128]{1,0:T(8,128)(2,1)S(1)}, u32[]{:S(2)}, u32[]{:S(2)}) collective-permute-start(bf16[272,128]{1,0:T(8,128)(2,1)} %get-tuple-element.13), channel_id=1, source_target_pairs={{0,48},{1,7},{8,56},{9,15},{64,112},{65,71},{72,120},{73,79},{128,... | collective-permute-start | bytes 208904 | tf_op jit(solution)/shard_map/ppermute | solution.py:46
  4.5 0.9 constant_dynamic-update-slice_fusion.5
  5.4 0.0 copy-start
  5.4 0.9 collective-permute-done.3
  6.3 0.0 copy-done.1
  6.3 1.4 %collective-permute-start.4 = (bf16[544,128]{1,0:T(8,128)(2,1)S(1)}, bf16[544,128]{1,0:T(8,128)(2,1)S(1)}, u32[]{:S(2)}, u32[]{:S(2)}) collective-permute-start(bf16[544,128]{1,0:T(8,128)(2,1)S(1)} %pad_maximum_fusion.2), channel_id=1, source_target_pairs={{0,2},{1,49},{8,10},{9,57},{64,66},{65,113},{72,74},{73,121},{128,... | collective-permute-start | bytes 417800 | tf_op jit(solution)/shard_map/ppermute | solution.py:46
  7.7 0.0 collective-permute-done.6
  7.7 0.0 copy-done
  7.7 0.1 collective-permute-start.7
  7.9 3.6 %collective-permute-done.4 = bf16[544,128]{1,0:T(8,128)(2,1)S(1)} collective-permute-done((bf16[544,128]{1,0:T(8,128)(2,1)S(1)}, bf16[544,128]{1,0:T(8,128)(2,1)S(1)}, u32[]{:S(2)}, u32[]{:S(2)}) %collective-permute-start.4) | collective-permute-done | bytes 139296 | tf_op jit(solution)/shard_map/ppermute | solution.py:46
  11.5 1.6 %collective-permute-start.5 = (bf16[1088,128]{1,0:T(8,128)(2,1)S(1)}, bf16[1088,128]{1,0:T(8,128)(2,1)S(1)}, u32[]{:S(2)}, u32[]{:S(2)}) collective-permute-start(bf16[1088,128]{1,0:T(8,128)(2,1)S(1)} %pad_maximum_fusion), channel_id=1, source_target_pairs={{0,48},{1,7},{8,56},{9,15},{64,112},{65,71},{72,120},{73,79},{128,... | collective-permute-start | bytes 835592 | tf_op jit(solution)/shard_map/ppermute | solution.py:46
  13.1 0.9 collective-permute-done.7
  14.0 2.3 %collective-permute-start.8 = (bf16[1088,128]{1,0:T(8,128)(2,1)S(1)}, bf16[1088,128]{1,0:T(8,128)(2,1)S(1)}, u32[]{:S(2)}, u32[]{:S(2)}) collective-permute-start(bf16[1088,128]{1,0:T(8,128)(2,1)S(1)} %pad_maximum_fusion.1), channel_id=1, source_target_pairs={{0,16},{1,3},{8,24},{9,11},{64,80},{65,67},{72,88},{73,75},{128,14... | collective-permute-start | bytes 835592 | tf_op jit(solution)/shard_map/ppermute | solution.py:46
  16.3 1.8 %collective-permute-done.5 = bf16[1088,128]{1,0:T(8,128)(2,1)S(1)} collective-permute-done((bf16[1088,128]{1,0:T(8,128)(2,1)S(1)}, bf16[1088,128]{1,0:T(8,128)(2,1)S(1)}, u32[]{:S(2)}, u32[]{:S(2)}) %collective-permute-start.5) | collective-permute-done | bytes 278560 | tf_op jit(solution)/shard_map/ppermute | solution.py:46
  18.2 0.0 copy-start.2
  18.2 0.5 collective-permute-start.11
  18.7 3.9 %collective-permute-done.8 = bf16[1088,128]{1,0:T(8,128)(2,1)S(1)} collective-permute-done((bf16[1088,128]{1,0:T(8,128)(2,1)S(1)}, bf16[1088,128]{1,0:T(8,128)(2,1)S(1)}, u32[]{:S(2)}, u32[]{:S(2)}) %collective-permute-start.8) | collective-permute-done | bytes 278560 | tf_op jit(solution)/shard_map/ppermute | solution.py:46
  22.7 2.6 %collective-permute-start.12 = (bf16[2176,128]{1,0:T(8,128)(2,1)S(1)}, bf16[2176,128]{1,0:T(8,128)(2,1)S(1)}, u32[]{:S(2)}, u32[]{:S(2)}) collective-permute-start(bf16[2176,128]{1,0:T(8,128)(2,1)S(1)} %constant_dynamic-update-slice_fusion.6), channel_id=1, source_target_pairs={{0,2},{1,49},{8,10},{9,57},{64,66},{65,113},{72,74},{73,121},{128,... | collective-permute-start | bytes 1671176 | tf_op jit(solution)/shard_map/ppermute | solution.py:46
  25.3 0.0 copy-done.2
  25.3 1.9 %collective-permute-start = (bf16[528,128]{1,0:T(8,128)(2,1)S(1)}, bf16[528,128]{1,0:T(8,128)(2,1)S(1)}, u32[]{:S(2)}, u32[]{:S(2)}) collective-permute-start(bf16[528,128]{1,0:T(8,128)(2,1)S(1)} %copy-done.2), channel_id=1, source_target_pairs={{0,8},{1,201},{8,0},{9,65},{64,72},{65,9},{72,64},{73,129},{128,13... | collective-permute-start | bytes 405512 | tf_op jit(solution)/shard_map/ppermute | solution.py:46
  27.2 3.9 %collective-permute-done = bf16[528,128]{1,0:T(8,128)(2,1)S(1)} collective-permute-done((bf16[528,128]{1,0:T(8,128)(2,1)S(1)}, bf16[528,128]{1,0:T(8,128)(2,1)S(1)}, u32[]{:S(2)}, u32[]{:S(2)}) %collective-permute-start) | collective-permute-done | bytes 135200 | tf_op jit(solution)/shard_map/ppermute | solution.py:46
  31.2 5.9 %collective-permute-start.1 = (bf16[1056,128]{1,0:T(8,128)(2,1)S(1)}, bf16[1056,128]{1,0:T(8,128)(2,1)S(1)}, u32[]{:S(2)}, u32[]{:S(2)}) collective-permute-start(bf16[1056,128]{1,0:T(8,128)(2,1)S(1)} %constant_dynamic-update-slice_fusion), channel_id=1, source_target_pairs={{0,200},{1,9},{8,64},{9,1},{64,8},{65,73},{72,128},{73,65},{128,72... | collective-permute-start | bytes 811016 | tf_op jit(solution)/shard_map/ppermute | solution.py:46
  37.1 0.0 collective-permute-start.9
  37.1 0.5 collective-permute-start.10
  37.6 0.0 collective-permute-done.11
  37.6 0.0 collective-permute-start.13
  37.6 0.0 collective-permute-done.12
  37.6 0.5 collective-permute-start.14
  38.1 4.7 %collective-permute-done.1 = bf16[1056,128]{1,0:T(8,128)(2,1)S(1)} collective-permute-done((bf16[1056,128]{1,0:T(8,128)(2,1)S(1)}, bf16[1056,128]{1,0:T(8,128)(2,1)S(1)}, u32[]{:S(2)}, u32[]{:S(2)}) %collective-permute-start.1) | collective-permute-done | bytes 270368 | tf_op jit(solution)/shard_map/ppermute | solution.py:46
  42.9 0.0 collective-permute-start.2
  42.9 8.5 %collective-permute-done.2 = bf16[1056,128]{1,0:T(8,128)(2,1)S(1)} collective-permute-done((bf16[1056,128]{1,0:T(8,128)(2,1)S(1)}, bf16[1056,128]{1,0:T(8,128)(2,1)S(1)}, u32[]{:S(2)}, u32[]{:S(2)}) %collective-permute-start.2) | collective-permute-done | bytes 270368 | tf_op jit(solution)/shard_map/ppermute | solution.py:46
  51.3 4.5 %collective-permute-start.15 = (bf16[1056,128]{1,0:T(8,128)(2,1)S(1)}, bf16[1056,128]{1,0:T(8,128)(2,1)S(1)}, u32[]{:S(2)}, u32[]{:S(2)}) collective-permute-start(bf16[1056,128]{1,0:T(8,128)(2,1)S(1)} %collective-permute-done.2), channel_id=1, source_target_pairs={{0,200},{1,9},{8,64},{9,1},{64,8},{65,73},{72,128},{73,65},{128,72... | collective-permute-start | bytes 811016 | tf_op jit(solution)/shard_map/ppermute | solution.py:46
  55.9 4.4 %collective-permute-done.15 = bf16[1056,128]{1,0:T(8,128)(2,1)S(1)} collective-permute-done((bf16[1056,128]{1,0:T(8,128)(2,1)S(1)}, bf16[1056,128]{1,0:T(8,128)(2,1)S(1)}, u32[]{:S(2)}, u32[]{:S(2)}) %collective-permute-start.15) | collective-permute-done | bytes 270368 | tf_op jit(solution)/shard_map/ppermute | solution.py:46
  60.3 0.0 collective-permute-done.9
  60.3 0.0 collective-permute-done.10
  60.3 0.0 collective-permute-done.13
  60.3 0.0 collective-permute-done.14
  60.3 4.4 %pair.3 = bf16[256,512]{1,0:T(8,128)(2,1)S(1)} custom-call(bf16[2,528,128]{2,1,0:T(8,128)(2,1)S(1)} %bitcast.33, bf16[8,272,128]{2,1,0:T(8,128)(2,1)S(1)} %bitcast.17, bf16[8,272,128]{2,1,0:T(8,128)(2,1)S(1)} %bitcast.15, bf16[8,272,128]{2,1,0:T(8,128)(2,1)S(1)} %bitcast.23, bf16[8,272,128]{2,1,0:T(8,128)(2,1)S(1)} %bitcast.25, ...), custom_call_target="tpu_custom_call" | custom-call | flops 2147483648 | bytes 4456448 | tf_op jit(solution)/shard_map/pair/pallas_call | solution.py:166
  64.8 3.5 %collective-permute-start.16 = (bf16[256,512]{1,0:T(8,128)(2,1)S(1)}, bf16[256,512]{1,0:T(8,128)(2,1)S(1)}, u32[]{:S(2)}, u32[]{:S(2)}) collective-permute-start(bf16[256,512]{1,0:T(8,128)(2,1)S(1)} %pair.3), channel_id=1, source_target_pairs={{0,200},{1,9},{8,64},{9,1},{64,8},{65,73},{72,128},{73,65},{128,72... | collective-permute-start | bytes 786440 | tf_op jit(solution)/shard_map/ppermute | solution.py:46
  68.3 9.2 %pair.2 = (f32[256,512]{1,0:T(8,128)S(1)}, f32[256,512]{1,0:T(8,128)S(1)}, f32[256,512]{1,0:T(8,128)S(1)}) custom-call(bf16[2,528,128]{2,1,0:T(8,128)(2,1)S(1)} %bitcast.14, bf16[2,528,128]{2,1,0:T(8,128)(2,1)S(1)} %bitcast.31, bf16[2,528,128]{2,1,0:T(8,128)(2,1)S(1)} %bitcast.32, bf16[8,272,128]{2,1,0:T(8,128)(2,1)S(1)} %bitcast.18, ...), custom_call_target="tpu_custom_call" | custom-call | flops 6442450944 | bytes 4980736 | tf_op jit(solution)/shard_map/pair/pallas_call | solution.py:166
  77.5 0.0 collective-permute-done.16
  77.5 0.1 add_convert_fusion.1
  77.6 0.1 collective-permute-start.17
  77.7 6.4 %collective-permute-done.17 = bf16[256,512]{1,0:T(8,128)(2,1)S(1)} collective-permute-done((bf16[256,512]{1,0:T(8,128)(2,1)S(1)}, bf16[256,512]{1,0:T(8,128)(2,1)S(1)}, u32[]{:S(2)}, u32[]{:S(2)}) %collective-permute-start.17) | collective-permute-done | bytes 262176 | tf_op jit(solution)/shard_map/ppermute | solution.py:46
  84.1 0.1 add_convert_fusion
  84.2 2.9 %collective-permute-start.18 = (bf16[256,512]{1,0:T(8,128)(2,1)S(1)}, bf16[256,512]{1,0:T(8,128)(2,1)S(1)}, u32[]{:S(2)}, u32[]{:S(2)}) collective-permute-start(bf16[256,512]{1,0:T(8,128)(2,1)S(1)} %add_convert_fusion), channel_id=1, source_target_pairs={{0,200},{1,9},{8,64},{9,1},{64,8},{65,73},{72,128},{73,65},{128,72... | collective-permute-start | bytes 786440 | tf_op jit(solution)/shard_map/ppermute | solution.py:46
  87.0 4.9 %collective-permute-done.18 = bf16[256,512]{1,0:T(8,128)(2,1)S(1)} collective-permute-done((bf16[256,512]{1,0:T(8,128)(2,1)S(1)}, bf16[256,512]{1,0:T(8,128)(2,1)S(1)}, u32[]{:S(2)}, u32[]{:S(2)}) %collective-permute-start.18) | collective-permute-done | bytes 262176 | tf_op jit(solution)/shard_map/ppermute | solution.py:46
  91.9 0.1 convert_add_fusion
  92.0 0.1 collective-permute-start.19
  92.1 0.7 slice.9.own
  92.9 4.2 %collective-permute-done.19.arrived = bf16[128,512]{1,0:T(8,128)(2,1)S(1)} collective-permute-done((bf16[128,512]{1,0:T(8,128)(2,1)S(1)}, bf16[128,512]{1,0:T(8,128)(2,1)S(1)}, u32[]{:S(2)}, u32[]{:S(2)}) %collective-permute-start.19) | collective-permute-done | bytes 131104 | tf_op jit(solution)/shard_map/ppermute | solution.py:46
  97.1 0.0 copy-start.3
  97.1 0.6 copy-done.3
  97.7 2.0 %final.1 = f32[128,512]{1,0:T(8,128)} custom-call(f32[128,512]{1,0:T(8,128)} %emb.3, f32[128,512]{1,0:T(8,128)} %slice.9.own, bf16[128,512]{1,0:T(8,128)(2,1)} %copy-done.3), custom_call_target="tpu_custom_call" | custom-call | tf_op jit(solution)/shard_map/final/pallas_call | solution.py:229
  (13 shorter events, 0.2 us)
Async XLA Ops:
  1.8 4.5 %collective-permute-start.3 = (bf16[272,128]{1,0:T(8,128)(2,1)}, bf16[272,128]{1,0:T(8,128)(2,1)S(1)}, u32[]{:S(2)}, u32[]{:S(2)}) collective-permute-start(bf16[272,128]{1,0:T(8,128)(2,1)} %get-tuple-element.12), channel_id=1, source_target_pairs={{0,16},{1,3},{8,24},{9,11},{64,80},{65,67},{72,88},{73,75},{128,14... | collective-permute-start | bytes 208904 | tf_op jit(solution)/shard_map/ppermute | solution.py:46
  2.3 4.0 %copy-start.1 = (bf16[272,128]{1,0:T(8,128)(2,1)S(1)}, bf16[272,128]{1,0:T(8,128)(2,1)}, u32[]{:S(2)}) copy-start(bf16[272,128]{1,0:T(8,128)(2,1)} %get-tuple-element.12) | copy-start | bytes 208900
  2.3 5.4 %collective-permute-start.6 = (bf16[272,128]{1,0:T(8,128)(2,1)}, bf16[272,128]{1,0:T(8,128)(2,1)S(1)}, u32[]{:S(2)}, u32[]{:S(2)}) collective-permute-start(bf16[272,128]{1,0:T(8,128)(2,1)} %get-tuple-element.13), channel_id=1, source_target_pairs={{0,48},{1,7},{8,56},{9,15},{64,112},{65,71},{72,120},{73,79},{128,... | collective-permute-start | bytes 208904 | tf_op jit(solution)/shard_map/ppermute | solution.py:46
  5.4 2.3 %copy-start = (bf16[272,128]{1,0:T(8,128)(2,1)S(1)}, bf16[272,128]{1,0:T(8,128)(2,1)}, u32[]{:S(2)}) copy-start(bf16[272,128]{1,0:T(8,128)(2,1)} %get-tuple-element.13) | copy-start | bytes 208900
  6.3 5.1 %collective-permute-start.4 = (bf16[544,128]{1,0:T(8,128)(2,1)S(1)}, bf16[544,128]{1,0:T(8,128)(2,1)S(1)}, u32[]{:S(2)}, u32[]{:S(2)}) collective-permute-start(bf16[544,128]{1,0:T(8,128)(2,1)S(1)} %pad_maximum_fusion.2), channel_id=1, source_target_pairs={{0,2},{1,49},{8,10},{9,57},{64,66},{65,113},{72,74},{73,121},{128,... | collective-permute-start | bytes 417800 | tf_op jit(solution)/shard_map/ppermute | solution.py:46
  7.7 6.3 %collective-permute-start.7 = (bf16[544,128]{1,0:T(8,128)(2,1)S(1)}, bf16[544,128]{1,0:T(8,128)(2,1)S(1)}, u32[]{:S(2)}, u32[]{:S(2)}) collective-permute-start(bf16[544,128]{1,0:T(8,128)(2,1)S(1)} %pad_maximum_fusion.3), channel_id=1, source_target_pairs={{0,6},{1,17},{8,14},{9,25},{64,70},{65,81},{72,78},{73,89},{128,13... | collective-permute-start | bytes 417800 | tf_op jit(solution)/shard_map/ppermute | solution.py:46
  11.5 6.6 %collective-permute-start.5 = (bf16[1088,128]{1,0:T(8,128)(2,1)S(1)}, bf16[1088,128]{1,0:T(8,128)(2,1)S(1)}, u32[]{:S(2)}, u32[]{:S(2)}) collective-permute-start(bf16[1088,128]{1,0:T(8,128)(2,1)S(1)} %pad_maximum_fusion), channel_id=1, source_target_pairs={{0,48},{1,7},{8,56},{9,15},{64,112},{65,71},{72,120},{73,79},{128,... | collective-permute-start | bytes 835592 | tf_op jit(solution)/shard_map/ppermute | solution.py:46
  14.0 8.6 %collective-permute-start.8 = (bf16[1088,128]{1,0:T(8,128)(2,1)S(1)}, bf16[1088,128]{1,0:T(8,128)(2,1)S(1)}, u32[]{:S(2)}, u32[]{:S(2)}) collective-permute-start(bf16[1088,128]{1,0:T(8,128)(2,1)S(1)} %pad_maximum_fusion.1), channel_id=1, source_target_pairs={{0,16},{1,3},{8,24},{9,11},{64,80},{65,67},{72,88},{73,75},{128,14... | collective-permute-start | bytes 835592 | tf_op jit(solution)/shard_map/ppermute | solution.py:46
  18.2 7.1 %copy-start.2 = (bf16[528,128]{1,0:T(8,128)(2,1)S(1)}, bf16[528,128]{1,0:T(8,128)(2,1)}, u32[]{:S(2)}) copy-start(bf16[528,128]{1,0:T(8,128)(2,1)} %get-tuple-element.11) | copy-start | bytes 405508
  18.2 19.4 %collective-permute-start.11 = (bf16[2176,128]{1,0:T(8,128)(2,1)S(1)}, bf16[2176,128]{1,0:T(8,128)(2,1)S(1)}, u32[]{:S(2)}, u32[]{:S(2)}) collective-permute-start(bf16[2176,128]{1,0:T(8,128)(2,1)S(1)} %constant_dynamic-update-slice_fusion.2), channel_id=1, source_target_pairs={{0,6},{1,17},{8,14},{9,25},{64,70},{65,81},{72,78},{73,89},{128,13... | collective-permute-start | bytes 1671176 | tf_op jit(solution)/shard_map/ppermute | solution.py:46
  22.7 14.9 %collective-permute-start.12 = (bf16[2176,128]{1,0:T(8,128)(2,1)S(1)}, bf16[2176,128]{1,0:T(8,128)(2,1)S(1)}, u32[]{:S(2)}, u32[]{:S(2)}) collective-permute-start(bf16[2176,128]{1,0:T(8,128)(2,1)S(1)} %constant_dynamic-update-slice_fusion.6), channel_id=1, source_target_pairs={{0,2},{1,49},{8,10},{9,57},{64,66},{65,113},{72,74},{73,121},{128,... | collective-permute-start | bytes 1671176 | tf_op jit(solution)/shard_map/ppermute | solution.py:46
  25.3 5.9 %collective-permute-start = (bf16[528,128]{1,0:T(8,128)(2,1)S(1)}, bf16[528,128]{1,0:T(8,128)(2,1)S(1)}, u32[]{:S(2)}, u32[]{:S(2)}) collective-permute-start(bf16[528,128]{1,0:T(8,128)(2,1)S(1)} %copy-done.2), channel_id=1, source_target_pairs={{0,8},{1,201},{8,0},{9,65},{64,72},{65,9},{72,64},{73,129},{128,13... | collective-permute-start | bytes 405512 | tf_op jit(solution)/shard_map/ppermute | solution.py:46
  31.2 11.7 %collective-permute-start.1 = (bf16[1056,128]{1,0:T(8,128)(2,1)S(1)}, bf16[1056,128]{1,0:T(8,128)(2,1)S(1)}, u32[]{:S(2)}, u32[]{:S(2)}) collective-permute-start(bf16[1056,128]{1,0:T(8,128)(2,1)S(1)} %constant_dynamic-update-slice_fusion), channel_id=1, source_target_pairs={{0,200},{1,9},{8,64},{9,1},{64,8},{65,73},{72,128},{73,65},{128,72... | collective-permute-start | bytes 811016 | tf_op jit(solution)/shard_map/ppermute | solution.py:46
  37.1 23.2 %collective-permute-start.9 = (bf16[2176,128]{1,0:T(8,128)(2,1)S(1)}, bf16[2176,128]{1,0:T(8,128)(2,1)S(1)}, u32[]{:S(2)}, u32[]{:S(2)}) collective-permute-start(bf16[2176,128]{1,0:T(8,128)(2,1)S(1)} %constant_dynamic-update-slice_fusion.2), channel_id=1, source_target_pairs={{0,1},{1,0},{2,3},{3,2},{4,5},{5,4},{6,7},{7,6},{8,9},{9,8},{10,11... | collective-permute-start | bytes 1671176 | tf_op jit(solution)/shard_map/ppermute | solution.py:50
  37.1 23.2 %collective-permute-start.10 = (bf16[2176,128]{1,0:T(8,128)(2,1)S(1)}, bf16[2176,128]{1,0:T(8,128)(2,1)S(1)}, u32[]{:S(2)}, u32[]{:S(2)}) collective-permute-start(bf16[2176,128]{1,0:T(8,128)(2,1)S(1)} %constant_dynamic-update-slice_fusion.6), channel_id=1, source_target_pairs={{0,1},{1,0},{2,3},{3,2},{4,5},{5,4},{6,7},{7,6},{8,9},{9,8},{10,11... | collective-permute-start | bytes 1671176 | tf_op jit(solution)/shard_map/ppermute | solution.py:50
  37.6 22.7 %collective-permute-start.13 = (bf16[2176,128]{1,0:T(8,128)(2,1)S(1)}, bf16[2176,128]{1,0:T(8,128)(2,1)S(1)}, u32[]{:S(2)}, u32[]{:S(2)}) collective-permute-start(bf16[2176,128]{1,0:T(8,128)(2,1)S(1)} %collective-permute-done.11), channel_id=1, source_target_pairs={{0,1},{1,0},{2,3},{3,2},{4,5},{5,4},{6,7},{7,6},{8,9},{9,8},{10,11... | collective-permute-start | bytes 1671176 | tf_op jit(solution)/shard_map/ppermute | solution.py:50
  37.6 22.7 %collective-permute-start.14 = (bf16[2176,128]{1,0:T(8,128)(2,1)S(1)}, bf16[2176,128]{1,0:T(8,128)(2,1)S(1)}, u32[]{:S(2)}, u32[]{:S(2)}) collective-permute-start(bf16[2176,128]{1,0:T(8,128)(2,1)S(1)} %collective-permute-done.12), channel_id=1, source_target_pairs={{0,1},{1,0},{2,3},{3,2},{4,5},{5,4},{6,7},{7,6},{8,9},{9,8},{10,11... | collective-permute-start | bytes 1671176 | tf_op jit(solution)/shard_map/ppermute | solution.py:50
  42.9 8.5 %collective-permute-start.2 = (bf16[1056,128]{1,0:T(8,128)(2,1)S(1)}, bf16[1056,128]{1,0:T(8,128)(2,1)S(1)}, u32[]{:S(2)}, u32[]{:S(2)}) collective-permute-start(bf16[1056,128]{1,0:T(8,128)(2,1)S(1)} %collective-permute-done.1), channel_id=1, source_target_pairs={{0,8},{1,201},{8,0},{9,65},{64,72},{65,9},{72,64},{73,129},{128,13... | collective-permute-start | bytes 811016 | tf_op jit(solution)/shard_map/ppermute | solution.py:46
  51.3 9.0 %collective-permute-start.15 = (bf16[1056,128]{1,0:T(8,128)(2,1)S(1)}, bf16[1056,128]{1,0:T(8,128)(2,1)S(1)}, u32[]{:S(2)}, u32[]{:S(2)}) collective-permute-start(bf16[1056,128]{1,0:T(8,128)(2,1)S(1)} %collective-permute-done.2), channel_id=1, source_target_pairs={{0,200},{1,9},{8,64},{9,1},{64,8},{65,73},{72,128},{73,65},{128,72... | collective-permute-start | bytes 811016 | tf_op jit(solution)/shard_map/ppermute | solution.py:46
  64.8 12.7 %collective-permute-start.16 = (bf16[256,512]{1,0:T(8,128)(2,1)S(1)}, bf16[256,512]{1,0:T(8,128)(2,1)S(1)}, u32[]{:S(2)}, u32[]{:S(2)}) collective-permute-start(bf16[256,512]{1,0:T(8,128)(2,1)S(1)} %pair.3), channel_id=1, source_target_pairs={{0,200},{1,9},{8,64},{9,1},{64,8},{65,73},{72,128},{73,65},{128,72... | collective-permute-start | bytes 786440 | tf_op jit(solution)/shard_map/ppermute | solution.py:46
  77.6 6.5 %collective-permute-start.17 = (bf16[256,512]{1,0:T(8,128)(2,1)S(1)}, bf16[256,512]{1,0:T(8,128)(2,1)S(1)}, u32[]{:S(2)}, u32[]{:S(2)}) collective-permute-start(bf16[256,512]{1,0:T(8,128)(2,1)S(1)} %add_convert_fusion.1), channel_id=1, source_target_pairs={{0,8},{1,201},{8,0},{9,65},{64,72},{65,9},{72,64},{73,129},{128,13... | collective-permute-start | bytes 786440 | tf_op jit(solution)/shard_map/ppermute | solution.py:46
  84.2 7.8 %collective-permute-start.18 = (bf16[256,512]{1,0:T(8,128)(2,1)S(1)}, bf16[256,512]{1,0:T(8,128)(2,1)S(1)}, u32[]{:S(2)}, u32[]{:S(2)}) collective-permute-start(bf16[256,512]{1,0:T(8,128)(2,1)S(1)} %add_convert_fusion), channel_id=1, source_target_pairs={{0,200},{1,9},{8,64},{9,1},{64,8},{65,73},{72,128},{73,65},{128,72... | collective-permute-start | bytes 786440 | tf_op jit(solution)/shard_map/ppermute | solution.py:46
  92.0 5.1 %collective-permute-start.19 = (bf16[128,512]{1,0:T(8,128)(2,1)S(1)}, bf16[128,512]{1,0:T(8,128)(2,1)S(1)}, u32[]{:S(2)}, u32[]{:S(2)}) collective-permute-start(bf16[128,512]{1,0:T(8,128)(2,1)S(1)} %slice.12), channel_id=1, source_target_pairs={{0,8},{1,201},{8,0},{9,65},{64,72},{65,9},{72,64},{73,129},{128,13... | collective-permute-start | bytes 393224 | tf_op jit(solution)/shard_map/ppermute | solution.py:46
  97.1 0.6 copy-start.3

commit v2 on v1

--- a/solution.py
+++ b/solution.py
@@ -19,6 +19,7 @@
 CHUNKS = D // LANES
 ROWS_R = CHUNKS * CPD + META
 ROWS_C = CHUNKS * HALF + META
+SMALL = 6 << 20
 AXES = ("row", "col")
 VMEM = pl.BlockSpec(memory_space=pltpu.VMEM)
 ANY = pl.BlockSpec(memory_space=pl.ANY)
@@ -72,6 +73,7 @@
         out_shape=shapes,
         in_specs=[VMEM] * 3,
         out_specs=[VMEM] * 3,
+        compiler_params=pltpu.CompilerParams(vmem_limit_bytes=SMALL),
         name="pack",
     )(embeddings, margin.reshape(1, CPD), group.reshape(1, CPD))
 
@@ -79,10 +81,10 @@
 TILE = 1024
 
 
-def pair_kernel(n_r, n_c, *refs):
+def pair_kernel(n_r, n_c, n_sum, *refs):
     r_in, c_in, rest = refs[:n_r], refs[n_r : n_r + n_c], refs[n_r + n_c :]
-    outs = rest[:n_r]
-    rbuf, rmeta, cbuf, cmeta, rm, rg, acc, r_sem, c_sem = rest[n_r:]
+    sums, outs = rest[:n_sum], rest[n_sum : n_sum + n_r]
+    rbuf, rmeta, cbuf, cmeta, rm, rg, acc, r_sem, c_sem = rest[n_sum + n_r :]
     tiles = n_c // 2
     r_copies, c_copies = [], []
     at = 0
@@ -126,7 +128,14 @@
         m = rmeta[k].astype(F32)
         rm[k * CPD : (k + 1) * CPD, :] = jnp.broadcast_to(m[0:1] * 0.0005, (CPD, CPD)).T
         rg[k * CPD : (k + 1) * CPD, :] = jnp.broadcast_to(m[1:2], (CPD, CPD)).T
-    acc[...] = jnp.zeros_like(acc)
+    if sums:
+        o = 0
+        for ref in sums:
+            n = ref.shape[0]
+            acc[o : o + n, :] = ref[...]
+            o += n
+    else:
+        acc[...] = jnp.zeros_like(acc)
     lane = lax.broadcasted_iota(jnp.int32, (1, LANES), 1)
 
     def body(t, carry):
@@ -159,14 +168,14 @@
         o += n
 
 
-def pair(r_in, c_in, out_dtype):
+def pair(r_in, c_in, out_dtype, sums=()):
     blocks = sum(a.shape[0] for a in r_in)
     rows, n_c = blocks * CPD, len(c_in)
     tiles = n_c // 2
     return pl.pallas_call(
-        functools.partial(pair_kernel, len(r_in), n_c),
+        functools.partial(pair_kernel, len(r_in), n_c, len(sums)),
         out_shape=[jax.ShapeDtypeStruct((a.shape[0] * CPD, D), out_dtype) for a in r_in],
-        in_specs=[ANY] * (len(r_in) + n_c),
+        in_specs=[ANY] * (len(r_in) + n_c) + [VMEM] * len(sums),
         out_specs=[VMEM] * len(r_in),
         scratch_shapes=[
             pltpu.VMEM((blocks, CPD, D), BF),
@@ -179,12 +188,38 @@
             pltpu.SemaphoreType.DMA((len(r_in), CHUNKS + 1)),
             pltpu.SemaphoreType.DMA((tiles, 2, CHUNKS + 1)),
         ],
-        compiler_params=pltpu.CompilerParams(vmem_limit_bytes=40 << 20),
+        compiler_params=pltpu.CompilerParams(vmem_limit_bytes=20 << 20),
         cost_estimate=pl.CostEstimate(
             flops=4 * rows * tiles * TILE * D, bytes_accessed=(tiles * TILE + rows) * D * 2, transcendentals=0
         ),
         name="pair",
-    )(*r_in, *c_in)
+    )(*r_in, *c_in, *sums)
+
+
+def join_kernel(pieces, n_in, *refs):
+    ins, outs, sem = refs[:n_in], refs[n_in:-1], refs[-1]
+    copies = []
+    for out, (i, j) in zip(outs, pieces, strict=True):
+        n = ins[i].shape[0]
+        copies.append((ins[i], out.at[:n]))
+        copies.append((ins[j], out.at[n:]))
+    copies = [pltpu.make_async_copy(src, dst, sem.at[k]) for k, (src, dst) in enumerate(copies)]
+    for c in copies:
+        c.start()
+    for c in copies:
+        c.wait()
+
+
+def join(pieces, *ins):
+    return pl.pallas_call(
+        functools.partial(join_kernel, pieces, len(ins)),
+        out_shape=[jax.ShapeDtypeStruct((ins[i].shape[0] + ins[j].shape[0], LANES), BF) for i, j in pieces],
+        in_specs=[ANY] * len(ins),
+        out_specs=[VMEM] * len(pieces),
+        scratch_shapes=[pltpu.SemaphoreType.DMA((2 * len(pieces),))],
+        compiler_params=pltpu.CompilerParams(vmem_limit_bytes=SMALL),
+        name="join",
+    )(*ins)
 
 
 def final_kernel(rate, emb, own, arrived, out):
@@ -200,26 +235,33 @@
     classes = embeddings.shape[0] * lax.axis_size("row") * lax.axis_size("col")
     whole, first, second = pack(embeddings, margin, group)
 
-    def cat(a, b):
-        return jnp.concatenate([a, b], axis=0)
-
-    z1 = cat(whole, swap(whole, "za", "zb"))
+    def round_xy(s, a, b):
+        return swap(a, RING[s], RING[(s + 1) % 4]), swap(b, RING[(s + 2) % 4], RING[(s + 3) % 4])
+
+    z = swap(whole, "za", "zb")
+    ra, rb = round_xy(0, first, second)
+    z1, a, b = join(((0, 1), (2, 3), (4, 5)), whole, z, first, ra, second, rb)
     z2 = swap(z1, "zb", "za")
+    ra, rb = round_xy(1, a, b)
+    a, b = join(((0, 1), (2, 3)), a, ra, b, rb, z2)
     z3 = swap(z2, "za", "zb")
+    ra, rb = round_xy(2, a, b)
+    a0, b0 = join(((0, 1), (2, 3)), a, ra, b, rb, z3)
     z4 = swap(z3, "zb", "za")
-    held = []
-    for start, block in ((0, first), (2, second)):
-        for s in range(3):
-            block = cat(block, swap(block, RING[(start + s) % 4], RING[(start + s + 1) % 4]))
-        held.append((block, swap(block, RING[(start + 3) % 4], RING[start])))
-    (a0, a1), (b0, b1) = held
-    c_in = [a0, b0, swap_cores(a0), swap_cores(b0), a1, b1, swap_cores(a1), swap_cores(b1)]
-    c_in = [a.reshape(-1, ROWS_C, LANES) for a in c_in]
-    z1, z2, z3, z4 = (a.reshape(-1, ROWS_R, LANES) for a in (z1, z2, z3, z4))
-
-    (p4,) = pair([z4], c_in, BF)
+    a1, b1 = round_xy(3, a0, b0)
+
+    def cols(*arrays):
+        return [v.reshape(-1, ROWS_C, LANES) for v in arrays]
+
+    early = cols(a0, b0, swap_cores(a0), swap_cores(b0))
+    z1, z2, z3, z4 = (v.reshape(-1, ROWS_R, LANES) for v in (z1, z2, z3, z4))
+    p1, p2, p3 = pair([z1, z2, z3], early, F32)
+    z4, a1, b1, p1, p2, p3 = lax.optimization_barrier((z4, a1, b1, p1, p2, p3))
+    late = cols(a1, b1, swap_cores(a1), swap_cores(b1))
+    (p4,) = pair([z4], early, F32)
+    (p4,) = pair([z4], late, BF, [p4])
     q = swap(p4, "zb", "za")
-    p1, p2, p3 = pair([z1, z2, z3], c_in, F32)
+    p1, p2, p3 = pair([z1, z2, z3], late, F32, [p1, p2, p3])
     q = swap((p3 + q).astype(BF), "za", "zb")
     q = swap((p2 + q).astype(BF), "zb", "za")
     own = p1 + q
@@ -231,6 +273,7 @@
         out_shape=jax.ShapeDtypeStruct((CPD, D), F32),
         in_specs=[VMEM] * 3,
         out_specs=VMEM,
+        compiler_params=pltpu.CompilerParams(vmem_limit_bytes=SMALL),
         name="final",
     )(embeddings, own[:CPD], q)
 

time: 99.9 us -> 80.6 us (0.81)
  the two profiles are of different devices: /device:TPU:18 before, /device:TPU:2 now
where the time goes in v2:
time: 80.6 us; the launch traced here: 80.5 us
  waiting for transfers between devices  36.9 us (46%)
  starting transfers between devices  24 us (30%)
  Pallas kernels  17.5 us (22%)
  local copies, waits for them, and re-layouts  1.66 us (2%)
    ppermute x16, waiting for transfers between devices, swap(): return lax.ppermute(block, AXES, pairs)  36.9 us
    ppermute x16, starting transfers between devices, swap(): return lax.ppermute(block, AXES, pairs)  22.9 us
    pallas_call x4, Pallas kernels, pair(): pl.pallas_call(functools.partial(pair_kernel, len(r_in), n_c, len(sums)),...  14.8 us
    pallas_call x3, Pallas kernels, join(): pl.pallas_call(functools.partial(join_kernel, pieces, len(ins)), out_shap...  1.69 us
    unnamed x8, local copies, waits for them, and re-layouts  1.63 us
  transfers between devices with their start and end apart: 20, of which 12 were waited for; matrix products, arithmetic and copies ran while one was open for 0% of the time, Pallas kernels for 15%

profile of v2, /device:TPU:2, one launch (start us, length us, event | category | flops | bytes accessed | tf_op | source)
XLA Modules:
  0.0 80.5 jit_solution(4638294098784309809)
XLA Ops:
  0.0 0.0 copy-start.2
  0.0 0.0 copy-start.3
  0.0 0.7 copy-done.2
  0.7 0.0 copy-done.3
  0.7 0.0 copy-start
  0.7 0.9 %copy-done = f32[128,512]{1,0:T(8,128)S(1)} copy-done((f32[128,512]{1,0:T(8,128)S(1)}, f32[128,512]{1,0:T(8,128)}, u32[]{:S(2)}) %copy-start) | copy-done | bytes 262168
  1.6 0.1 pack.1
  1.8 2.0 %collective-permute-start = (bf16[528,128]{1,0:T(8,128)(2,1)S(1)}, bf16[528,128]{1,0:T(8,128)(2,1)S(1)}, u32[]{:S(2)}, u32[]{:S(2)}) collective-permute-start(bf16[528,128]{1,0:T(8,128)(2,1)S(1)} %get-tuple-element.27.refs_0_), channel_id=1, source_target_pairs={{0,8},{1,201},{8,0},{9,65},{64,72},{65,9},{72,64},{73,129},{128,13... | collective-permute-start | bytes 405512 | tf_op jit(solution)/shard_map/ppermute | solution.py:47
  3.8 0.5 collective-permute-start.1
  4.3 2.2 %collective-permute-start.2 = (bf16[272,128]{1,0:T(8,128)(2,1)S(1)}, bf16[272,128]{1,0:T(8,128)(2,1)S(1)}, u32[]{:S(2)}, u32[]{:S(2)}) collective-permute-start(bf16[272,128]{1,0:T(8,128)(2,1)S(1)} %get-tuple-element.29.refs_4_), channel_id=1, source_target_pairs={{0,48},{1,7},{8,56},{9,15},{64,112},{65,71},{72,120},{73,79},{128,... | collective-permute-start | bytes 208904 | tf_op jit(solution)/shard_map/ppermute | solution.py:47
  6.4 1.6 %collective-permute-done.1.refs_3_ = bf16[272,128]{1,0:T(8,128)(2,1)S(1)} collective-permute-done((bf16[272,128]{1,0:T(8,128)(2,1)S(1)}, bf16[272,128]{1,0:T(8,128)(2,1)S(1)}, u32[]{:S(2)}, u32[]{:S(2)}) %collective-permute-start.1) | collective-permute-done | bytes 69664 | tf_op jit(solution)/shard_map/ppermute | solution.py:47
  8.1 0.7 collective-permute-done.2.refs_5_
  8.7 0.0 collective-permute-done.refs_1_
  8.7 0.8 join.3
  9.5 5.0 %collective-permute-start.3 = (bf16[1056,128]{1,0:T(8,128)(2,1)S(1)}, bf16[1056,128]{1,0:T(8,128)(2,1)S(1)}, u32[]{:S(2)}, u32[]{:S(2)}) collective-permute-start(bf16[1056,128]{1,0:T(8,128)(2,1)S(1)} %get-tuple-element.30), channel_id=1, source_target_pairs={{0,200},{1,9},{8,64},{9,1},{64,8},{65,73},{72,128},{73,65},{128,72... | collective-permute-start | bytes 811016 | tf_op jit(solution)/shard_map/ppermute | solution.py:47
  14.5 1.6 %collective-permute-start.6 = (bf16[544,128]{1,0:T(8,128)(2,1)S(1)}, bf16[544,128]{1,0:T(8,128)(2,1)S(1)}, u32[]{:S(2)}, u32[]{:S(2)}) collective-permute-start(bf16[544,128]{1,0:T(8,128)(2,1)S(1)} %get-tuple-element.31.refs_0_), channel_id=1, source_target_pairs={{0,2},{1,49},{8,10},{9,57},{64,66},{65,113},{72,74},{73,121},{128,... | collective-permute-start | bytes 417800 | tf_op jit(solution)/shard_map/ppermute | solution.py:47
  16.1 2.2 %collective-permute-start.7 = (bf16[544,128]{1,0:T(8,128)(2,1)S(1)}, bf16[544,128]{1,0:T(8,128)(2,1)S(1)}, u32[]{:S(2)}, u32[]{:S(2)}) collective-permute-start(bf16[544,128]{1,0:T(8,128)(2,1)S(1)} %get-tuple-element.32.refs_2_), channel_id=1, source_target_pairs={{0,6},{1,17},{8,14},{9,25},{64,70},{65,81},{72,78},{73,89},{128,13... | collective-permute-start | bytes 417800 | tf_op jit(solution)/shard_map/ppermute | solution.py:47
  18.3 1.3 %collective-permute-done.6.refs_1_ = bf16[544,128]{1,0:T(8,128)(2,1)S(1)} collective-permute-done((bf16[544,128]{1,0:T(8,128)(2,1)S(1)}, bf16[544,128]{1,0:T(8,128)(2,1)S(1)}, u32[]{:S(2)}, u32[]{:S(2)}) %collective-permute-start.6) | collective-permute-done | bytes 139296 | tf_op jit(solution)/shard_map/ppermute | solution.py:47
  19.6 2.8 %collective-permute-done.7.refs_3_ = bf16[544,128]{1,0:T(8,128)(2,1)S(1)} collective-permute-done((bf16[544,128]{1,0:T(8,128)(2,1)S(1)}, bf16[544,128]{1,0:T(8,128)(2,1)S(1)}, u32[]{:S(2)}, u32[]{:S(2)}) %collective-permute-start.7) | collective-permute-done | bytes 139296 | tf_op jit(solution)/shard_map/ppermute | solution.py:47
  22.4 0.0 collective-permute-done.3.refs_4_
  22.4 0.7 join.4
  23.1 2.1 %collective-permute-start.8 = (bf16[1088,128]{1,0:T(8,128)(2,1)S(1)}, bf16[1088,128]{1,0:T(8,128)(2,1)S(1)}, u32[]{:S(2)}, u32[]{:S(2)}) collective-permute-start(bf16[1088,128]{1,0:T(8,128)(2,1)S(1)} %get-tuple-element.33.refs_0_), channel_id=1, source_target_pairs={{0,48},{1,7},{8,56},{9,15},{64,112},{65,71},{72,120},{73,79},{128,... | collective-permute-start | bytes 835592 | tf_op jit(solution)/shard_map/ppermute | solution.py:47
  25.2 2.6 %collective-permute-start.9 = (bf16[1088,128]{1,0:T(8,128)(2,1)S(1)}, bf16[1088,128]{1,0:T(8,128)(2,1)S(1)}, u32[]{:S(2)}, u32[]{:S(2)}) collective-permute-start(bf16[1088,128]{1,0:T(8,128)(2,1)S(1)} %get-tuple-element.34.refs_2_), channel_id=1, source_target_pairs={{0,16},{1,3},{8,24},{9,11},{64,80},{65,67},{72,88},{73,75},{128,14... | collective-permute-start | bytes 835592 | tf_op jit(solution)/shard_map/ppermute | solution.py:47
  27.9 0.0 collective-permute-start.4
  27.9 6.5 %collective-permute-done.4.refs_4_ = bf16[1056,128]{1,0:T(8,128)(2,1)S(1)} collective-permute-done((bf16[1056,128]{1,0:T(8,128)(2,1)S(1)}, bf16[1056,128]{1,0:T(8,128)(2,1)S(1)}, u32[]{:S(2)}, u32[]{:S(2)}) %collective-permute-start.4) | collective-permute-done | bytes 270368 | tf_op jit(solution)/shard_map/ppermute | solution.py:47
  34.3 0.0 collective-permute-done.8.refs_1_
  34.3 0.0 collective-permute-done.9.refs_3_
  34.3 0.2 join.5
  34.5 0.1 collective-permute-start.12
  34.6 0.5 collective-permute-start.13
  35.1 2.2 %collective-permute-start.10 = (bf16[2176,128]{1,0:T(8,128)(2,1)S(1)}, bf16[2176,128]{1,0:T(8,128)(2,1)S(1)}, u32[]{:S(2)}, u32[]{:S(2)}) collective-permute-start(bf16[2176,128]{1,0:T(8,128)(2,1)S(1)} %get-tuple-element.35), channel_id=1, source_target_pairs={{0,6},{1,17},{8,14},{9,25},{64,70},{65,81},{72,78},{73,89},{128,13... | collective-permute-start | bytes 1671176 | tf_op jit(solution)/shard_map/ppermute | solution.py:47
  37.3 0.5 collective-permute-start.11
  37.8 0.3 collective-permute-start.5
  38.1 0.0 collective-permute-done.12
  38.1 0.0 collective-permute-done.13
  38.1 5.0 %pair.4 = (f32[256,512]{1,0:T(8,128)S(1)}, f32[256,512]{1,0:T(8,128)S(1)}, f32[256,512]{1,0:T(8,128)S(1)}) custom-call(bf16[2,528,128]{2,1,0:T(8,128)(2,1)S(1)} %bitcast.36, bf16[2,528,128]{2,1,0:T(8,128)(2,1)S(1)} %bitcast.14, bf16[2,528,128]{2,1,0:T(8,128)(2,1)S(1)} %bitcast.16, bf16[8,272,128]{2,1,0:T(8,128)(2,1)S(1)} %bitcast.24, ...), custom_call_target="tpu_custom_call" | custom-call | flops 3221225472 | bytes 2883584 | tf_op jit(solution)/shard_map/pair/pallas_call | solution.py:175
  43.1 2.4 %collective-permute-done.5 = bf16[1056,128]{1,0:T(8,128)(2,1)S(1)} collective-permute-done((bf16[1056,128]{1,0:T(8,128)(2,1)S(1)}, bf16[1056,128]{1,0:T(8,128)(2,1)S(1)}, u32[]{:S(2)}, u32[]{:S(2)}) %collective-permute-start.5) | collective-permute-done | bytes 270368 | tf_op jit(solution)/shard_map/ppermute | solution.py:47
  45.5 0.4 collective-permute-done.10
  45.9 1.0 %collective-permute-done.11 = bf16[2176,128]{1,0:T(8,128)(2,1)S(1)} collective-permute-done((bf16[2176,128]{1,0:T(8,128)(2,1)S(1)}, bf16[2176,128]{1,0:T(8,128)(2,1)S(1)}, u32[]{:S(2)}, u32[]{:S(2)}) %collective-permute-start.11) | collective-permute-done | bytes 557088 | tf_op jit(solution)/shard_map/ppermute | solution.py:47
  46.9 0.0 collective-permute-start.14
  46.9 0.5 collective-permute-start.15
  47.4 2.4 %pair.6.refs_5_ = f32[256,512]{1,0:T(8,128)S(1)} custom-call(bf16[2,528,128]{2,1,0:T(8,128)(2,1)S(1)} %bitcast.38, bf16[8,272,128]{2,1,0:T(8,128)(2,1)S(1)} %bitcast.25, bf16[8,272,128]{2,1,0:T(8,128)(2,1)S(1)} %bitcast.27, bf16[8,272,128]{2,1,0:T(8,128)(2,1)S(1)} %bitcast.29, bf16[8,272,128]{2,1,0:T(8,128)(2,1)S(1)} %bitcast.31), custom_call_target="tpu_custom_call" | custom-call | flops 1073741824 | bytes 2359296 | tf_op jit(solution)/shard_map/pair/pallas_call | solution.py:175
  49.7 0.0 collective-permute-done.14
  49.7 0.0 collective-permute-done.15
  49.8 2.4 %pair.7 = bf16[256,512]{1,0:T(8,128)(2,1)S(1)} custom-call(bf16[2,528,128]{2,1,0:T(8,128)(2,1)S(1)} %bitcast.39, bf16[8,272,128]{2,1,0:T(8,128)(2,1)S(1)} %bitcast.20, bf16[8,272,128]{2,1,0:T(8,128)(2,1)S(1)} %bitcast.22, bf16[8,272,128]{2,1,0:T(8,128)(2,1)S(1)} %bitcast.32, bf16[8,272,128]{2,1,0:T(8,128)(2,1)S(1)} %bitcast.34, f32[256,512]{1,0:T(8,128)S(1)} %pair.6.refs_5_), custom_call_target="tpu_custom_call" | custom-call | flops 1073741824 | bytes 2359296 | tf_op jit(solution)/shard_map/pair/pallas_call | solution.py:175
  52.2 0.7 collective-permute-start.16
  52.9 5.1 %pair.5 = (f32[256,512]{1,0:T(8,128)S(1)}, f32[256,512]{1,0:T(8,128)S(1)}, f32[256,512]{1,0:T(8,128)S(1)}) custom-call(bf16[2,528,128]{2,1,0:T(8,128)(2,1)S(1)} %bitcast.37, bf16[2,528,128]{2,1,0:T(8,128)(2,1)S(1)} %bitcast.15, bf16[2,528,128]{2,1,0:T(8,128)(2,1)S(1)} %bitcast.17, bf16[8,272,128]{2,1,0:T(8,128)(2,1)S(1)} %bitcast.21, ...), custom_call_target="tpu_custom_call" | custom-call | flops 3221225472 | bytes 2883584 | tf_op jit(solution)/shard_map/pair/pallas_call | solution.py:175
  57.9 1.9 %collective-permute-done.16 = bf16[256,512]{1,0:T(8,128)(2,1)S(1)} collective-permute-done((bf16[256,512]{1,0:T(8,128)(2,1)S(1)}, bf16[256,512]{1,0:T(8,128)(2,1)S(1)}, u32[]{:S(2)}, u32[]{:S(2)}) %collective-permute-start.16) | collective-permute-done | bytes 262176 | tf_op jit(solution)/shard_map/ppermute | solution.py:47
  59.8 0.1 add_convert_fusion.1
  59.9 0.1 collective-permute-start.17
  60.0 6.4 %collective-permute-done.17 = bf16[256,512]{1,0:T(8,128)(2,1)S(1)} collective-permute-done((bf16[256,512]{1,0:T(8,128)(2,1)S(1)}, bf16[256,512]{1,0:T(8,128)(2,1)S(1)}, u32[]{:S(2)}, u32[]{:S(2)}) %collective-permute-start.17) | collective-permute-done | bytes 262176 | tf_op jit(solution)/shard_map/ppermute | solution.py:47
  66.4 0.1 add_convert_fusion
  66.4 0.8 %collective-permute-start.18 = (bf16[256,512]{1,0:T(8,128)(2,1)S(1)}, bf16[256,512]{1,0:T(8,128)(2,1)S(1)}, u32[]{:S(2)}, u32[]{:S(2)}) collective-permute-start(bf16[256,512]{1,0:T(8,128)(2,1)S(1)} %add_convert_fusion), channel_id=1, source_target_pairs={{0,200},{1,9},{8,64},{9,1},{64,8},{65,73},{72,128},{73,65},{128,72... | collective-permute-start | bytes 786440 | tf_op jit(solution)/shard_map/ppermute | solution.py:47
  67.2 7.1 %collective-permute-done.18 = bf16[256,512]{1,0:T(8,128)(2,1)S(1)} collective-permute-done((bf16[256,512]{1,0:T(8,128)(2,1)S(1)}, bf16[256,512]{1,0:T(8,128)(2,1)S(1)}, u32[]{:S(2)}, u32[]{:S(2)}) %collective-permute-start.18) | collective-permute-done | bytes 262176 | tf_op jit(solution)/shard_map/ppermute | solution.py:47
  74.4 0.1 convert_add_fusion
  74.5 0.0 copy-start.1
  74.5 0.1 collective-permute-start.19
  74.6 4.9 %collective-permute-done.19.arrived = bf16[128,512]{1,0:T(8,128)(2,1)S(1)} collective-permute-done((bf16[128,512]{1,0:T(8,128)(2,1)S(1)}, bf16[128,512]{1,0:T(8,128)(2,1)S(1)}, u32[]{:S(2)}, u32[]{:S(2)}) %collective-permute-start.19) | collective-permute-done | bytes 131104 | tf_op jit(solution)/shard_map/ppermute | solution.py:47
  79.6 0.0 copy-done.1
  79.6 0.9 %final.1 = f32[128,512]{1,0:T(8,128)} custom-call(f32[128,512]{1,0:T(8,128)S(1)} %copy-done.1, f32[128,512]{1,0:T(8,128)S(1)} %slice.9.own, bf16[128,512]{1,0:T(8,128)(2,1)S(1)} %collective-permute-done.19.arrived), custom_call_target="tpu_custom_call" | custom-call | tf_op jit(solution)/shard_map/final/pallas_call | solution.py:271
  (2 shorter events, 0.0 us)
Async XLA Ops:
  0.0 0.7 copy-start.2
  0.0 0.7 copy-start.3
  0.7 0.9 %copy-start = (f32[128,512]{1,0:T(8,128)S(1)}, f32[128,512]{1,0:T(8,128)}, u32[]{:S(2)}) copy-start(f32[128,512]{1,0:T(8,128)} %emb.3) | copy-start | bytes 786436
  1.8 7.0 %collective-permute-start = (bf16[528,128]{1,0:T(8,128)(2,1)S(1)}, bf16[528,128]{1,0:T(8,128)(2,1)S(1)}, u32[]{:S(2)}, u32[]{:S(2)}) collective-permute-start(bf16[528,128]{1,0:T(8,128)(2,1)S(1)} %get-tuple-element.27.refs_0_), channel_id=1, source_target_pairs={{0,8},{1,201},{8,0},{9,65},{64,72},{65,9},{72,64},{73,129},{128,13... | collective-permute-start | bytes 405512 | tf_op jit(solution)/shard_map/ppermute | solution.py:47
  3.8 4.3 %collective-permute-start.1 = (bf16[272,128]{1,0:T(8,128)(2,1)S(1)}, bf16[272,128]{1,0:T(8,128)(2,1)S(1)}, u32[]{:S(2)}, u32[]{:S(2)}) collective-permute-start(bf16[272,128]{1,0:T(8,128)(2,1)S(1)} %get-tuple-element.28.refs_2_), channel_id=1, source_target_pairs={{0,16},{1,3},{8,24},{9,11},{64,80},{65,67},{72,88},{73,75},{128,14... | collective-permute-start | bytes 208904 | tf_op jit(solution)/shard_map/ppermute | solution.py:47
  4.3 4.4 %collective-permute-start.2 = (bf16[272,128]{1,0:T(8,128)(2,1)S(1)}, bf16[272,128]{1,0:T(8,128)(2,1)S(1)}, u32[]{:S(2)}, u32[]{:S(2)}) collective-permute-start(bf16[272,128]{1,0:T(8,128)(2,1)S(1)} %get-tuple-element.29.refs_4_), channel_id=1, source_target_pairs={{0,48},{1,7},{8,56},{9,15},{64,112},{65,71},{72,120},{73,79},{128,... | collective-permute-start | bytes 208904 | tf_op jit(solution)/shard_map/ppermute | solution.py:47
  9.5 12.9 %collective-permute-start.3 = (bf16[1056,128]{1,0:T(8,128)(2,1)S(1)}, bf16[1056,128]{1,0:T(8,128)(2,1)S(1)}, u32[]{:S(2)}, u32[]{:S(2)}) collective-permute-start(bf16[1056,128]{1,0:T(8,128)(2,1)S(1)} %get-tuple-element.30), channel_id=1, source_target_pairs={{0,200},{1,9},{8,64},{9,1},{64,8},{65,73},{72,128},{73,65},{128,72... | collective-permute-start | bytes 811016 | tf_op jit(solution)/shard_map/ppermute | solution.py:47
  14.5 5.1 %collective-permute-start.6 = (bf16[544,128]{1,0:T(8,128)(2,1)S(1)}, bf16[544,128]{1,0:T(8,128)(2,1)S(1)}, u32[]{:S(2)}, u32[]{:S(2)}) collective-permute-start(bf16[544,128]{1,0:T(8,128)(2,1)S(1)} %get-tuple-element.31.refs_0_), channel_id=1, source_target_pairs={{0,2},{1,49},{8,10},{9,57},{64,66},{65,113},{72,74},{73,121},{128,... | collective-permute-start | bytes 417800 | tf_op jit(solution)/shard_map/ppermute | solution.py:47
  16.1 6.3 %collective-permute-start.7 = (bf16[544,128]{1,0:T(8,128)(2,1)S(1)}, bf16[544,128]{1,0:T(8,128)(2,1)S(1)}, u32[]{:S(2)}, u32[]{:S(2)}) collective-permute-start(bf16[544,128]{1,0:T(8,128)(2,1)S(1)} %get-tuple-element.32.refs_2_), channel_id=1, source_target_pairs={{0,6},{1,17},{8,14},{9,25},{64,70},{65,81},{72,78},{73,89},{128,13... | collective-permute-start | bytes 417800 | tf_op jit(solution)/shard_map/ppermute | solution.py:47
  23.1 11.2 %collective-permute-start.8 = (bf16[1088,128]{1,0:T(8,128)(2,1)S(1)}, bf16[1088,128]{1,0:T(8,128)(2,1)S(1)}, u32[]{:S(2)}, u32[]{:S(2)}) collective-permute-start(bf16[1088,128]{1,0:T(8,128)(2,1)S(1)} %get-tuple-element.33.refs_0_), channel_id=1, source_target_pairs={{0,48},{1,7},{8,56},{9,15},{64,112},{65,71},{72,120},{73,79},{128,... | collective-permute-start | bytes 835592 | tf_op jit(solution)/shard_map/ppermute | solution.py:47
  25.2 9.1 %collective-permute-start.9 = (bf16[1088,128]{1,0:T(8,128)(2,1)S(1)}, bf16[1088,128]{1,0:T(8,128)(2,1)S(1)}, u32[]{:S(2)}, u32[]{:S(2)}) collective-permute-start(bf16[1088,128]{1,0:T(8,128)(2,1)S(1)} %get-tuple-element.34.refs_2_), channel_id=1, source_target_pairs={{0,16},{1,3},{8,24},{9,11},{64,80},{65,67},{72,88},{73,75},{128,14... | collective-permute-start | bytes 835592 | tf_op jit(solution)/shard_map/ppermute | solution.py:47
  27.9 6.5 %collective-permute-start.4 = (bf16[1056,128]{1,0:T(8,128)(2,1)S(1)}, bf16[1056,128]{1,0:T(8,128)(2,1)S(1)}, u32[]{:S(2)}, u32[]{:S(2)}) collective-permute-start(bf16[1056,128]{1,0:T(8,128)(2,1)S(1)} %collective-permute-done.3.refs_4_), channel_id=1, source_target_pairs={{0,8},{1,201},{8,0},{9,65},{64,72},{65,9},{72,64},{73,129},{128,13... | collective-permute-start | bytes 811016 | tf_op jit(solution)/shard_map/ppermute | solution.py:47
  34.5 3.6 %collective-permute-start.12 = (bf16[2176,128]{1,0:T(8,128)(2,1)S(1)}, bf16[2176,128]{1,0:T(8,128)(2,1)S(1)}, u32[]{:S(2)}, u32[]{:S(2)}) collective-permute-start(bf16[2176,128]{1,0:T(8,128)(2,1)S(1)} %get-tuple-element.35), channel_id=1, source_target_pairs={{0,1},{1,0},{2,3},{3,2},{4,5},{5,4},{6,7},{7,6},{8,9},{9,8},{10,11... | collective-permute-start | bytes 1671176 | tf_op jit(solution)/shard_map/ppermute | solution.py:51
  34.6 3.5 %collective-permute-start.13 = (bf16[2176,128]{1,0:T(8,128)(2,1)S(1)}, bf16[2176,128]{1,0:T(8,128)(2,1)S(1)}, u32[]{:S(2)}, u32[]{:S(2)}) collective-permute-start(bf16[2176,128]{1,0:T(8,128)(2,1)S(1)} %get-tuple-element.36), channel_id=1, source_target_pairs={{0,1},{1,0},{2,3},{3,2},{4,5},{5,4},{6,7},{7,6},{8,9},{9,8},{10,11... | collective-permute-start | bytes 1671176 | tf_op jit(solution)/shard_map/ppermute | solution.py:51
  35.1 10.7 %collective-permute-start.10 = (bf16[2176,128]{1,0:T(8,128)(2,1)S(1)}, bf16[2176,128]{1,0:T(8,128)(2,1)S(1)}, u32[]{:S(2)}, u32[]{:S(2)}) collective-permute-start(bf16[2176,128]{1,0:T(8,128)(2,1)S(1)} %get-tuple-element.35), channel_id=1, source_target_pairs={{0,6},{1,17},{8,14},{9,25},{64,70},{65,81},{72,78},{73,89},{128,13... | collective-permute-start | bytes 1671176 | tf_op jit(solution)/shard_map/ppermute | solution.py:47
  37.3 9.5 %collective-permute-start.11 = (bf16[2176,128]{1,0:T(8,128)(2,1)S(1)}, bf16[2176,128]{1,0:T(8,128)(2,1)S(1)}, u32[]{:S(2)}, u32[]{:S(2)}) collective-permute-start(bf16[2176,128]{1,0:T(8,128)(2,1)S(1)} %get-tuple-element.36), channel_id=1, source_target_pairs={{0,2},{1,49},{8,10},{9,57},{64,66},{65,113},{72,74},{73,121},{128,... | collective-permute-start | bytes 1671176 | tf_op jit(solution)/shard_map/ppermute | solution.py:47
  37.8 7.7 %collective-permute-start.5 = (bf16[1056,128]{1,0:T(8,128)(2,1)S(1)}, bf16[1056,128]{1,0:T(8,128)(2,1)S(1)}, u32[]{:S(2)}, u32[]{:S(2)}) collective-permute-start(bf16[1056,128]{1,0:T(8,128)(2,1)S(1)} %collective-permute-done.4.refs_4_), channel_id=1, source_target_pairs={{0,200},{1,9},{8,64},{9,1},{64,8},{65,73},{72,128},{73,65},{128,72... | collective-permute-start | bytes 811016 | tf_op jit(solution)/shard_map/ppermute | solution.py:47
  46.9 2.9 %collective-permute-start.14 = (bf16[2176,128]{1,0:T(8,128)(2,1)S(1)}, bf16[2176,128]{1,0:T(8,128)(2,1)S(1)}, u32[]{:S(2)}, u32[]{:S(2)}) collective-permute-start(bf16[2176,128]{1,0:T(8,128)(2,1)S(1)} %collective-permute-done.10), channel_id=1, source_target_pairs={{0,1},{1,0},{2,3},{3,2},{4,5},{5,4},{6,7},{7,6},{8,9},{9,8},{10,11... | collective-permute-start | bytes 1671176 | tf_op jit(solution)/shard_map/ppermute | solution.py:51
  46.9 2.9 %collective-permute-start.15 = (bf16[2176,128]{1,0:T(8,128)(2,1)S(1)}, bf16[2176,128]{1,0:T(8,128)(2,1)S(1)}, u32[]{:S(2)}, u32[]{:S(2)}) collective-permute-start(bf16[2176,128]{1,0:T(8,128)(2,1)S(1)} %collective-permute-done.11), channel_id=1, source_target_pairs={{0,1},{1,0},{2,3},{3,2},{4,5},{5,4},{6,7},{7,6},{8,9},{9,8},{10,11... | collective-permute-start | bytes 1671176 | tf_op jit(solution)/shard_map/ppermute | solution.py:51
  52.2 7.7 %collective-permute-start.16 = (bf16[256,512]{1,0:T(8,128)(2,1)S(1)}, bf16[256,512]{1,0:T(8,128)(2,1)S(1)}, u32[]{:S(2)}, u32[]{:S(2)}) collective-permute-start(bf16[256,512]{1,0:T(8,128)(2,1)S(1)} %pair.7), channel_id=1, source_target_pairs={{0,200},{1,9},{8,64},{9,1},{64,8},{65,73},{72,128},{73,65},{128,72... | collective-permute-start | bytes 786440 | tf_op jit(solution)/shard_map/ppermute | solution.py:47
  59.9 6.5 %collective-permute-start.17 = (bf16[256,512]{1,0:T(8,128)(2,1)S(1)}, bf16[256,512]{1,0:T(8,128)(2,1)S(1)}, u32[]{:S(2)}, u32[]{:S(2)}) collective-permute-start(bf16[256,512]{1,0:T(8,128)(2,1)S(1)} %add_convert_fusion.1), channel_id=1, source_target_pairs={{0,8},{1,201},{8,0},{9,65},{64,72},{65,9},{72,64},{73,129},{128,13... | collective-permute-start | bytes 786440 | tf_op jit(solution)/shard_map/ppermute | solution.py:47
  66.4 8.0 %collective-permute-start.18 = (bf16[256,512]{1,0:T(8,128)(2,1)S(1)}, bf16[256,512]{1,0:T(8,128)(2,1)S(1)}, u32[]{:S(2)}, u32[]{:S(2)}) collective-permute-start(bf16[256,512]{1,0:T(8,128)(2,1)S(1)} %add_convert_fusion), channel_id=1, source_target_pairs={{0,200},{1,9},{8,64},{9,1},{64,8},{65,73},{72,128},{73,65},{128,72... | collective-permute-start | bytes 786440 | tf_op jit(solution)/shard_map/ppermute | solution.py:47
  74.5 5.1 %copy-start.1 = (f32[128,512]{1,0:T(8,128)S(1)}, f32[128,512]{1,0:T(8,128)}, u32[]{:S(2)}) copy-start(f32[128,512]{1,0:T(8,128)} %emb.3) | copy-start | bytes 786436
  74.5 5.1 %collective-permute-start.19 = (bf16[128,512]{1,0:T(8,128)(2,1)S(1)}, bf16[128,512]{1,0:T(8,128)(2,1)S(1)}, u32[]{:S(2)}, u32[]{:S(2)}) collective-permute-start(bf16[128,512]{1,0:T(8,128)(2,1)S(1)} %slice.12), channel_id=1, source_target_pairs={{0,8},{1,201},{8,0},{9,65},{64,72},{65,9},{72,64},{73,129},{128,13... | collective-permute-start | bytes 393224 | tf_op jit(solution)/shard_map/ppermute | solution.py:47

commit v3 on v2

v3 whole, which is shorter than its diff:
```python
import functools
import itertools
import math

import jax
import jax.numpy as jnp
from jax import lax
from jax.experimental import pallas as pl
from jax.experimental.pallas import tpu as pltpu
from jax.sharding import PartitionSpec as P

BF = jnp.bfloat16
F32 = jnp.float32
D = 512
CPD = 128
META = 16
LANES = 128
CHUNKS = D // LANES
PACKED = CHUNKS * CPD + META
SMALL = 6 << 20
AXES = ("row", "col")
VMEM = pl.BlockSpec(memory_space=pltpu.VMEM)
ANY = pl.BlockSpec(memory_space=pl.ANY)


def _flat(x, y, z, core):
    return ((((z // 2) * 4 + x) * 2 + z % 2) * 4 + y) * 2 + core


LINKS = {
    "xa": lambda x, y, z: (x ^ 1, y, z),
    "xb": lambda x, y, z: (3 - x, y, z),
    "xaya": lambda x, y, z: (x ^ 1, y ^ 1, z),
    "xbyb": lambda x, y, z: (3 - x, 3 - y, z),
    "ya": lambda x, y, z: (x, y ^ 1, z),
    "yb": lambda x, y, z: (x, 3 - y, z),
    "za": lambda x, y, z: (x, y, z ^ 1),
    "zb": lambda x, y, z: (x, y, (z - 1) % 8 if z % 2 == 0 else (z + 1) % 8),
}


def swap(block, link0, link1):
    pairs = []
    for x, y, z, core in itertools.product(range(4), range(4), range(8), range(2)):
        pairs.append((_flat(x, y, z, core), _flat(*LINKS[(link0, link1)[core]](x, y, z), core)))
    return lax.ppermute(block, AXES, pairs)


def shift(block, sign):
    pairs = []
    for x, y, z, core in itertools.product(range(4), range(4), range(8), range(2)):
        step = 2 * sign * (1 if (z + core) % 2 == 0 else -1)
        pairs.append((_flat(x, y, z, core), _flat(x, y, (z + step) % 8, core)))
    return lax.ppermute(block, AXES, pairs)


def swap_cores(block):
    return lax.ppermute(block, AXES, [(i, i ^ 1) for i in range(256)])


def pack_kernel(emb, margin, group, whole):
    e = emb[...]
    unit = (e / jnp.sqrt(jnp.sum(e * e, axis=1, keepdims=True) + 1e-06)).astype(BF)
    row = lax.broadcasted_iota(jnp.int32, (META, LANES), 0)
    meta = jnp.where(row == 0, margin[...], jnp.where(row == 1, group[...], 0)).astype(F32).astype(BF)
    for f in range(CHUNKS):
        whole[f * CPD : (f + 1) * CPD, :] = unit[:, f * LANES : (f + 1) * LANES]
    whole[CHUNKS * CPD :, :] = meta


def pack(embeddings, margin, group):
    return pl.pallas_call(
        pack_kernel,
        out_shape=jax.ShapeDtypeStruct((PACKED, LANES), BF),
        in_specs=[VMEM] * 3,
        out_specs=VMEM,
        compiler_params=pltpu.CompilerParams(vmem_limit_bytes=SMALL),
        name="pack",
    )(embeddings, margin.reshape(1, CPD), group.reshape(1, CPD))


TILE = 1024
TB = TILE // CPD


def pair_kernel(n_r, n_c, n_sum, *refs):
    r_in, c_in, rest = refs[:n_r], refs[n_r : n_r + n_c], refs[n_r + n_c :]
    sums, outs = rest[:n_sum], rest[n_sum : n_sum + n_r]
    rbuf, rmeta, cbuf, cmeta, rm, rg, acc, r_sem, c_sem = rest[n_sum + n_r :]

    def unpack(ref, buf, meta, at, sems):
        n = ref.shape[0]
        own = [
            pltpu.make_async_copy(
                ref.at[:, f * CPD : (f + 1) * CPD, :],
                buf.at[at : at + n, :, f * LANES : (f + 1) * LANES],
                sems(f),
            )
            for f in range(CHUNKS)
        ]
        own.append(pltpu.make_async_copy(ref.at[:, CHUNKS * CPD :, :], meta.at[at : at + n], sems(CHUNKS)))
        return own

    copies, waits, at = [], {}, 0
    for i, ref in enumerate(r_in):
        copies += unpack(ref, rbuf, rmeta, at, lambda f, i=i: r_sem.at[i, f])
        at += ref.shape[0]
    col = 0
    for i, ref in enumerate(c_in):
        own = unpack(ref, cbuf, cmeta, col, lambda f, i=i: c_sem.at[i, f])
        waits.setdefault(col // TB, []).extend(own)
        col += ref.shape[0]
    for c in copies + sum(waits.values(), []):
        c.start()
    for c in copies:
        c.wait()
    for k in range(at):
        m = rmeta[k].astype(F32)
        rm[k * CPD : (k + 1) * CPD, :] = jnp.broadcast_to(m[0:1] * 0.0005, (CPD, CPD)).T
        rg[k * CPD : (k + 1) * CPD, :] = jnp.broadcast_to(m[1:2], (CPD, CPD)).T
    if sums:
        o = 0
        for ref in sums:
            n = ref.shape[0]
            acc[o : o + n, :] = ref[...]
            o += n
    else:
        acc[...] = jnp.zeros_like(acc)
    for t in range(col // TB):
        for c in waits[t]:
            c.wait()

    def body(t, carry):
        ct = cbuf[pl.ds(t * TB, TB)].reshape(TILE, D)
        margins, groups = [], []
        for k in range(TB):
            m = cmeta[t * TB + k].astype(F32)
            margins.append(m[0:1] * 0.0005)
            groups.append(m[1:2])
        for r0 in range(0, at * CPD, 256):
            rt = rbuf[r0 // CPD : r0 // CPD + 2].reshape(256, D)
            cos = lax.dot_general(rt, ct, (((1,), (1,)), ((), ())), preferred_element_type=F32)
            parts = []
            for k in range(TB):
                over = jnp.maximum(cos[:, k * LANES : (k + 1) * LANES] - rm[r0 : r0 + 256, :] - margins[k], 0.0)
                parts.append(jnp.where(rg[r0 : r0 + 256, :] != groups[k], over, 0.0).astype(BF))
            s = jnp.concatenate(parts, axis=1)
            acc[r0 : r0 + 256, :] += jnp.dot(s, ct, preferred_element_type=F32)
        return carry

    lax.fori_loop(0, col // TB, body, 0)
    o = 0
    for out in outs:
        n = out.shape[0]
        out[...] = acc[o : o + n, :].astype(out.dtype)
        o += n


def pair(r_in, c_in, out_dtype, sums=()):
    r_in, c_in = ([a.reshape(-1, PACKED, LANES) for a in v] for v in (r_in, c_in))
    r_blocks, c_blocks = (sum(a.shape[0] for a in v) for v in (r_in, c_in))
    rows, n_c = r_blocks * CPD, len(c_in)
    return pl.pallas_call(
        functools.partial(pair_kernel, len(r_in), n_c, len(sums)),
        out_shape=[jax.ShapeDtypeStruct((a.shape[0] * CPD, D), out_dtype) for a in r_in],
        in_specs=[ANY] * (len(r_in) + n_c) + [VMEM] * len(sums),
        out_specs=[VMEM] * len(r_in),
        scratch_shapes=[
            pltpu.VMEM((r_blocks, CPD, D), BF),
            pltpu.VMEM((r_blocks, META, LANES), BF),
            pltpu.VMEM((c_blocks, CPD, D), BF),
            pltpu.VMEM((c_blocks, META, LANES), BF),
            pltpu.VMEM((rows, CPD), F32),
            pltpu.VMEM((rows, CPD), F32),
            pltpu.VMEM((rows, D), F32),
            pltpu.SemaphoreType.DMA((len(r_in), CHUNKS + 1)),
            pltpu.SemaphoreType.DMA((n_c, CHUNKS + 1)),
        ],
        compiler_params=pltpu.CompilerParams(vmem_limit_bytes=20 << 20),
        cost_estimate=pl.CostEstimate(
            flops=4 * rows * c_blocks * CPD * D, bytes_accessed=(c_blocks * CPD + rows) * D * 2, transcendentals=0
        ),
        name="pair",
    )(*r_in, *c_in, *sums)


def join_kernel(pieces, n_in, *refs):
    ins, outs, sem = refs[:n_in], refs[n_in:-1], refs[-1]
    copies = []
    for out, which in zip(outs, pieces, strict=True):
        at = 0
        for i in which:
            n = ins[i].shape[0]
            copies.append(pltpu.make_async_copy(ins[i], out.at[at : at + n], sem.at[len(copies)]))
            at += n
    for c in copies:
        c.start()
    for c in copies:
        c.wait()


def join(pieces, *ins):
    return pl.pallas_call(
        functools.partial(join_kernel, pieces, len(ins)),
        out_shape=[jax.ShapeDtypeStruct((sum(ins[i].shape[0] for i in p), LANES), BF) for p in pieces],
        in_specs=[ANY] * len(ins),
        out_specs=[VMEM] * len(pieces),
        scratch_shapes=[pltpu.SemaphoreType.DMA((sum(map(len, pieces)),))],
        compiler_params=pltpu.CompilerParams(vmem_limit_bytes=SMALL),
        name="join",
    )(*ins)


def final_kernel(rate, emb, own, *refs):
    arrived, out = refs[:-1], refs[-1]
    e = emb[...]
    lengths = jnp.sqrt(jnp.sum(e * e, axis=1, keepdims=True) + 1e-06)
    unit = e / lengths
    grad = 4.0 * sum((ref[...].astype(F32) for ref in arrived), own[...])
    radial = jnp.sum(unit * grad, axis=1, keepdims=True)
    out[...] = e - rate * ((grad - unit * radial) / lengths)


def per_device(embeddings, margin, group):
    classes = embeddings.shape[0] * lax.axis_size("row") * lax.axis_size("col")
    whole = pack(embeddings, margin, group)

    near = swap(whole, "za", "zb")
    square = [swap(whole, a, b) for a, b in (("xa", "xb"), ("ya", "yb"), ("xaya", "xbyb"))]
    both, c0 = join(((0, 1), (0, 2, 3, 4)), whole, near, *square)
    back = swap(both, "zb", "za")
    c3, c1, c2 = (swap(c0, b, a) for a, b in (("xaya", "xbyb"), ("xa", "xb"), ("ya", "yb")))
    ahead = swap(back, "za", "zb")
    far = swap(ahead, "zb", "za")
    e0, e1 = swap_cores(c0), swap_cores(c1)
    sums = pair([ahead, back, both], [c0, e0, c1, e1], F32)
    far, c2, c3, *sums = lax.optimization_barrier((far, c2, c3, *sums))
    e2, e3 = swap_cores(c2), swap_cores(c3)
    (p_far,) = pair([far], [c0, e0, c1, e1], F32)
    (p_far,) = pair([far], [c2, e2, c3, e3], BF, [p_far])
    q = swap(p_far, "zb", "za")
    p_ahead, p_back, p_own = pair([ahead, back, both], [c2, e2, c3, e3], F32, sums)
    q_near = swap(p_own[CPD:].astype(BF), "za", "zb")
    q = swap((p_ahead + q).astype(BF), "za", "zb")
    p_back = (p_back + q).astype(BF)
    arrived = (q_near, swap(p_back[:CPD], "zb", "za"), shift(p_back[CPD:], -1))

    rate = D * math.sqrt(D) / (3.0 * math.sqrt(classes))
    return pl.pallas_call(
        functools.partial(final_kernel, rate),
        out_shape=jax.ShapeDtypeStruct((CPD, D), F32),
        in_specs=[VMEM] * 5,
        out_specs=VMEM,
        compiler_params=pltpu.CompilerParams(vmem_limit_bytes=SMALL),
        name="final",
    )(embeddings, p_own[:CPD], *arrived)


def solution(mesh):
    in_specs = (P(("row", "col"), None), P(("row", "col")), P(("row", "col")))
    out_specs = P(("row", "col"), None)
    return jax.shard_map(per_device, mesh=mesh, in_specs=in_specs, out_specs=out_specs, check_vma=False)
```

time: 80.6 us -> 74.3 us (0.922)
  the two profiles are of different devices: /device:TPU:2 before, /device:TPU:32 now
where the time goes in v3:
time: 74.3 us; the launch traced here: 74.2 us
  starting transfers between devices  32.3 us (43%)
  waiting for transfers between devices  23 us (31%)
  Pallas kernels  16.9 us (23%)
  local copies, waits for them, and re-layouts  1.68 us (2%)
    ppermute x14, starting transfers between devices, swap(): return lax.ppermute(block, AXES, pairs)  23.9 us
    ppermute x14, waiting for transfers between devices, swap(): return lax.ppermute(block, AXES, pairs)  20.1 us
    pallas_call x4, Pallas kernels, pair(): pl.pallas_call(functools.partial(pair_kernel, len(r_in), n_c, len(sums)),...  14.8 us
    ppermute x4, starting transfers between devices, swap_cores(): return lax.ppermute(block, AXES, [(i, i ^ 1) for i in range(256)])  5.75 us
    ppermute x1, waiting for transfers between devices, shift(): return lax.ppermute(block, AXES, pairs)  2.87 us
    ppermute x1, starting transfers between devices, shift(): return lax.ppermute(block, AXES, pairs)  2.69 us
    unnamed x8, local copies, waits for them, and re-layouts  1.62 us
  transfers between devices with their start and end apart: 19, of which 9 were waited for; matrix products, arithmetic and copies ran while one was open for 0% of the time, Pallas kernels for 17%

profile of v3, /device:TPU:32, one launch (start us, length us, event | category | flops | bytes accessed | tf_op | source)
XLA Modules:
  0.0 74.2 jit_solution(9256489579231953155)
XLA Ops:
  0.0 0.0 copy-start.2
  0.0 0.0 copy-start.3
  0.0 0.7 copy-done.2
  0.7 0.0 copy-done.3
  0.7 0.0 copy-start
  0.7 0.9 %copy-done = f32[128,512]{1,0:T(8,128)S(1)} copy-done((f32[128,512]{1,0:T(8,128)S(1)}, f32[128,512]{1,0:T(8,128)}, u32[]{:S(2)}) %copy-start) | copy-done | bytes 262168
  1.6 0.1 pack.1.refs_0_
  1.8 1.9 %collective-permute-start = (bf16[528,128]{1,0:T(8,128)(2,1)S(1)}, bf16[528,128]{1,0:T(8,128)(2,1)S(1)}, u32[]{:S(2)}, u32[]{:S(2)}) collective-permute-start(bf16[528,128]{1,0:T(8,128)(2,1)S(1)} %pack.1.refs_0_), channel_id=1, source_target_pairs={{0,8},{1,201},{8,0},{9,65},{64,72},{65,9},{72,64},{73,129},{128,13... | collective-permute-start | bytes 405512 | tf_op jit(solution)/shard_map/ppermute | solution.py:46
  3.7 0.0 collective-permute-start.1
  3.7 1.3 %collective-permute-start.2 = (bf16[528,128]{1,0:T(8,128)(2,1)S(1)}, bf16[528,128]{1,0:T(8,128)(2,1)S(1)}, u32[]{:S(2)}, u32[]{:S(2)}) collective-permute-start(bf16[528,128]{1,0:T(8,128)(2,1)S(1)} %pack.1.refs_0_), channel_id=1, source_target_pairs={{0,2},{1,7},{8,10},{9,15},{64,66},{65,71},{72,74},{73,79},{128,130... | collective-permute-start | bytes 405512 | tf_op jit(solution)/shard_map/ppermute | solution.py:46
  5.0 2.2 %collective-permute-start.3 = (bf16[528,128]{1,0:T(8,128)(2,1)S(1)}, bf16[528,128]{1,0:T(8,128)(2,1)S(1)}, u32[]{:S(2)}, u32[]{:S(2)}) collective-permute-start(bf16[528,128]{1,0:T(8,128)(2,1)S(1)} %pack.1.refs_0_), channel_id=1, source_target_pairs={{0,18},{1,55},{8,26},{9,63},{64,82},{65,119},{72,90},{73,127},{128... | collective-permute-start | bytes 405512 | tf_op jit(solution)/shard_map/ppermute | solution.py:46
  7.2 0.0 collective-permute-done.refs_1_
  7.2 1.5 %collective-permute-done.1.refs_2_ = bf16[528,128]{1,0:T(8,128)(2,1)S(1)} collective-permute-done((bf16[528,128]{1,0:T(8,128)(2,1)S(1)}, bf16[528,128]{1,0:T(8,128)(2,1)S(1)}, u32[]{:S(2)}, u32[]{:S(2)}) %collective-permute-start.1) | collective-permute-done | bytes 135200 | tf_op jit(solution)/shard_map/ppermute | solution.py:46
  8.7 0.0 collective-permute-done.2.refs_3_
  8.7 2.2 %collective-permute-done.3.refs_4_ = bf16[528,128]{1,0:T(8,128)(2,1)S(1)} collective-permute-done((bf16[528,128]{1,0:T(8,128)(2,1)S(1)}, bf16[528,128]{1,0:T(8,128)(2,1)S(1)}, u32[]{:S(2)}, u32[]{:S(2)}) %collective-permute-start.3) | collective-permute-done | bytes 135200 | tf_op jit(solution)/shard_map/ppermute | solution.py:46
  10.9 1.1 %join.1 = (bf16[1056,128]{1,0:T(8,128)(2,1)S(1)}, bf16[2112,128]{1,0:T(8,128)(2,1)S(1)}) custom-call(bf16[528,128]{1,0:T(8,128)(2,1)S(1)} %pack.1.refs_0_, bf16[528,128]{1,0:T(8,128)(2,1)S(1)} %collective-permute-done.refs_1_, bf16[528,128]{1,0:T(8,128)(2,1)S(1)} %collective-permute-done.1.refs_2_, bf16[528,128]{1,0:T(8,128)(2,1)S(1)} %collective-permute-done.2.refs_3_, ...), custom_call_target="tpu_custom_call" | custom-call | tf_op jit(solution)/shard_map/join/pallas_call | solution.py:203
  12.0 2.2 %collective-permute-start.10 = (bf16[2112,128]{1,0:T(8,128)(2,1)S(1)}, bf16[2112,128]{1,0:T(8,128)(2,1)S(1)}, u32[]{:S(2)}, u32[]{:S(2)}) collective-permute-start(bf16[2112,128]{1,0:T(8,128)(2,1)S(1)} %get-tuple-element.20), channel_id=1, source_target_pairs={{0,48},{1,17},{8,56},{9,25},{64,112},{65,81},{72,120},{73,89},{128... | collective-permute-start | bytes 1622024 | tf_op jit(solution)/shard_map/ppermute | solution.py:46
  14.2 3.7 %collective-permute-start.4 = (bf16[1056,128]{1,0:T(8,128)(2,1)S(1)}, bf16[1056,128]{1,0:T(8,128)(2,1)S(1)}, u32[]{:S(2)}, u32[]{:S(2)}) collective-permute-start(bf16[1056,128]{1,0:T(8,128)(2,1)S(1)} %get-tuple-element.19), channel_id=1, source_target_pairs={{0,200},{1,9},{8,64},{9,1},{64,8},{65,73},{72,128},{73,65},{128,72... | collective-permute-start | bytes 811016 | tf_op jit(solution)/shard_map/ppermute | solution.py:46
  17.9 2.8 %collective-permute-start.9 = (bf16[2112,128]{1,0:T(8,128)(2,1)S(1)}, bf16[2112,128]{1,0:T(8,128)(2,1)S(1)}, u32[]{:S(2)}, u32[]{:S(2)}) collective-permute-start(bf16[2112,128]{1,0:T(8,128)(2,1)S(1)} %get-tuple-element.20), channel_id=1, source_target_pairs={{0,1},{1,0},{2,3},{3,2},{4,5},{5,4},{6,7},{7,6},{8,9},{9,8},{10,11... | collective-permute-start | bytes 1622024 | tf_op jit(solution)/shard_map/ppermute | solution.py:58
  20.7 1.9 %collective-permute-done.10 = bf16[2112,128]{1,0:T(8,128)(2,1)S(1)} collective-permute-done((bf16[2112,128]{1,0:T(8,128)(2,1)S(1)}, bf16[2112,128]{1,0:T(8,128)(2,1)S(1)}, u32[]{:S(2)}, u32[]{:S(2)}) %collective-permute-start.10) | collective-permute-done | bytes 540704 | tf_op jit(solution)/shard_map/ppermute | solution.py:46
  22.7 2.4 %collective-permute-start.11 = (bf16[2112,128]{1,0:T(8,128)(2,1)S(1)}, bf16[2112,128]{1,0:T(8,128)(2,1)S(1)}, u32[]{:S(2)}, u32[]{:S(2)}) collective-permute-start(bf16[2112,128]{1,0:T(8,128)(2,1)S(1)} %collective-permute-done.10), channel_id=1, source_target_pairs={{0,1},{1,0},{2,3},{3,2},{4,5},{5,4},{6,7},{7,6},{8,9},{9,8},{10,11... | collective-permute-start | bytes 1622024 | tf_op jit(solution)/shard_map/ppermute | solution.py:58
  25.1 0.0 collective-permute-done.4
  25.1 4.0 %collective-permute-start.5 = (bf16[1056,128]{1,0:T(8,128)(2,1)S(1)}, bf16[1056,128]{1,0:T(8,128)(2,1)S(1)}, u32[]{:S(2)}, u32[]{:S(2)}) collective-permute-start(bf16[1056,128]{1,0:T(8,128)(2,1)S(1)} %collective-permute-done.4), channel_id=1, source_target_pairs={{0,8},{1,201},{8,0},{9,65},{64,72},{65,9},{72,64},{73,129},{128,13... | collective-permute-start | bytes 811016 | tf_op jit(solution)/shard_map/ppermute | solution.py:46
  29.1 0.3 collective-permute-start.7
  29.4 2.9 %collective-permute-start.8 = (bf16[2112,128]{1,0:T(8,128)(2,1)S(1)}, bf16[2112,128]{1,0:T(8,128)(2,1)S(1)}, u32[]{:S(2)}, u32[]{:S(2)}) collective-permute-start(bf16[2112,128]{1,0:T(8,128)(2,1)S(1)} %get-tuple-element.20), channel_id=1, source_target_pairs={{0,54},{1,19},{8,62},{9,27},{64,118},{65,83},{72,126},{73,91},{128... | collective-permute-start | bytes 1622024 | tf_op jit(solution)/shard_map/ppermute | solution.py:46
  32.3 1.3 %collective-permute-done.5 = bf16[1056,128]{1,0:T(8,128)(2,1)S(1)} collective-permute-done((bf16[1056,128]{1,0:T(8,128)(2,1)S(1)}, bf16[1056,128]{1,0:T(8,128)(2,1)S(1)}, u32[]{:S(2)}, u32[]{:S(2)}) %collective-permute-start.5) | collective-permute-done | bytes 270368 | tf_op jit(solution)/shard_map/ppermute | solution.py:46
  33.6 1.0 %collective-permute-start.6 = (bf16[1056,128]{1,0:T(8,128)(2,1)S(1)}, bf16[1056,128]{1,0:T(8,128)(2,1)S(1)}, u32[]{:S(2)}, u32[]{:S(2)}) collective-permute-start(bf16[1056,128]{1,0:T(8,128)(2,1)S(1)} %collective-permute-done.5), channel_id=1, source_target_pairs={{0,200},{1,9},{8,64},{9,1},{64,8},{65,73},{72,128},{73,65},{128,72... | collective-permute-start | bytes 811016 | tf_op jit(solution)/shard_map/ppermute | solution.py:46
  34.6 0.0 collective-permute-done.9
  34.6 0.0 collective-permute-done.11
  34.6 5.0 %pair.4 = (f32[256,512]{1,0:T(8,128)S(1)}, f32[256,512]{1,0:T(8,128)S(1)}, f32[256,512]{1,0:T(8,128)S(1)}) custom-call(bf16[2,528,128]{2,1,0:T(8,128)(2,1)S(1)} %bitcast.36, bf16[2,528,128]{2,1,0:T(8,128)(2,1)S(1)} %bitcast.34, bf16[2,528,128]{2,1,0:T(8,128)(2,1)S(1)} %bitcast.32, bf16[4,528,128]{2,1,0:T(8,128)(2,1)S(1)} %bitcast.16, ...), custom_call_target="tpu_custom_call" | custom-call | flops 3221225472 | bytes 2883584 | tf_op jit(solution)/shard_map/pair/pallas_call | solution.py:163
  39.5 6.0 %collective-permute-done.7 = bf16[2112,128]{1,0:T(8,128)(2,1)S(1)} collective-permute-done((bf16[2112,128]{1,0:T(8,128)(2,1)S(1)}, bf16[2112,128]{1,0:T(8,128)(2,1)S(1)}, u32[]{:S(2)}, u32[]{:S(2)}) %collective-permute-start.7) | collective-permute-done | bytes 540704 | tf_op jit(solution)/shard_map/ppermute | solution.py:46
  45.5 0.0 collective-permute-done.8
  45.5 0.0 collective-permute-done.6
  45.5 0.0 collective-permute-start.12
  45.5 0.5 collective-permute-start.13
  46.0 2.4 %pair.6.refs_5_ = f32[256,512]{1,0:T(8,128)S(1)} custom-call(bf16[2,528,128]{2,1,0:T(8,128)(2,1)S(1)} %bitcast.38, bf16[4,528,128]{2,1,0:T(8,128)(2,1)S(1)} %bitcast.17, bf16[4,528,128]{2,1,0:T(8,128)(2,1)S(1)} %bitcast.25, bf16[4,528,128]{2,1,0:T(8,128)(2,1)S(1)} %bitcast.19, bf16[4,528,128]{2,1,0:T(8,128)(2,1)S(1)} %bitcast.27), custom_call_target="tpu_custom_call" | custom-call | flops 1073741824 | bytes 2359296 | tf_op jit(solution)/shard_map/pair/pallas_call | solution.py:163
  48.4 0.0 collective-permute-done.12
  48.4 0.0 collective-permute-done.13
  48.4 2.4 %pair.7 = bf16[256,512]{1,0:T(8,128)(2,1)S(1)} custom-call(bf16[2,528,128]{2,1,0:T(8,128)(2,1)S(1)} %bitcast.39, bf16[4,528,128]{2,1,0:T(8,128)(2,1)S(1)} %bitcast.20, bf16[4,528,128]{2,1,0:T(8,128)(2,1)S(1)} %bitcast.28, bf16[4,528,128]{2,1,0:T(8,128)(2,1)S(1)} %bitcast.22, bf16[4,528,128]{2,1,0:T(8,128)(2,1)S(1)} %bitcast.30, f32[256,512]{1,0:T(8,128)S(1)} %pair.6.refs_5_), custom_call_target="tpu_custom_call" | custom-call | flops 1073741824 | bytes 2359296 | tf_op jit(solution)/shard_map/pair/pallas_call | solution.py:163
  50.8 1.1 %collective-permute-start.15 = (bf16[256,512]{1,0:T(8,128)(2,1)S(1)}, bf16[256,512]{1,0:T(8,128)(2,1)S(1)}, u32[]{:S(2)}, u32[]{:S(2)}) collective-permute-start(bf16[256,512]{1,0:T(8,128)(2,1)S(1)} %pair.7), channel_id=1, source_target_pairs={{0,200},{1,9},{8,64},{9,1},{64,8},{65,73},{72,128},{73,65},{128,72... | collective-permute-start | bytes 786440 | tf_op jit(solution)/shard_map/ppermute | solution.py:46
  51.9 5.1 %pair.5 = (f32[256,512]{1,0:T(8,128)S(1)}, f32[256,512]{1,0:T(8,128)S(1)}, f32[256,512]{1,0:T(8,128)S(1)}) custom-call(bf16[2,528,128]{2,1,0:T(8,128)(2,1)S(1)} %bitcast.37, bf16[2,528,128]{2,1,0:T(8,128)(2,1)S(1)} %bitcast.35, bf16[2,528,128]{2,1,0:T(8,128)(2,1)S(1)} %bitcast.33, bf16[4,528,128]{2,1,0:T(8,128)(2,1)S(1)} %bitcast.21, ...), custom_call_target="tpu_custom_call" | custom-call | flops 3221225472 | bytes 2883584 | tf_op jit(solution)/shard_map/pair/pallas_call | solution.py:163
  56.9 0.3 collective-permute-done.15
  57.3 0.1 add_convert_fusion.1
  57.3 1.3 %collective-permute-start.16 = (bf16[256,512]{1,0:T(8,128)(2,1)S(1)}, bf16[256,512]{1,0:T(8,128)(2,1)S(1)}, u32[]{:S(2)}, u32[]{:S(2)}) collective-permute-start(bf16[256,512]{1,0:T(8,128)(2,1)S(1)} %add_convert_fusion.1), channel_id=1, source_target_pairs={{0,8},{1,201},{8,0},{9,65},{64,72},{65,9},{72,64},{73,129},{128,13... | collective-permute-start | bytes 786440 | tf_op jit(solution)/shard_map/ppermute | solution.py:46
  58.7 0.9 %collective-permute-start.14 = (bf16[128,512]{1,0:T(8,128)(2,1)S(1)}, bf16[128,512]{1,0:T(8,128)(2,1)S(1)}, u32[]{:S(2)}, u32[]{:S(2)}) collective-permute-start(bf16[128,512]{1,0:T(8,128)(2,1)S(1)} %slice.21), channel_id=1, source_target_pairs={{0,8},{1,201},{8,0},{9,65},{64,72},{65,9},{72,64},{73,129},{128,13... | collective-permute-start | bytes 393224 | tf_op jit(solution)/shard_map/ppermute | solution.py:46
  59.6 4.2 %collective-permute-done.16 = bf16[256,512]{1,0:T(8,128)(2,1)S(1)} collective-permute-done((bf16[256,512]{1,0:T(8,128)(2,1)S(1)}, bf16[256,512]{1,0:T(8,128)(2,1)S(1)}, u32[]{:S(2)}, u32[]{:S(2)}) %collective-permute-start.16) | collective-permute-done | bytes 262176 | tf_op jit(solution)/shard_map/ppermute | solution.py:46
  63.8 0.1 add_convert_fusion
  63.9 1.1 %collective-permute-start.17 = (bf16[128,512]{1,0:T(8,128)(2,1)S(1)}, bf16[128,512]{1,0:T(8,128)(2,1)S(1)}, u32[]{:S(2)}, u32[]{:S(2)}) collective-permute-start(bf16[128,512]{1,0:T(8,128)(2,1)S(1)} %get-tuple-element.34), channel_id=1, source_target_pairs={{0,200},{1,9},{8,64},{9,1},{64,8},{65,73},{72,128},{73,65},{128,72... | collective-permute-start | bytes 393224 | tf_op jit(solution)/shard_map/ppermute | solution.py:46
  65.0 0.0 copy-start.1
  65.0 2.7 %collective-permute-start.18 = (bf16[128,512]{1,0:T(8,128)(2,1)S(1)}, bf16[128,512]{1,0:T(8,128)(2,1)S(1)}, u32[]{:S(2)}, u32[]{:S(2)}) collective-permute-start(bf16[128,512]{1,0:T(8,128)(2,1)S(1)} %get-tuple-element.33), channel_id=1, source_target_pairs={{0,192},{1,65},{8,72},{9,201},{64,0},{65,129},{72,136},{73,9},{128... | collective-permute-start | bytes 393224 | tf_op jit(solution)/shard_map/ppermute | solution.py:54
  67.7 0.0 collective-permute-done.14.refs_0_
  67.7 2.7 %collective-permute-done.17.refs_1_ = bf16[128,512]{1,0:T(8,128)(2,1)S(1)} collective-permute-done((bf16[128,512]{1,0:T(8,128)(2,1)S(1)}, bf16[128,512]{1,0:T(8,128)(2,1)S(1)}, u32[]{:S(2)}, u32[]{:S(2)}) %collective-permute-start.17) | collective-permute-done | bytes 131104 | tf_op jit(solution)/shard_map/ppermute | solution.py:46
  70.4 2.9 %collective-permute-done.18.refs_2_ = bf16[128,512]{1,0:T(8,128)(2,1)S(1)} collective-permute-done((bf16[128,512]{1,0:T(8,128)(2,1)S(1)}, bf16[128,512]{1,0:T(8,128)(2,1)S(1)}, u32[]{:S(2)}, u32[]{:S(2)}) %collective-permute-start.18) | collective-permute-done | bytes 131104 | tf_op jit(solution)/shard_map/ppermute | solution.py:54
  73.2 0.0 copy-done.1
  73.2 0.9 %final.1 = f32[128,512]{1,0:T(8,128)} custom-call(f32[128,512]{1,0:T(8,128)S(1)} %copy-done.1, f32[128,512]{1,0:T(8,128)S(1)} %slice.13.own, bf16[128,512]{1,0:T(8,128)(2,1)S(1)} %collective-permute-done.14.refs_0_, bf16[128,512]{1,0:T(8,128)(2,1)S(1)} %collective-permute-done.17.refs_1_, bf16[128,512]{1,0:T(8,128)(2,1)S(1)} %collective-permute-done.18.refs_2_), custom_call_target="tpu_custom_call" | custom-call | tf_op jit(solution)/shard_map/final/pallas_call | solution.py:249
  (3 shorter events, 0.1 us)
Async XLA Ops:
  0.0 0.7 copy-start.2
  0.0 0.7 copy-start.3
  0.7 0.9 %copy-start = (f32[128,512]{1,0:T(8,128)S(1)}, f32[128,512]{1,0:T(8,128)}, u32[]{:S(2)}) copy-start(f32[128,512]{1,0:T(8,128)} %emb.3) | copy-start | bytes 786436
  1.8 5.4 %collective-permute-start = (bf16[528,128]{1,0:T(8,128)(2,1)S(1)}, bf16[528,128]{1,0:T(8,128)(2,1)S(1)}, u32[]{:S(2)}, u32[]{:S(2)}) collective-permute-start(bf16[528,128]{1,0:T(8,128)(2,1)S(1)} %pack.1.refs_0_), channel_id=1, source_target_pairs={{0,8},{1,201},{8,0},{9,65},{64,72},{65,9},{72,64},{73,129},{128,13... | collective-permute-start | bytes 405512 | tf_op jit(solution)/shard_map/ppermute | solution.py:46
  3.7 5.0 %collective-permute-start.1 = (bf16[528,128]{1,0:T(8,128)(2,1)S(1)}, bf16[528,128]{1,0:T(8,128)(2,1)S(1)}, u32[]{:S(2)}, u32[]{:S(2)}) collective-permute-start(bf16[528,128]{1,0:T(8,128)(2,1)S(1)} %pack.1.refs_0_), channel_id=1, source_target_pairs={{0,16},{1,49},{8,24},{9,57},{64,80},{65,113},{72,88},{73,121},{128... | collective-permute-start | bytes 405512 | tf_op jit(solution)/shard_map/ppermute | solution.py:46
  3.7 5.0 %collective-permute-start.2 = (bf16[528,128]{1,0:T(8,128)(2,1)S(1)}, bf16[528,128]{1,0:T(8,128)(2,1)S(1)}, u32[]{:S(2)}, u32[]{:S(2)}) collective-permute-start(bf16[528,128]{1,0:T(8,128)(2,1)S(1)} %pack.1.refs_0_), channel_id=1, source_target_pairs={{0,2},{1,7},{8,10},{9,15},{64,66},{65,71},{72,74},{73,79},{128,130... | collective-permute-start | bytes 405512 | tf_op jit(solution)/shard_map/ppermute | solution.py:46
  5.0 5.9 %collective-permute-start.3 = (bf16[528,128]{1,0:T(8,128)(2,1)S(1)}, bf16[528,128]{1,0:T(8,128)(2,1)S(1)}, u32[]{:S(2)}, u32[]{:S(2)}) collective-permute-start(bf16[528,128]{1,0:T(8,128)(2,1)S(1)} %pack.1.refs_0_), channel_id=1, source_target_pairs={{0,18},{1,55},{8,26},{9,63},{64,82},{65,119},{72,90},{73,127},{128... | collective-permute-start | bytes 405512 | tf_op jit(solution)/shard_map/ppermute | solution.py:46
  12.0 10.7 %collective-permute-start.10 = (bf16[2112,128]{1,0:T(8,128)(2,1)S(1)}, bf16[2112,128]{1,0:T(8,128)(2,1)S(1)}, u32[]{:S(2)}, u32[]{:S(2)}) collective-permute-start(bf16[2112,128]{1,0:T(8,128)(2,1)S(1)} %get-tuple-element.20), channel_id=1, source_target_pairs={{0,48},{1,17},{8,56},{9,25},{64,112},{65,81},{72,120},{73,89},{128... | collective-permute-start | bytes 1622024 | tf_op jit(solution)/shard_map/ppermute | solution.py:46
  14.2 10.9 %collective-permute-start.4 = (bf16[1056,128]{1,0:T(8,128)(2,1)S(1)}, bf16[1056,128]{1,0:T(8,128)(2,1)S(1)}, u32[]{:S(2)}, u32[]{:S(2)}) collective-permute-start(bf16[1056,128]{1,0:T(8,128)(2,1)S(1)} %get-tuple-element.19), channel_id=1, source_target_pairs={{0,200},{1,9},{8,64},{9,1},{64,8},{65,73},{72,128},{73,65},{128,72... | collective-permute-start | bytes 811016 | tf_op jit(solution)/shard_map/ppermute | solution.py:46
  17.9 16.7 %collective-permute-start.9 = (bf16[2112,128]{1,0:T(8,128)(2,1)S(1)}, bf16[2112,128]{1,0:T(8,128)(2,1)S(1)}, u32[]{:S(2)}, u32[]{:S(2)}) collective-permute-start(bf16[2112,128]{1,0:T(8,128)(2,1)S(1)} %get-tuple-element.20), channel_id=1, source_target_pairs={{0,1},{1,0},{2,3},{3,2},{4,5},{5,4},{6,7},{7,6},{8,9},{9,8},{10,11... | collective-permute-start | bytes 1622024 | tf_op jit(solution)/shard_map/ppermute | solution.py:58
  22.7 11.9 %collective-permute-start.11 = (bf16[2112,128]{1,0:T(8,128)(2,1)S(1)}, bf16[2112,128]{1,0:T(8,128)(2,1)S(1)}, u32[]{:S(2)}, u32[]{:S(2)}) collective-permute-start(bf16[2112,128]{1,0:T(8,128)(2,1)S(1)} %collective-permute-done.10), channel_id=1, source_target_pairs={{0,1},{1,0},{2,3},{3,2},{4,5},{5,4},{6,7},{7,6},{8,9},{9,8},{10,11... | collective-permute-start | bytes 1622024 | tf_op jit(solution)/shard_map/ppermute | solution.py:58
  25.1 8.5 %collective-permute-start.5 = (bf16[1056,128]{1,0:T(8,128)(2,1)S(1)}, bf16[1056,128]{1,0:T(8,128)(2,1)S(1)}, u32[]{:S(2)}, u32[]{:S(2)}) collective-permute-start(bf16[1056,128]{1,0:T(8,128)(2,1)S(1)} %collective-permute-done.4), channel_id=1, source_target_pairs={{0,8},{1,201},{8,0},{9,65},{64,72},{65,9},{72,64},{73,129},{128,13... | collective-permute-start | bytes 811016 | tf_op jit(solution)/shard_map/ppermute | solution.py:46
  29.1 16.4 %collective-permute-start.7 = (bf16[2112,128]{1,0:T(8,128)(2,1)S(1)}, bf16[2112,128]{1,0:T(8,128)(2,1)S(1)}, u32[]{:S(2)}, u32[]{:S(2)}) collective-permute-start(bf16[2112,128]{1,0:T(8,128)(2,1)S(1)} %get-tuple-element.20), channel_id=1, source_target_pairs={{0,6},{1,3},{8,14},{9,11},{64,70},{65,67},{72,78},{73,75},{128,134... | collective-permute-start | bytes 1622024 | tf_op jit(solution)/shard_map/ppermute | solution.py:46
  29.4 16.1 %collective-permute-start.8 = (bf16[2112,128]{1,0:T(8,128)(2,1)S(1)}, bf16[2112,128]{1,0:T(8,128)(2,1)S(1)}, u32[]{:S(2)}, u32[]{:S(2)}) collective-permute-start(bf16[2112,128]{1,0:T(8,128)(2,1)S(1)} %get-tuple-element.20), channel_id=1, source_target_pairs={{0,54},{1,19},{8,62},{9,27},{64,118},{65,83},{72,126},{73,91},{128... | collective-permute-start | bytes 1622024 | tf_op jit(solution)/shard_map/ppermute | solution.py:46
  33.6 11.9 %collective-permute-start.6 = (bf16[1056,128]{1,0:T(8,128)(2,1)S(1)}, bf16[1056,128]{1,0:T(8,128)(2,1)S(1)}, u32[]{:S(2)}, u32[]{:S(2)}) collective-permute-start(bf16[1056,128]{1,0:T(8,128)(2,1)S(1)} %collective-permute-done.5), channel_id=1, source_target_pairs={{0,200},{1,9},{8,64},{9,1},{64,8},{65,73},{72,128},{73,65},{128,72... | collective-permute-start | bytes 811016 | tf_op jit(solution)/shard_map/ppermute | solution.py:46
  45.5 2.9 %collective-permute-start.12 = (bf16[2112,128]{1,0:T(8,128)(2,1)S(1)}, bf16[2112,128]{1,0:T(8,128)(2,1)S(1)}, u32[]{:S(2)}, u32[]{:S(2)}) collective-permute-start(bf16[2112,128]{1,0:T(8,128)(2,1)S(1)} %collective-permute-done.7), channel_id=1, source_target_pairs={{0,1},{1,0},{2,3},{3,2},{4,5},{5,4},{6,7},{7,6},{8,9},{9,8},{10,11... | collective-permute-start | bytes 1622024 | tf_op jit(solution)/shard_map/ppermute | solution.py:58
  45.5 2.9 %collective-permute-start.13 = (bf16[2112,128]{1,0:T(8,128)(2,1)S(1)}, bf16[2112,128]{1,0:T(8,128)(2,1)S(1)}, u32[]{:S(2)}, u32[]{:S(2)}) collective-permute-start(bf16[2112,128]{1,0:T(8,128)(2,1)S(1)} %collective-permute-done.8), channel_id=1, source_target_pairs={{0,1},{1,0},{2,3},{3,2},{4,5},{5,4},{6,7},{7,6},{8,9},{9,8},{10,11... | collective-permute-start | bytes 1622024 | tf_op jit(solution)/shard_map/ppermute | solution.py:58
  50.8 6.5 %collective-permute-start.15 = (bf16[256,512]{1,0:T(8,128)(2,1)S(1)}, bf16[256,512]{1,0:T(8,128)(2,1)S(1)}, u32[]{:S(2)}, u32[]{:S(2)}) collective-permute-start(bf16[256,512]{1,0:T(8,128)(2,1)S(1)} %pair.7), channel_id=1, source_target_pairs={{0,200},{1,9},{8,64},{9,1},{64,8},{65,73},{72,128},{73,65},{128,72... | collective-permute-start | bytes 786440 | tf_op jit(solution)/shard_map/ppermute | solution.py:46
  57.3 6.5 %collective-permute-start.16 = (bf16[256,512]{1,0:T(8,128)(2,1)S(1)}, bf16[256,512]{1,0:T(8,128)(2,1)S(1)}, u32[]{:S(2)}, u32[]{:S(2)}) collective-permute-start(bf16[256,512]{1,0:T(8,128)(2,1)S(1)} %add_convert_fusion.1), channel_id=1, source_target_pairs={{0,8},{1,201},{8,0},{9,65},{64,72},{65,9},{72,64},{73,129},{128,13... | collective-permute-start | bytes 786440 | tf_op jit(solution)/shard_map/ppermute | solution.py:46
  58.7 9.0 %collective-permute-start.14 = (bf16[128,512]{1,0:T(8,128)(2,1)S(1)}, bf16[128,512]{1,0:T(8,128)(2,1)S(1)}, u32[]{:S(2)}, u32[]{:S(2)}) collective-permute-start(bf16[128,512]{1,0:T(8,128)(2,1)S(1)} %slice.21), channel_id=1, source_target_pairs={{0,8},{1,201},{8,0},{9,65},{64,72},{65,9},{72,64},{73,129},{128,13... | collective-permute-start | bytes 393224 | tf_op jit(solution)/shard_map/ppermute | solution.py:46
  63.9 6.5 %collective-permute-start.17 = (bf16[128,512]{1,0:T(8,128)(2,1)S(1)}, bf16[128,512]{1,0:T(8,128)(2,1)S(1)}, u32[]{:S(2)}, u32[]{:S(2)}) collective-permute-start(bf16[128,512]{1,0:T(8,128)(2,1)S(1)} %get-tuple-element.34), channel_id=1, source_target_pairs={{0,200},{1,9},{8,64},{9,1},{64,8},{65,73},{72,128},{73,65},{128,72... | collective-permute-start | bytes 393224 | tf_op jit(solution)/shard_map/ppermute | solution.py:46
  65.0 8.2 %copy-start.1 = (f32[128,512]{1,0:T(8,128)S(1)}, f32[128,512]{1,0:T(8,128)}, u32[]{:S(2)}) copy-start(f32[128,512]{1,0:T(8,128)} %emb.3) | copy-start | bytes 786436
  65.0 8.2 %collective-permute-start.18 = (bf16[128,512]{1,0:T(8,128)(2,1)S(1)}, bf16[128,512]{1,0:T(8,128)(2,1)S(1)}, u32[]{:S(2)}, u32[]{:S(2)}) collective-permute-start(bf16[128,512]{1,0:T(8,128)(2,1)S(1)} %get-tuple-element.33), channel_id=1, source_target_pairs={{0,192},{1,65},{8,72},{9,201},{64,0},{65,129},{72,136},{73,9},{128... | collective-permute-start | bytes 393224 | tf_op jit(solution)/shard_map/ppermute | solution.py:54

commit v4 on v3

--- a/solution.py
+++ b/solution.py
@@ -156,7 +156,7 @@
         o += n
 
 
-def pair(r_in, c_in, out_dtype, sums=()):
+def pair(r_in, c_in, out_dtype, sums=(), weight=1.0):
     r_in, c_in = ([a.reshape(-1, PACKED, LANES) for a in v] for v in (r_in, c_in))
     r_blocks, c_blocks = (sum(a.shape[0] for a in v) for v in (r_in, c_in))
     rows, n_c = r_blocks * CPD, len(c_in)
@@ -178,7 +178,8 @@
         ],
         compiler_params=pltpu.CompilerParams(vmem_limit_bytes=20 << 20),
         cost_estimate=pl.CostEstimate(
-            flops=4 * rows * c_blocks * CPD * D, bytes_accessed=(c_blocks * CPD + rows) * D * 2, transcendentals=0
+            flops=int(weight * 4 * rows * c_blocks * CPD * D),
+            bytes_accessed=int(weight * (c_blocks * CPD + rows) * D * 2), transcendentals=0
         ),
         name="pair",
     )(*r_in, *c_in, *sums)
@@ -227,21 +228,22 @@
 
     near = swap(whole, "za", "zb")
     square = [swap(whole, a, b) for a, b in (("xa", "xb"), ("ya", "yb"), ("xaya", "xbyb"))]
-    both, c0 = join(((0, 1), (0, 2, 3, 4)), whole, near, *square)
+    (both,) = join(((0, 1),), whole, near)
     back = swap(both, "zb", "za")
+    (c0,) = join(((0, 1, 2, 3),), whole, *square)
+    far, ahead = shift(back, 1), swap(back, "za", "zb")
     c3, c1, c2 = (swap(c0, b, a) for a, b in (("xaya", "xbyb"), ("xa", "xb"), ("ya", "yb")))
-    ahead = swap(back, "za", "zb")
-    far = swap(ahead, "zb", "za")
-    e0, e1 = swap_cores(c0), swap_cores(c1)
-    sums = pair([ahead, back, both], [c0, e0, c1, e1], F32)
-    far, c2, c3, *sums = lax.optimization_barrier((far, c2, c3, *sums))
-    e2, e3 = swap_cores(c2), swap_cores(c3)
-    (p_far,) = pair([far], [c0, e0, c1, e1], F32)
-    (p_far,) = pair([far], [c2, e2, c3, e3], BF, [p_far])
+    e0 = swap_cores(c0)
+    far, ahead, c1, c2, c3 = lax.optimization_barrier((far, ahead, c1, c2, c3))
+    e1, e2, e3 = swap_cores(c1), swap_cores(c2), swap_cores(c3)
+    cols = [c0, c1, c2, c3, e0, e1, e2, e3]
+    (p_far,) = pair([far], cols[:4], F32)
+    (p_far,) = pair([far], cols[4:], BF, [p_far])
     q = swap(p_far, "zb", "za")
-    p_ahead, p_back, p_own = pair([ahead, back, both], [c2, e2, c3, e3], F32, sums)
+    p_ahead, p_own = pair([ahead, both], cols, F32)
     q_near = swap(p_own[CPD:].astype(BF), "za", "zb")
     q = swap((p_ahead + q).astype(BF), "za", "zb")
+    (p_back,) = pair([back], cols, F32)
     p_back = (p_back + q).astype(BF)
     arrived = (q_near, swap(p_back[:CPD], "zb", "za"), shift(p_back[CPD:], -1))
 

time: 74.3 us -> 66.5 us (0.90)
  the two profiles are of different devices: /device:TPU:32 before, /device:TPU:1 now
where the time goes in v4:
time: 66.5 us; the launch traced here: 65.4 us
  starting transfers between devices  24.7 us (37%)
  waiting for transfers between devices  20.6 us (31%)
  Pallas kernels  18.2 us (27%)
  local copies, waits for them, and re-layouts  1.68 us (3%)
    ppermute x13, starting transfers between devices, swap(): return lax.ppermute(block, AXES, pairs)  18 us
    pallas_call x4, Pallas kernels, pair(): pl.pallas_call(functools.partial(pair_kernel, len(r_in), n_c, len(sums)),...  16 us
    ppermute x13, waiting for transfers between devices, swap(): return lax.ppermute(block, AXES, pairs)  10.6 us
    ppermute x2, waiting for transfers between devices, shift(): return lax.ppermute(block, AXES, pairs)  9.78 us
    ppermute x4, starting transfers between devices, swap_cores(): return lax.ppermute(block, AXES, [(i, i ^ 1) for i in range(256)])  3.77 us
    ppermute x2, starting transfers between devices, shift(): return lax.ppermute(block, AXES, pairs)  2.94 us
    unnamed x8, local copies, waits for them, and re-layouts  1.62 us
  transfers between devices with their start and end apart: 19, of which 8 were waited for; matrix products, arithmetic and copies ran while one was open for 0% of the time, Pallas kernels for 22%

profile of v4, /device:TPU:1, one launch (start us, length us, event | category | flops | bytes accessed | tf_op | source)
XLA Modules:
  0.0 65.4 jit_solution(5283261902845467338)
XLA Ops:
  0.0 0.0 copy-start.2
  0.0 0.0 copy-start.3
  0.0 0.7 copy-done.2
  0.7 0.0 copy-done.3
  0.7 0.0 copy-start
  0.7 0.9 %copy-done = f32[128,512]{1,0:T(8,128)S(1)} copy-done((f32[128,512]{1,0:T(8,128)S(1)}, f32[128,512]{1,0:T(8,128)}, u32[]{:S(2)}) %copy-start) | copy-done | bytes 262168
  1.6 0.1 pack.1.refs_0_
  1.8 6.5 %collective-permute-start = (bf16[528,128]{1,0:T(8,128)(2,1)S(1)}, bf16[528,128]{1,0:T(8,128)(2,1)S(1)}, u32[]{:S(2)}, u32[]{:S(2)}) collective-permute-start(bf16[528,128]{1,0:T(8,128)(2,1)S(1)} %pack.1.refs_0_), channel_id=1, source_target_pairs={{0,8},{1,201},{8,0},{9,65},{64,72},{65,9},{72,64},{73,129},{128,13... | collective-permute-start | bytes 405512 | tf_op jit(solution)/shard_map/ppermute | solution.py:46
  8.2 2.5 %collective-permute-start.4 = (bf16[528,128]{1,0:T(8,128)(2,1)S(1)}, bf16[528,128]{1,0:T(8,128)(2,1)S(1)}, u32[]{:S(2)}, u32[]{:S(2)}) collective-permute-start(bf16[528,128]{1,0:T(8,128)(2,1)S(1)} %pack.1.refs_0_), channel_id=1, source_target_pairs={{0,16},{1,49},{8,24},{9,57},{64,80},{65,113},{72,88},{73,121},{128... | collective-permute-start | bytes 405512 | tf_op jit(solution)/shard_map/ppermute | solution.py:46
  10.7 2.7 %collective-permute-start.5 = (bf16[528,128]{1,0:T(8,128)(2,1)S(1)}, bf16[528,128]{1,0:T(8,128)(2,1)S(1)}, u32[]{:S(2)}, u32[]{:S(2)}) collective-permute-start(bf16[528,128]{1,0:T(8,128)(2,1)S(1)} %pack.1.refs_0_), channel_id=1, source_target_pairs={{0,2},{1,7},{8,10},{9,15},{64,66},{65,71},{72,74},{73,79},{128,130... | collective-permute-start | bytes 405512 | tf_op jit(solution)/shard_map/ppermute | solution.py:46
  13.5 0.0 collective-permute-start.6
  13.5 0.0 collective-permute-done.refs_1_
  13.5 0.4 join.2
  13.8 0.1 collective-permute-start.1
  13.9 0.0 collective-permute-done.4.refs_1_
  13.9 2.2 %collective-permute-done.5.refs_2_ = bf16[528,128]{1,0:T(8,128)(2,1)S(1)} collective-permute-done((bf16[528,128]{1,0:T(8,128)(2,1)S(1)}, bf16[528,128]{1,0:T(8,128)(2,1)S(1)}, u32[]{:S(2)}, u32[]{:S(2)}) %collective-permute-start.5) | collective-permute-done | bytes 135200 | tf_op jit(solution)/shard_map/ppermute | solution.py:46
  16.2 4.5 %collective-permute-done.6.refs_3_ = bf16[528,128]{1,0:T(8,128)(2,1)S(1)} collective-permute-done((bf16[528,128]{1,0:T(8,128)(2,1)S(1)}, bf16[528,128]{1,0:T(8,128)(2,1)S(1)}, u32[]{:S(2)}, u32[]{:S(2)}) %collective-permute-start.6) | collective-permute-done | bytes 135200 | tf_op jit(solution)/shard_map/ppermute | solution.py:46
  20.6 0.7 %join.3 = bf16[2112,128]{1,0:T(8,128)(2,1)S(1)} custom-call(bf16[528,128]{1,0:T(8,128)(2,1)S(1)} %pack.1.refs_0_, bf16[528,128]{1,0:T(8,128)(2,1)S(1)} %collective-permute-done.4.refs_1_, bf16[528,128]{1,0:T(8,128)(2,1)S(1)} %collective-permute-done.5.refs_2_, bf16[528,128]{1,0:T(8,128)(2,1)S(1)} %collective-permute-done.6.refs_3_), custom_call_target="tpu_custom_call" | custom-call | tf_op jit(solution)/shard_map/join/pallas_call | solution.py:204
  21.4 0.1 collective-permute-start.7
  21.5 0.1 collective-permute-start.8
  21.6 2.5 %collective-permute-start.9 = (bf16[2112,128]{1,0:T(8,128)(2,1)S(1)}, bf16[2112,128]{1,0:T(8,128)(2,1)S(1)}, u32[]{:S(2)}, u32[]{:S(2)}) collective-permute-start(bf16[2112,128]{1,0:T(8,128)(2,1)S(1)} %join.3), channel_id=1, source_target_pairs={{0,54},{1,19},{8,62},{9,27},{64,118},{65,83},{72,126},{73,91},{128... | collective-permute-start | bytes 1622024 | tf_op jit(solution)/shard_map/ppermute | solution.py:46
  24.1 0.0 collective-permute-done.1
  24.1 1.2 %collective-permute-start.2 = (bf16[1056,128]{1,0:T(8,128)(2,1)S(1)}, bf16[1056,128]{1,0:T(8,128)(2,1)S(1)}, u32[]{:S(2)}, u32[]{:S(2)}) collective-permute-start(bf16[1056,128]{1,0:T(8,128)(2,1)S(1)} %collective-permute-done.1), channel_id=1, source_target_pairs={{0,64},{1,193},{8,200},{9,73},{64,128},{65,1},{72,8},{73,137},{128... | collective-permute-start | bytes 811016 | tf_op jit(solution)/shard_map/ppermute | solution.py:54
  25.3 0.0 collective-permute-start.3
  25.3 6.3 %collective-permute-done.2 = bf16[1056,128]{1,0:T(8,128)(2,1)S(1)} collective-permute-done((bf16[1056,128]{1,0:T(8,128)(2,1)S(1)}, bf16[1056,128]{1,0:T(8,128)(2,1)S(1)}, u32[]{:S(2)}, u32[]{:S(2)}) %collective-permute-start.2) | collective-permute-done | bytes 270368 | tf_op jit(solution)/shard_map/ppermute | solution.py:54
  31.5 2.2 %collective-permute-start.10 = (bf16[2112,128]{1,0:T(8,128)(2,1)S(1)}, bf16[2112,128]{1,0:T(8,128)(2,1)S(1)}, u32[]{:S(2)}, u32[]{:S(2)}) collective-permute-start(bf16[2112,128]{1,0:T(8,128)(2,1)S(1)} %join.3), channel_id=1, source_target_pairs={{0,1},{1,0},{2,3},{3,2},{4,5},{5,4},{6,7},{7,6},{8,9},{9,8},{10,11... | collective-permute-start | bytes 1622024 | tf_op jit(solution)/shard_map/ppermute | solution.py:58
  33.8 0.8 %collective-permute-done.3 = bf16[1056,128]{1,0:T(8,128)(2,1)S(1)} collective-permute-done((bf16[1056,128]{1,0:T(8,128)(2,1)S(1)}, bf16[1056,128]{1,0:T(8,128)(2,1)S(1)}, u32[]{:S(2)}, u32[]{:S(2)}) %collective-permute-start.3) | collective-permute-done | bytes 270368 | tf_op jit(solution)/shard_map/ppermute | solution.py:46
  34.6 0.0 collective-permute-done.7
  34.6 1.3 %collective-permute-done.8 = bf16[2112,128]{1,0:T(8,128)(2,1)S(1)} collective-permute-done((bf16[2112,128]{1,0:T(8,128)(2,1)S(1)}, bf16[2112,128]{1,0:T(8,128)(2,1)S(1)}, u32[]{:S(2)}, u32[]{:S(2)}) %collective-permute-start.8) | collective-permute-done | bytes 540704 | tf_op jit(solution)/shard_map/ppermute | solution.py:46
  35.8 0.0 collective-permute-done.9
  35.8 1.0 %collective-permute-start.12 = (bf16[2112,128]{1,0:T(8,128)(2,1)S(1)}, bf16[2112,128]{1,0:T(8,128)(2,1)S(1)}, u32[]{:S(2)}, u32[]{:S(2)}) collective-permute-start(bf16[2112,128]{1,0:T(8,128)(2,1)S(1)} %collective-permute-done.8), channel_id=1, source_target_pairs={{0,1},{1,0},{2,3},{3,2},{4,5},{5,4},{6,7},{7,6},{8,9},{9,8},{10,11... | collective-permute-start | bytes 1622024 | tf_op jit(solution)/shard_map/ppermute | solution.py:58
  36.9 0.1 collective-permute-start.13
  37.0 0.4 collective-permute-start.11
  37.4 2.4 %pair.6.refs_5_ = f32[256,512]{1,0:T(8,128)S(1)} custom-call(bf16[2,528,128]{2,1,0:T(8,128)(2,1)S(1)} %bitcast.43, bf16[4,528,128]{2,1,0:T(8,128)(2,1)S(1)} %bitcast.14, bf16[4,528,128]{2,1,0:T(8,128)(2,1)S(1)} %bitcast.20, bf16[4,528,128]{2,1,0:T(8,128)(2,1)S(1)} %bitcast.23, bf16[4,528,128]{2,1,0:T(8,128)(2,1)S(1)} %bitcast.26), custom_call_target="tpu_custom_call" | custom-call | flops 1073741824 | bytes 2359296 | tf_op jit(solution)/shard_map/pair/pallas_call | solution.py:163
  39.8 0.0 collective-permute-done.10
  39.8 0.0 collective-permute-done.12
  39.8 0.0 collective-permute-done.13
  39.8 0.2 collective-permute-done.11
  40.0 2.4 %pair.7 = bf16[256,512]{1,0:T(8,128)(2,1)S(1)} custom-call(bf16[2,528,128]{2,1,0:T(8,128)(2,1)S(1)} %bitcast.44, bf16[4,528,128]{2,1,0:T(8,128)(2,1)S(1)} %bitcast.29, bf16[4,528,128]{2,1,0:T(8,128)(2,1)S(1)} %bitcast.38, bf16[4,528,128]{2,1,0:T(8,128)(2,1)S(1)} %bitcast.32, bf16[4,528,128]{2,1,0:T(8,128)(2,1)S(1)} %bitcast.35, f32[256,512]{1,0:T(8,128)S(1)} %pair.6.refs_5_), custom_call_target="tpu_custom_call" | custom-call | flops 1073741824 | bytes 2359296 | tf_op jit(solution)/shard_map/pair/pallas_call | solution.py:163
  42.4 0.3 collective-permute-start.15
  42.7 6.8 %pair.4 = (f32[256,512]{1,0:T(8,128)S(1)}, f32[256,512]{1,0:T(8,128)S(1)}) custom-call(bf16[2,528,128]{2,1,0:T(8,128)(2,1)S(1)} %bitcast.42, bf16[2,528,128]{2,1,0:T(8,128)(2,1)S(1)} %bitcast.17, bf16[4,528,128]{2,1,0:T(8,128)(2,1)S(1)} %bitcast.15, bf16[4,528,128]{2,1,0:T(8,128)(2,1)S(1)} %bitcast.21, bf16[4,528,128]{2,1,0:T(8,128)(2,1)S(1)} %bitcast.24, ...), custom_call_target="tpu_custom_call" | custom-call | flops 4294967296 | bytes 4718592 | tf_op jit(solution)/shard_map/pair/pallas_call | solution.py:163
  49.5 0.0 collective-permute-done.15
  49.5 0.1 add_convert_fusion.1
  49.6 2.4 %collective-permute-start.16 = (bf16[256,512]{1,0:T(8,128)(2,1)S(1)}, bf16[256,512]{1,0:T(8,128)(2,1)S(1)}, u32[]{:S(2)}, u32[]{:S(2)}) collective-permute-start(bf16[256,512]{1,0:T(8,128)(2,1)S(1)} %add_convert_fusion.1), channel_id=1, source_target_pairs={{0,8},{1,201},{8,0},{9,65},{64,72},{65,9},{72,64},{73,129},{128,13... | collective-permute-start | bytes 786440 | tf_op jit(solution)/shard_map/ppermute | solution.py:46
  52.0 0.5 collective-permute-start.14
  52.5 4.4 %pair.5 = f32[256,512]{1,0:T(8,128)S(1)} custom-call(bf16[2,528,128]{2,1,0:T(8,128)(2,1)S(1)} %bitcast.41, bf16[4,528,128]{2,1,0:T(8,128)(2,1)S(1)} %bitcast.16, bf16[4,528,128]{2,1,0:T(8,128)(2,1)S(1)} %bitcast.22, bf16[4,528,128]{2,1,0:T(8,128)(2,1)S(1)} %bitcast.25, bf16[4,528,128]{2,1,0:T(8,128)(2,1)S(1)} %bitcast.28, bf16[4,528,128]{2,1,0:T(8,128)(2,1)S(1)} %bitcast.31, ...), custom_call_target="tpu_custom_call" | custom-call | flops 2147483648 | bytes 4456448 | tf_op jit(solution)/shard_map/pair/pallas_call | solution.py:163
  56.9 0.0 collective-permute-done.16
  57.0 0.1 add_convert_fusion
  57.1 0.3 collective-permute-start.17
  57.4 0.0 copy-start.1
  57.4 1.8 %collective-permute-start.18 = (bf16[128,512]{1,0:T(8,128)(2,1)S(1)}, bf16[128,512]{1,0:T(8,128)(2,1)S(1)}, u32[]{:S(2)}, u32[]{:S(2)}) collective-permute-start(bf16[128,512]{1,0:T(8,128)(2,1)S(1)} %get-tuple-element.19), channel_id=1, source_target_pairs={{0,192},{1,65},{8,72},{9,201},{64,0},{65,129},{72,136},{73,9},{128... | collective-permute-start | bytes 393224 | tf_op jit(solution)/shard_map/ppermute | solution.py:54
  59.2 0.0 collective-permute-done.14.refs_0_
  59.2 1.8 %collective-permute-done.17.refs_1_ = bf16[128,512]{1,0:T(8,128)(2,1)S(1)} collective-permute-done((bf16[128,512]{1,0:T(8,128)(2,1)S(1)}, bf16[128,512]{1,0:T(8,128)(2,1)S(1)}, u32[]{:S(2)}, u32[]{:S(2)}) %collective-permute-start.17) | collective-permute-done | bytes 131104 | tf_op jit(solution)/shard_map/ppermute | solution.py:46
  61.0 3.5 %collective-permute-done.18.refs_2_ = bf16[128,512]{1,0:T(8,128)(2,1)S(1)} collective-permute-done((bf16[128,512]{1,0:T(8,128)(2,1)S(1)}, bf16[128,512]{1,0:T(8,128)(2,1)S(1)}, u32[]{:S(2)}, u32[]{:S(2)}) %collective-permute-start.18) | collective-permute-done | bytes 131104 | tf_op jit(solution)/shard_map/ppermute | solution.py:54
  64.5 0.0 copy-done.1
  64.5 0.9 %final.1 = f32[128,512]{1,0:T(8,128)} custom-call(f32[128,512]{1,0:T(8,128)S(1)} %copy-done.1, f32[128,512]{1,0:T(8,128)S(1)} %slice.13.own, bf16[128,512]{1,0:T(8,128)(2,1)S(1)} %collective-permute-done.14.refs_0_, bf16[128,512]{1,0:T(8,128)(2,1)S(1)} %collective-permute-done.17.refs_1_, bf16[128,512]{1,0:T(8,128)(2,1)S(1)} %collective-permute-done.18.refs_2_), custom_call_target="tpu_custom_call" | custom-call | tf_op jit(solution)/shard_map/final/pallas_call | solution.py:251
  (3 shorter events, 0.1 us)
Async XLA Ops:
  0.0 0.7 %copy-start.2 = (s32[128]{0:T(128)S(1)}, s32[128]{0:T(128)}, u32[]{:S(2)}) copy-start(s32[128]{0:T(128)} %param.4) | copy-start | bytes 1540
  0.0 0.7 %copy-start.3 = (s32[128]{0:T(128)S(1)}, s32[128]{0:T(128)}, u32[]{:S(2)}) copy-start(s32[128]{0:T(128)} %param.5) | copy-start | bytes 1540
  0.7 0.9 %copy-start = (f32[128,512]{1,0:T(8,128)S(1)}, f32[128,512]{1,0:T(8,128)}, u32[]{:S(2)}) copy-start(f32[128,512]{1,0:T(8,128)} %emb.3) | copy-start | bytes 786436
  1.8 11.7 %collective-permute-start = (bf16[528,128]{1,0:T(8,128)(2,1)S(1)}, bf16[528,128]{1,0:T(8,128)(2,1)S(1)}, u32[]{:S(2)}, u32[]{:S(2)}) collective-permute-start(bf16[528,128]{1,0:T(8,128)(2,1)S(1)} %pack.1.refs_0_), channel_id=1, source_target_pairs={{0,8},{1,201},{8,0},{9,65},{64,72},{65,9},{72,64},{73,129},{128,13... | collective-permute-start | bytes 405512 | tf_op jit(solution)/shard_map/ppermute | solution.py:46
  8.2 5.7 %collective-permute-start.4 = (bf16[528,128]{1,0:T(8,128)(2,1)S(1)}, bf16[528,128]{1,0:T(8,128)(2,1)S(1)}, u32[]{:S(2)}, u32[]{:S(2)}) collective-permute-start(bf16[528,128]{1,0:T(8,128)(2,1)S(1)} %pack.1.refs_0_), channel_id=1, source_target_pairs={{0,16},{1,49},{8,24},{9,57},{64,80},{65,113},{72,88},{73,121},{128... | collective-permute-start | bytes 405512 | tf_op jit(solution)/shard_map/ppermute | solution.py:46
  10.7 5.4 %collective-permute-start.5 = (bf16[528,128]{1,0:T(8,128)(2,1)S(1)}, bf16[528,128]{1,0:T(8,128)(2,1)S(1)}, u32[]{:S(2)}, u32[]{:S(2)}) collective-permute-start(bf16[528,128]{1,0:T(8,128)(2,1)S(1)} %pack.1.refs_0_), channel_id=1, source_target_pairs={{0,2},{1,7},{8,10},{9,15},{64,66},{65,71},{72,74},{73,79},{128,130... | collective-permute-start | bytes 405512 | tf_op jit(solution)/shard_map/ppermute | solution.py:46
  13.5 7.2 %collective-permute-start.6 = (bf16[528,128]{1,0:T(8,128)(2,1)S(1)}, bf16[528,128]{1,0:T(8,128)(2,1)S(1)}, u32[]{:S(2)}, u32[]{:S(2)}) collective-permute-start(bf16[528,128]{1,0:T(8,128)(2,1)S(1)} %pack.1.refs_0_), channel_id=1, source_target_pairs={{0,18},{1,55},{8,26},{9,63},{64,82},{65,119},{72,90},{73,127},{128... | collective-permute-start | bytes 405512 | tf_op jit(solution)/shard_map/ppermute | solution.py:46
  13.8 10.3 %collective-permute-start.1 = (bf16[1056,128]{1,0:T(8,128)(2,1)S(1)}, bf16[1056,128]{1,0:T(8,128)(2,1)S(1)}, u32[]{:S(2)}, u32[]{:S(2)}) collective-permute-start(bf16[1056,128]{1,0:T(8,128)(2,1)S(1)} %join.2), channel_id=1, source_target_pairs={{0,200},{1,9},{8,64},{9,1},{64,8},{65,73},{72,128},{73,65},{128,72... | collective-permute-start | bytes 811016 | tf_op jit(solution)/shard_map/ppermute | solution.py:46
  21.4 13.2 %collective-permute-start.7 = (bf16[2112,128]{1,0:T(8,128)(2,1)S(1)}, bf16[2112,128]{1,0:T(8,128)(2,1)S(1)}, u32[]{:S(2)}, u32[]{:S(2)}) collective-permute-start(bf16[2112,128]{1,0:T(8,128)(2,1)S(1)} %join.3), channel_id=1, source_target_pairs={{0,48},{1,17},{8,56},{9,25},{64,112},{65,81},{72,120},{73,89},{128... | collective-permute-start | bytes 1622024 | tf_op jit(solution)/shard_map/ppermute | solution.py:46
  21.5 14.4 %collective-permute-start.8 = (bf16[2112,128]{1,0:T(8,128)(2,1)S(1)}, bf16[2112,128]{1,0:T(8,128)(2,1)S(1)}, u32[]{:S(2)}, u32[]{:S(2)}) collective-permute-start(bf16[2112,128]{1,0:T(8,128)(2,1)S(1)} %join.3), channel_id=1, source_target_pairs={{0,6},{1,3},{8,14},{9,11},{64,70},{65,67},{72,78},{73,75},{128,134... | collective-permute-start | bytes 1622024 | tf_op jit(solution)/shard_map/ppermute | solution.py:46
  21.6 14.3 %collective-permute-start.9 = (bf16[2112,128]{1,0:T(8,128)(2,1)S(1)}, bf16[2112,128]{1,0:T(8,128)(2,1)S(1)}, u32[]{:S(2)}, u32[]{:S(2)}) collective-permute-start(bf16[2112,128]{1,0:T(8,128)(2,1)S(1)} %join.3), channel_id=1, source_target_pairs={{0,54},{1,19},{8,62},{9,27},{64,118},{65,83},{72,126},{73,91},{128... | collective-permute-start | bytes 1622024 | tf_op jit(solution)/shard_map/ppermute | solution.py:46
  24.1 7.4 %collective-permute-start.2 = (bf16[1056,128]{1,0:T(8,128)(2,1)S(1)}, bf16[1056,128]{1,0:T(8,128)(2,1)S(1)}, u32[]{:S(2)}, u32[]{:S(2)}) collective-permute-start(bf16[1056,128]{1,0:T(8,128)(2,1)S(1)} %collective-permute-done.1), channel_id=1, source_target_pairs={{0,64},{1,193},{8,200},{9,73},{64,128},{65,1},{72,8},{73,137},{128... | collective-permute-start | bytes 811016 | tf_op jit(solution)/shard_map/ppermute | solution.py:54
  25.3 9.3 %collective-permute-start.3 = (bf16[1056,128]{1,0:T(8,128)(2,1)S(1)}, bf16[1056,128]{1,0:T(8,128)(2,1)S(1)}, u32[]{:S(2)}, u32[]{:S(2)}) collective-permute-start(bf16[1056,128]{1,0:T(8,128)(2,1)S(1)} %collective-permute-done.1), channel_id=1, source_target_pairs={{0,8},{1,201},{8,0},{9,65},{64,72},{65,9},{72,64},{73,129},{128,13... | collective-permute-start | bytes 811016 | tf_op jit(solution)/shard_map/ppermute | solution.py:46
  31.5 8.2 %collective-permute-start.10 = (bf16[2112,128]{1,0:T(8,128)(2,1)S(1)}, bf16[2112,128]{1,0:T(8,128)(2,1)S(1)}, u32[]{:S(2)}, u32[]{:S(2)}) collective-permute-start(bf16[2112,128]{1,0:T(8,128)(2,1)S(1)} %join.3), channel_id=1, source_target_pairs={{0,1},{1,0},{2,3},{3,2},{4,5},{5,4},{6,7},{7,6},{8,9},{9,8},{10,11... | collective-permute-start | bytes 1622024 | tf_op jit(solution)/shard_map/ppermute | solution.py:58
  35.8 3.9 %collective-permute-start.12 = (bf16[2112,128]{1,0:T(8,128)(2,1)S(1)}, bf16[2112,128]{1,0:T(8,128)(2,1)S(1)}, u32[]{:S(2)}, u32[]{:S(2)}) collective-permute-start(bf16[2112,128]{1,0:T(8,128)(2,1)S(1)} %collective-permute-done.8), channel_id=1, source_target_pairs={{0,1},{1,0},{2,3},{3,2},{4,5},{5,4},{6,7},{7,6},{8,9},{9,8},{10,11... | collective-permute-start | bytes 1622024 | tf_op jit(solution)/shard_map/ppermute | solution.py:58
  36.9 2.9 %collective-permute-start.13 = (bf16[2112,128]{1,0:T(8,128)(2,1)S(1)}, bf16[2112,128]{1,0:T(8,128)(2,1)S(1)}, u32[]{:S(2)}, u32[]{:S(2)}) collective-permute-start(bf16[2112,128]{1,0:T(8,128)(2,1)S(1)} %collective-permute-done.9), channel_id=1, source_target_pairs={{0,1},{1,0},{2,3},{3,2},{4,5},{5,4},{6,7},{7,6},{8,9},{9,8},{10,11... | collective-permute-start | bytes 1622024 | tf_op jit(solution)/shard_map/ppermute | solution.py:58
  37.0 3.0 %collective-permute-start.11 = (bf16[2112,128]{1,0:T(8,128)(2,1)S(1)}, bf16[2112,128]{1,0:T(8,128)(2,1)S(1)}, u32[]{:S(2)}, u32[]{:S(2)}) collective-permute-start(bf16[2112,128]{1,0:T(8,128)(2,1)S(1)} %collective-permute-done.7), channel_id=1, source_target_pairs={{0,1},{1,0},{2,3},{3,2},{4,5},{5,4},{6,7},{7,6},{8,9},{9,8},{10,11... | collective-permute-start | bytes 1622024 | tf_op jit(solution)/shard_map/ppermute | solution.py:58
  42.4 7.1 %collective-permute-start.15 = (bf16[256,512]{1,0:T(8,128)(2,1)S(1)}, bf16[256,512]{1,0:T(8,128)(2,1)S(1)}, u32[]{:S(2)}, u32[]{:S(2)}) collective-permute-start(bf16[256,512]{1,0:T(8,128)(2,1)S(1)} %pair.7), channel_id=1, source_target_pairs={{0,200},{1,9},{8,64},{9,1},{64,8},{65,73},{72,128},{73,65},{128,72... | collective-permute-start | bytes 786440 | tf_op jit(solution)/shard_map/ppermute | solution.py:46
  49.6 7.3 %collective-permute-start.16 = (bf16[256,512]{1,0:T(8,128)(2,1)S(1)}, bf16[256,512]{1,0:T(8,128)(2,1)S(1)}, u32[]{:S(2)}, u32[]{:S(2)}) collective-permute-start(bf16[256,512]{1,0:T(8,128)(2,1)S(1)} %add_convert_fusion.1), channel_id=1, source_target_pairs={{0,8},{1,201},{8,0},{9,65},{64,72},{65,9},{72,64},{73,129},{128,13... | collective-permute-start | bytes 786440 | tf_op jit(solution)/shard_map/ppermute | solution.py:46
  52.0 7.2 %collective-permute-start.14 = (bf16[128,512]{1,0:T(8,128)(2,1)S(1)}, bf16[128,512]{1,0:T(8,128)(2,1)S(1)}, u32[]{:S(2)}, u32[]{:S(2)}) collective-permute-start(bf16[128,512]{1,0:T(8,128)(2,1)S(1)} %slice.21), channel_id=1, source_target_pairs={{0,8},{1,201},{8,0},{9,65},{64,72},{65,9},{72,64},{73,129},{128,13... | collective-permute-start | bytes 393224 | tf_op jit(solution)/shard_map/ppermute | solution.py:46
  57.1 3.9 %collective-permute-start.17 = (bf16[128,512]{1,0:T(8,128)(2,1)S(1)}, bf16[128,512]{1,0:T(8,128)(2,1)S(1)}, u32[]{:S(2)}, u32[]{:S(2)}) collective-permute-start(bf16[128,512]{1,0:T(8,128)(2,1)S(1)} %get-tuple-element.20), channel_id=1, source_target_pairs={{0,200},{1,9},{8,64},{9,1},{64,8},{65,73},{72,128},{73,65},{128,72... | collective-permute-start | bytes 393224 | tf_op jit(solution)/shard_map/ppermute | solution.py:46
  57.4 7.1 %copy-start.1 = (f32[128,512]{1,0:T(8,128)S(1)}, f32[128,512]{1,0:T(8,128)}, u32[]{:S(2)}) copy-start(f32[128,512]{1,0:T(8,128)} %emb.3) | copy-start | bytes 786436
  57.4 7.1 %collective-permute-start.18 = (bf16[128,512]{1,0:T(8,128)(2,1)S(1)}, bf16[128,512]{1,0:T(8,128)(2,1)S(1)}, u32[]{:S(2)}, u32[]{:S(2)}) collective-permute-start(bf16[128,512]{1,0:T(8,128)(2,1)S(1)} %get-tuple-element.19), channel_id=1, source_target_pairs={{0,192},{1,65},{8,72},{9,201},{64,0},{65,129},{72,136},{73,9},{128... | collective-permute-start | bytes 393224 | tf_op jit(solution)/shard_map/ppermute | solution.py:54

commit v5 on v4

--- a/solution.py
+++ b/solution.py
@@ -58,7 +58,13 @@
     return lax.ppermute(block, AXES, [(i, i ^ 1) for i in range(256)])
 
 
-def pack_kernel(emb, margin, group, whole):
+def pack_kernel(emb_hbm, margin_hbm, group_hbm, whole, emb, margin, group, sem):
+    pairs = ((emb_hbm, emb), (margin_hbm, margin), (group_hbm, group))
+    copies = [pltpu.make_async_copy(src, dst, sem.at[i]) for i, (src, dst) in enumerate(pairs)]
+    for c in copies:
+        c.start()
+    for c in copies:
+        c.wait()
     e = emb[...]
     unit = (e / jnp.sqrt(jnp.sum(e * e, axis=1, keepdims=True) + 1e-06)).astype(BF)
     row = lax.broadcasted_iota(jnp.int32, (META, LANES), 0)
@@ -72,114 +78,68 @@
     return pl.pallas_call(
         pack_kernel,
         out_shape=jax.ShapeDtypeStruct((PACKED, LANES), BF),
-        in_specs=[VMEM] * 3,
+        in_specs=[pl.BlockSpec(memory_space=pltpu.HBM)] * 3,
         out_specs=VMEM,
+        scratch_shapes=[
+            pltpu.VMEM((CPD, D), F32),
+            pltpu.VMEM((1, CPD), jnp.int32),
+            pltpu.VMEM((1, CPD), jnp.int32),
+            pltpu.SemaphoreType.DMA((3,)),
+        ],
         compiler_params=pltpu.CompilerParams(vmem_limit_bytes=SMALL),
         name="pack",
     )(embeddings, margin.reshape(1, CPD), group.reshape(1, CPD))
 
 
-TILE = 1024
-TB = TILE // CPD
+TB = 8
+
+
+def units(ref, k):
+    return jnp.concatenate([ref[k, f * CPD : (f + 1) * CPD, :] for f in range(CHUNKS)], axis=1)
 
 
 def pair_kernel(n_r, n_c, n_sum, *refs):
     r_in, c_in, rest = refs[:n_r], refs[n_r : n_r + n_c], refs[n_r + n_c :]
-    sums, outs = rest[:n_sum], rest[n_sum : n_sum + n_r]
-    rbuf, rmeta, cbuf, cmeta, rm, rg, acc, r_sem, c_sem = rest[n_sum + n_r :]
-
-    def unpack(ref, buf, meta, at, sems):
-        n = ref.shape[0]
-        own = [
-            pltpu.make_async_copy(
-                ref.at[:, f * CPD : (f + 1) * CPD, :],
-                buf.at[at : at + n, :, f * LANES : (f + 1) * LANES],
-                sems(f),
-            )
-            for f in range(CHUNKS)
-        ]
-        own.append(pltpu.make_async_copy(ref.at[:, CHUNKS * CPD :, :], meta.at[at : at + n], sems(CHUNKS)))
-        return own
-
-    copies, waits, at = [], {}, 0
-    for i, ref in enumerate(r_in):
-        copies += unpack(ref, rbuf, rmeta, at, lambda f, i=i: r_sem.at[i, f])
-        at += ref.shape[0]
-    col = 0
-    for i, ref in enumerate(c_in):
-        own = unpack(ref, cbuf, cmeta, col, lambda f, i=i: c_sem.at[i, f])
-        waits.setdefault(col // TB, []).extend(own)
-        col += ref.shape[0]
-    for c in copies + sum(waits.values(), []):
-        c.start()
-    for c in copies:
-        c.wait()
-    for k in range(at):
-        m = rmeta[k].astype(F32)
-        rm[k * CPD : (k + 1) * CPD, :] = jnp.broadcast_to(m[0:1] * 0.0005, (CPD, CPD)).T
-        rg[k * CPD : (k + 1) * CPD, :] = jnp.broadcast_to(m[1:2], (CPD, CPD)).T
-    if sums:
-        o = 0
-        for ref in sums:
-            n = ref.shape[0]
-            acc[o : o + n, :] = ref[...]
-            o += n
-    else:
-        acc[...] = jnp.zeros_like(acc)
-    for t in range(col // TB):
-        for c in waits[t]:
-            c.wait()
-
-    def body(t, carry):
-        ct = cbuf[pl.ds(t * TB, TB)].reshape(TILE, D)
-        margins, groups = [], []
-        for k in range(TB):
-            m = cmeta[t * TB + k].astype(F32)
-            margins.append(m[0:1] * 0.0005)
-            groups.append(m[1:2])
-        for r0 in range(0, at * CPD, 256):
-            rt = rbuf[r0 // CPD : r0 // CPD + 2].reshape(256, D)
+    sums, outs = rest[:n_sum], rest[n_sum:]
+    r_blocks, c_blocks = ([(ref, k) for ref in v for k in range(ref.shape[0])] for v in (r_in, c_in))
+    acc, r_margin, r_group = [], [], []
+    for i in range(0, len(r_blocks), 2):
+        meta = [ref[k, CHUNKS * CPD :, :].astype(F32) for ref, k in r_blocks[i : i + 2]]
+        r_margin.append(jnp.concatenate([jnp.broadcast_to(m[0:1] * 0.0005, (CPD, CPD)).T for m in meta], axis=0))
+        r_group.append(jnp.concatenate([jnp.broadcast_to(m[1:2], (CPD, CPD)).T for m in meta], axis=0))
+        acc.append(None)
+    halves = [(ref, o) for ref in sums for o in range(0, ref.shape[0], 2 * CPD)]
+    for i, (ref, o) in enumerate(halves):
+        acc[i] = ref[o : o + 2 * CPD, :]
+    for t in range(0, len(c_blocks), TB):
+        tile = c_blocks[t : t + TB]
+        meta = [ref[k, CHUNKS * CPD :, :].astype(F32) for ref, k in tile]
+        ct = jnp.concatenate([units(ref, k) for ref, k in tile], axis=0)
+        for i in range(len(acc)):
+            rt = jnp.concatenate([units(ref, k) for ref, k in r_blocks[2 * i : 2 * i + 2]], axis=0)
             cos = lax.dot_general(rt, ct, (((1,), (1,)), ((), ())), preferred_element_type=F32)
             parts = []
-            for k in range(TB):
-                over = jnp.maximum(cos[:, k * LANES : (k + 1) * LANES] - rm[r0 : r0 + 256, :] - margins[k], 0.0)
-                parts.append(jnp.where(rg[r0 : r0 + 256, :] != groups[k], over, 0.0).astype(BF))
-            s = jnp.concatenate(parts, axis=1)
-            acc[r0 : r0 + 256, :] += jnp.dot(s, ct, preferred_element_type=F32)
-        return carry
-
-    lax.fori_loop(0, col // TB, body, 0)
-    o = 0
-    for out in outs:
-        n = out.shape[0]
-        out[...] = acc[o : o + n, :].astype(out.dtype)
-        o += n
-
-
-def pair(r_in, c_in, out_dtype, sums=(), weight=1.0):
+            for k, m in enumerate(meta):
+                over = jnp.maximum(cos[:, k * LANES : (k + 1) * LANES] - r_margin[i] - m[0:1] * 0.0005, 0.0)
+                parts.append(jnp.where(r_group[i] != m[1:2], over, 0.0).astype(BF))
+            part = jnp.dot(jnp.concatenate(parts, axis=1), ct, preferred_element_type=F32)
+            acc[i] = part if acc[i] is None else acc[i] + part
+    halves = [(ref, o) for ref in outs for o in range(0, ref.shape[0], 2 * CPD)]
+    for i, (ref, o) in enumerate(halves):
+        ref[o : o + 2 * CPD, :] = acc[i].astype(ref.dtype)
+
+
+def pair(r_in, c_in, out_dtype, sums=()):
     r_in, c_in = ([a.reshape(-1, PACKED, LANES) for a in v] for v in (r_in, c_in))
-    r_blocks, c_blocks = (sum(a.shape[0] for a in v) for v in (r_in, c_in))
-    rows, n_c = r_blocks * CPD, len(c_in)
-    return pl.pallas_call(
-        functools.partial(pair_kernel, len(r_in), n_c, len(sums)),
+    rows, cols = (sum(a.shape[0] for a in v) * CPD for v in (r_in, c_in))
+    return pl.pallas_call(
+        functools.partial(pair_kernel, len(r_in), len(c_in), len(sums)),
         out_shape=[jax.ShapeDtypeStruct((a.shape[0] * CPD, D), out_dtype) for a in r_in],
-        in_specs=[ANY] * (len(r_in) + n_c) + [VMEM] * len(sums),
+        in_specs=[VMEM] * (len(r_in) + len(c_in) + len(sums)),
         out_specs=[VMEM] * len(r_in),
-        scratch_shapes=[
-            pltpu.VMEM((r_blocks, CPD, D), BF),
-            pltpu.VMEM((r_blocks, META, LANES), BF),
-            pltpu.VMEM((c_blocks, CPD, D), BF),
-            pltpu.VMEM((c_blocks, META, LANES), BF),
-            pltpu.VMEM((rows, CPD), F32),
-            pltpu.VMEM((rows, CPD), F32),
-            pltpu.VMEM((rows, D), F32),
-            pltpu.SemaphoreType.DMA((len(r_in), CHUNKS + 1)),
-            pltpu.SemaphoreType.DMA((n_c, CHUNKS + 1)),
-        ],
         compiler_params=pltpu.CompilerParams(vmem_limit_bytes=20 << 20),
         cost_estimate=pl.CostEstimate(
-            flops=int(weight * 4 * rows * c_blocks * CPD * D),
-            bytes_accessed=int(weight * (c_blocks * CPD + rows) * D * 2), transcendentals=0
+            flops=4 * rows * cols * D, bytes_accessed=(cols + rows) * D * 2, transcendentals=0
         ),
         name="pair",
     )(*r_in, *c_in, *sums)
@@ -234,11 +194,12 @@
     far, ahead = shift(back, 1), swap(back, "za", "zb")
     c3, c1, c2 = (swap(c0, b, a) for a, b in (("xaya", "xbyb"), ("xa", "xb"), ("ya", "yb")))
     e0 = swap_cores(c0)
-    far, ahead, c1, c2, c3 = lax.optimization_barrier((far, ahead, c1, c2, c3))
+    (p_far,) = pair([far], [c0, c1], F32)
+    c1, c2, c3, ahead, p_far = lax.optimization_barrier((c1, c2, c3, ahead, p_far))
     e1, e2, e3 = swap_cores(c1), swap_cores(c2), swap_cores(c3)
     cols = [c0, c1, c2, c3, e0, e1, e2, e3]
-    (p_far,) = pair([far], cols[:4], F32)
-    (p_far,) = pair([far], cols[4:], BF, [p_far])
+    (p_far,) = pair([far], [c2, c3, e0, e1], F32, [p_far])
+    (p_far,) = pair([far], [e2, e3], BF, [p_far])
     q = swap(p_far, "zb", "za")
     p_ahead, p_own = pair([ahead, both], cols, F32)
     q_near = swap(p_own[CPD:].astype(BF), "za", "zb")

time: 66.5 us -> 62.7 us (0.943)
  the two profiles are of different devices: /device:TPU:1 before, /device:TPU:32 now
where the time goes in v5:
time: 62.7 us; the launch traced here: 62.6 us
  starting transfers between devices  30.2 us (48%)
  waiting for transfers between devices  18.5 us (30%)
  Pallas kernels  12 us (19%)
  local copies, waits for them, and re-layouts  1.68 us (3%)
    ppermute x13, starting transfers between devices, swap(): return lax.ppermute(block, AXES, pairs)  20.3 us
    pallas_call x5, Pallas kernels, pair(): pl.pallas_call(functools.partial(pair_kernel, len(r_in), len(c_in), len(s...  9.79 us
    ppermute x2, starting transfers between devices, shift(): return lax.ppermute(block, AXES, pairs)  9.32 us
    ppermute x2, waiting for transfers between devices, shift(): return lax.ppermute(block, AXES, pairs)  9.27 us
    ppermute x13, waiting for transfers between devices, swap(): return lax.ppermute(block, AXES, pairs)  7.64 us
    unnamed x8, local copies, waits for them, and re-layouts  1.62 us
    ppermute x4, waiting for transfers between devices, swap_cores(): return lax.ppermute(block, AXES, [(i, i ^ 1) for i in range(256)])  1.57 us
  transfers between devices with their start and end apart: 19, of which 9 were waited for; matrix products, arithmetic and copies ran while one was open for 0% of the time, Pallas kernels for 16%

profile of v5, /device:TPU:32, one launch (start us, length us, event | category | flops | bytes accessed | tf_op | source)
XLA Modules:
  0.0 62.6 jit_solution(17923107205563594888)
XLA Ops:
  0.0 0.0 copy-start.2
  0.0 0.0 copy-start.3
  0.0 0.7 %copy-done.2 = s32[128]{0:T(128)S(1)} copy-done((s32[128]{0:T(128)S(1)}, s32[128]{0:T(128)}, u32[]{:S(2)}) %copy-start.2) | copy-done | bytes 536
  0.7 0.0 copy-done.3
  0.7 0.0 copy-start
  0.7 0.9 %copy-done = f32[128,512]{1,0:T(8,128)S(1)} copy-done((f32[128,512]{1,0:T(8,128)S(1)}, f32[128,512]{1,0:T(8,128)}, u32[]{:S(2)}) %copy-start) | copy-done | bytes 262168
  1.6 0.2 pack.1.refs_0_
  1.8 1.9 %collective-permute-start.6 = (bf16[528,128]{1,0:T(8,128)(2,1)S(1)}, bf16[528,128]{1,0:T(8,128)(2,1)S(1)}, u32[]{:S(2)}, u32[]{:S(2)}) collective-permute-start(bf16[528,128]{1,0:T(8,128)(2,1)S(1)} %pack.1.refs_0_), channel_id=1, source_target_pairs={{0,8},{1,201},{8,0},{9,65},{64,72},{65,9},{72,64},{73,129},{128,13... | collective-permute-start | bytes 405512 | tf_op jit(solution)/shard_map/ppermute | solution.py:46
  3.7 0.0 collective-permute-start
  3.7 1.3 %collective-permute-start.1 = (bf16[528,128]{1,0:T(8,128)(2,1)S(1)}, bf16[528,128]{1,0:T(8,128)(2,1)S(1)}, u32[]{:S(2)}, u32[]{:S(2)}) collective-permute-start(bf16[528,128]{1,0:T(8,128)(2,1)S(1)} %pack.1.refs_0_), channel_id=1, source_target_pairs={{0,2},{1,7},{8,10},{9,15},{64,66},{65,71},{72,74},{73,79},{128,130... | collective-permute-start | bytes 405512 | tf_op jit(solution)/shard_map/ppermute | solution.py:46
  5.1 2.2 %collective-permute-start.2 = (bf16[528,128]{1,0:T(8,128)(2,1)S(1)}, bf16[528,128]{1,0:T(8,128)(2,1)S(1)}, u32[]{:S(2)}, u32[]{:S(2)}) collective-permute-start(bf16[528,128]{1,0:T(8,128)(2,1)S(1)} %pack.1.refs_0_), channel_id=1, source_target_pairs={{0,18},{1,55},{8,26},{9,63},{64,82},{65,119},{72,90},{73,127},{128... | collective-permute-start | bytes 405512 | tf_op jit(solution)/shard_map/ppermute | solution.py:46
  7.2 0.0 collective-permute-done.6.refs_1_
  7.2 0.3 join.3
  7.6 2.1 %collective-permute-start.7 = (bf16[1056,128]{1,0:T(8,128)(2,1)S(1)}, bf16[1056,128]{1,0:T(8,128)(2,1)S(1)}, u32[]{:S(2)}, u32[]{:S(2)}) collective-permute-start(bf16[1056,128]{1,0:T(8,128)(2,1)S(1)} %join.3), channel_id=1, source_target_pairs={{0,200},{1,9},{8,64},{9,1},{64,8},{65,73},{72,128},{73,65},{128,72... | collective-permute-start | bytes 811016 | tf_op jit(solution)/shard_map/ppermute | solution.py:46
  9.7 0.0 collective-permute-done.refs_1_
  9.7 0.0 collective-permute-done.1.refs_2_
  9.7 1.3 %collective-permute-done.2.refs_3_ = bf16[528,128]{1,0:T(8,128)(2,1)S(1)} collective-permute-done((bf16[528,128]{1,0:T(8,128)(2,1)S(1)}, bf16[528,128]{1,0:T(8,128)(2,1)S(1)}, u32[]{:S(2)}, u32[]{:S(2)}) %collective-permute-start.2) | collective-permute-done | bytes 135200 | tf_op jit(solution)/shard_map/ppermute | solution.py:46
  11.0 0.7 %join.2 = bf16[2112,128]{1,0:T(8,128)(2,1)S(1)} custom-call(bf16[528,128]{1,0:T(8,128)(2,1)S(1)} %pack.1.refs_0_, bf16[528,128]{1,0:T(8,128)(2,1)S(1)} %collective-permute-done.refs_1_, bf16[528,128]{1,0:T(8,128)(2,1)S(1)} %collective-permute-done.1.refs_2_, bf16[528,128]{1,0:T(8,128)(2,1)S(1)} %collective-permute-done.2.refs_3_), custom_call_target="tpu_custom_call" | custom-call | tf_op jit(solution)/shard_map/join/pallas_call | solution.py:164
  11.7 2.2 %collective-permute-start.3 = (bf16[2112,128]{1,0:T(8,128)(2,1)S(1)}, bf16[2112,128]{1,0:T(8,128)(2,1)S(1)}, u32[]{:S(2)}, u32[]{:S(2)}) collective-permute-start(bf16[2112,128]{1,0:T(8,128)(2,1)S(1)} %join.2), channel_id=1, source_target_pairs={{0,48},{1,17},{8,56},{9,25},{64,112},{65,81},{72,120},{73,89},{128... | collective-permute-start | bytes 1622024 | tf_op jit(solution)/shard_map/ppermute | solution.py:46
  13.9 2.4 %collective-permute-start.4 = (bf16[2112,128]{1,0:T(8,128)(2,1)S(1)}, bf16[2112,128]{1,0:T(8,128)(2,1)S(1)}, u32[]{:S(2)}, u32[]{:S(2)}) collective-permute-start(bf16[2112,128]{1,0:T(8,128)(2,1)S(1)} %join.2), channel_id=1, source_target_pairs={{0,6},{1,3},{8,14},{9,11},{64,70},{65,67},{72,78},{73,75},{128,134... | collective-permute-start | bytes 1622024 | tf_op jit(solution)/shard_map/ppermute | solution.py:46
  16.3 1.4 %collective-permute-start.5 = (bf16[2112,128]{1,0:T(8,128)(2,1)S(1)}, bf16[2112,128]{1,0:T(8,128)(2,1)S(1)}, u32[]{:S(2)}, u32[]{:S(2)}) collective-permute-start(bf16[2112,128]{1,0:T(8,128)(2,1)S(1)} %join.2), channel_id=1, source_target_pairs={{0,54},{1,19},{8,62},{9,27},{64,118},{65,83},{72,126},{73,91},{128... | collective-permute-start | bytes 1622024 | tf_op jit(solution)/shard_map/ppermute | solution.py:46
  17.7 0.0 collective-permute-done.7
  17.7 6.3 %collective-permute-start.9 = (bf16[1056,128]{1,0:T(8,128)(2,1)S(1)}, bf16[1056,128]{1,0:T(8,128)(2,1)S(1)}, u32[]{:S(2)}, u32[]{:S(2)}) collective-permute-start(bf16[1056,128]{1,0:T(8,128)(2,1)S(1)} %collective-permute-done.7), channel_id=1, source_target_pairs={{0,64},{1,193},{8,200},{9,73},{64,128},{65,1},{72,8},{73,137},{128... | collective-permute-start | bytes 811016 | tf_op jit(solution)/shard_map/ppermute | solution.py:54
  24.0 0.0 collective-permute-start.8
  24.0 6.1 %collective-permute-done.9 = bf16[1056,128]{1,0:T(8,128)(2,1)S(1)} collective-permute-done((bf16[1056,128]{1,0:T(8,128)(2,1)S(1)}, bf16[1056,128]{1,0:T(8,128)(2,1)S(1)}, u32[]{:S(2)}, u32[]{:S(2)}) %collective-permute-start.9) | collective-permute-done | bytes 270368 | tf_op jit(solution)/shard_map/ppermute | solution.py:54
  30.1 0.0 collective-permute-start.10
  30.1 0.0 collective-permute-done.3
  30.1 0.8 %pair.5.refs_5_ = f32[256,512]{1,0:T(8,128)S(1)} custom-call(bf16[2,528,128]{2,1,0:T(8,128)(2,1)S(1)} %bitcast.25, bf16[4,528,128]{2,1,0:T(8,128)(2,1)S(1)} %bitcast.15, bf16[4,528,128]{2,1,0:T(8,128)(2,1)S(1)} %bitcast.30), custom_call_target="tpu_custom_call" | custom-call | flops 536870912 | bytes 1310720 | tf_op jit(solution)/shard_map/pair/pallas_call | solution.py:135
  30.8 2.1 %collective-permute-done.8 = bf16[1056,128]{1,0:T(8,128)(2,1)S(1)} collective-permute-done((bf16[1056,128]{1,0:T(8,128)(2,1)S(1)}, bf16[1056,128]{1,0:T(8,128)(2,1)S(1)}, u32[]{:S(2)}, u32[]{:S(2)}) %collective-permute-start.8) | collective-permute-done | bytes 270368 | tf_op jit(solution)/shard_map/ppermute | solution.py:46
  33.0 0.0 collective-permute-done.4
  33.0 0.0 collective-permute-done.5
  33.0 0.0 collective-permute-start.11
  33.0 0.5 collective-permute-start.12
  33.5 0.1 collective-permute-start.13
  33.6 0.0 collective-permute-done.10
  33.6 1.3 %collective-permute-done.11 = bf16[2112,128]{1,0:T(8,128)(2,1)S(1)} collective-permute-done((bf16[2112,128]{1,0:T(8,128)(2,1)S(1)}, bf16[2112,128]{1,0:T(8,128)(2,1)S(1)}, u32[]{:S(2)}, u32[]{:S(2)}) %collective-permute-start.11) | collective-permute-done | bytes 540704 | tf_op jit(solution)/shard_map/ppermute | solution.py:58
  34.9 1.3 %pair.8.refs_3_ = f32[256,512]{1,0:T(8,128)S(1)} custom-call(bf16[2,528,128]{2,1,0:T(8,128)(2,1)S(1)} %bitcast.26, bf16[4,528,128]{2,1,0:T(8,128)(2,1)S(1)} %bitcast.33, bf16[4,528,128]{2,1,0:T(8,128)(2,1)S(1)} %bitcast.36, bf16[4,528,128]{2,1,0:T(8,128)(2,1)S(1)} %bitcast.39, bf16[4,528,128]{2,1,0:T(8,128)(2,1)S(1)} %bitcast.42, f32[256,512]{1,0:T(8,128)S(1)} %pair.5.refs_5_), custom_call_target="tpu_custom_call" | custom-call | flops 1073741824 | bytes 2359296 | tf_op jit(solution)/shard_map/pair/pallas_call | solution.py:135
  36.2 0.0 collective-permute-done.12
  36.2 0.2 collective-permute-done.13
  36.5 0.7 %pair.9 = bf16[256,512]{1,0:T(8,128)(2,1)S(1)} custom-call(bf16[2,528,128]{2,1,0:T(8,128)(2,1)S(1)} %bitcast.27, bf16[4,528,128]{2,1,0:T(8,128)(2,1)S(1)} %bitcast.18, bf16[4,528,128]{2,1,0:T(8,128)(2,1)S(1)} %bitcast.21, f32[256,512]{1,0:T(8,128)S(1)} %pair.8.refs_3_), custom_call_target="tpu_custom_call" | custom-call | flops 536870912 | bytes 1310720 | tf_op jit(solution)/shard_map/pair/pallas_call | solution.py:135
  37.2 1.7 %collective-permute-start.15 = (bf16[256,512]{1,0:T(8,128)(2,1)S(1)}, bf16[256,512]{1,0:T(8,128)(2,1)S(1)}, u32[]{:S(2)}, u32[]{:S(2)}) collective-permute-start(bf16[256,512]{1,0:T(8,128)(2,1)S(1)} %pair.9), channel_id=1, source_target_pairs={{0,200},{1,9},{8,64},{9,1},{64,8},{65,73},{72,128},{73,65},{128,72... | collective-permute-start | bytes 786440 | tf_op jit(solution)/shard_map/ppermute | solution.py:46
  38.9 4.6 %pair.6 = (f32[256,512]{1,0:T(8,128)S(1)}, f32[256,512]{1,0:T(8,128)S(1)}) custom-call(bf16[2,528,128]{2,1,0:T(8,128)(2,1)S(1)} %bitcast.46, bf16[2,528,128]{2,1,0:T(8,128)(2,1)S(1)} %bitcast.24, bf16[4,528,128]{2,1,0:T(8,128)(2,1)S(1)} %bitcast.16, bf16[4,528,128]{2,1,0:T(8,128)(2,1)S(1)} %bitcast.31, bf16[4,528,128]{2,1,0:T(8,128)(2,1)S(1)} %bitcast.34, ...), custom_call_target="tpu_custom_call" | custom-call | flops 4294967296 | bytes 4718592 | tf_op jit(solution)/shard_map/pair/pallas_call | solution.py:135
  43.5 0.3 collective-permute-done.15
  43.9 0.1 add_convert_fusion.1
  43.9 3.8 %collective-permute-start.16 = (bf16[256,512]{1,0:T(8,128)(2,1)S(1)}, bf16[256,512]{1,0:T(8,128)(2,1)S(1)}, u32[]{:S(2)}, u32[]{:S(2)}) collective-permute-start(bf16[256,512]{1,0:T(8,128)(2,1)S(1)} %add_convert_fusion.1), channel_id=1, source_target_pairs={{0,8},{1,201},{8,0},{9,65},{64,72},{65,9},{72,64},{73,129},{128,13... | collective-permute-start | bytes 786440 | tf_op jit(solution)/shard_map/ppermute | solution.py:46
  47.7 0.1 collective-permute-start.14
  47.8 2.4 %pair.7 = f32[256,512]{1,0:T(8,128)S(1)} custom-call(bf16[2,528,128]{2,1,0:T(8,128)(2,1)S(1)} %bitcast.45, bf16[4,528,128]{2,1,0:T(8,128)(2,1)S(1)} %bitcast.17, bf16[4,528,128]{2,1,0:T(8,128)(2,1)S(1)} %bitcast.32, bf16[4,528,128]{2,1,0:T(8,128)(2,1)S(1)} %bitcast.35, bf16[4,528,128]{2,1,0:T(8,128)(2,1)S(1)} %bitcast.38, bf16[4,528,128]{2,1,0:T(8,128)(2,1)S(1)} %bitcast.41, ...), custom_call_target="tpu_custom_call" | custom-call | flops 2147483648 | bytes 4456448 | tf_op jit(solution)/shard_map/pair/pallas_call | solution.py:135
  50.2 1.8 %collective-permute-done.16 = bf16[256,512]{1,0:T(8,128)(2,1)S(1)} collective-permute-done((bf16[256,512]{1,0:T(8,128)(2,1)S(1)}, bf16[256,512]{1,0:T(8,128)(2,1)S(1)}, u32[]{:S(2)}, u32[]{:S(2)}) %collective-permute-start.16) | collective-permute-done | bytes 262176 | tf_op jit(solution)/shard_map/ppermute | solution.py:46
  52.1 0.1 add_convert_fusion
  52.2 1.2 %collective-permute-start.17 = (bf16[128,512]{1,0:T(8,128)(2,1)S(1)}, bf16[128,512]{1,0:T(8,128)(2,1)S(1)}, u32[]{:S(2)}, u32[]{:S(2)}) collective-permute-start(bf16[128,512]{1,0:T(8,128)(2,1)S(1)} %get-tuple-element.20), channel_id=1, source_target_pairs={{0,200},{1,9},{8,64},{9,1},{64,8},{65,73},{72,128},{73,65},{128,72... | collective-permute-start | bytes 393224 | tf_op jit(solution)/shard_map/ppermute | solution.py:46
  53.4 0.0 copy-start.1
  53.4 3.0 %collective-permute-start.18 = (bf16[128,512]{1,0:T(8,128)(2,1)S(1)}, bf16[128,512]{1,0:T(8,128)(2,1)S(1)}, u32[]{:S(2)}, u32[]{:S(2)}) collective-permute-start(bf16[128,512]{1,0:T(8,128)(2,1)S(1)} %get-tuple-element.19), channel_id=1, source_target_pairs={{0,192},{1,65},{8,72},{9,201},{64,0},{65,129},{72,136},{73,9},{128... | collective-permute-start | bytes 393224 | tf_op jit(solution)/shard_map/ppermute | solution.py:54
  56.4 0.0 collective-permute-done.14.refs_0_
  56.4 2.0 %collective-permute-done.17.refs_1_ = bf16[128,512]{1,0:T(8,128)(2,1)S(1)} collective-permute-done((bf16[128,512]{1,0:T(8,128)(2,1)S(1)}, bf16[128,512]{1,0:T(8,128)(2,1)S(1)}, u32[]{:S(2)}, u32[]{:S(2)}) %collective-permute-start.17) | collective-permute-done | bytes 131104 | tf_op jit(solution)/shard_map/ppermute | solution.py:46
  58.4 3.2 %collective-permute-done.18.refs_2_ = bf16[128,512]{1,0:T(8,128)(2,1)S(1)} collective-permute-done((bf16[128,512]{1,0:T(8,128)(2,1)S(1)}, bf16[128,512]{1,0:T(8,128)(2,1)S(1)}, u32[]{:S(2)}, u32[]{:S(2)}) %collective-permute-start.18) | collective-permute-done | bytes 131104 | tf_op jit(solution)/shard_map/ppermute | solution.py:54
  61.6 0.0 copy-done.1
  61.6 0.9 %final.1 = f32[128,512]{1,0:T(8,128)} custom-call(f32[128,512]{1,0:T(8,128)S(1)} %copy-done.1, f32[128,512]{1,0:T(8,128)S(1)} %slice.13.own, bf16[128,512]{1,0:T(8,128)(2,1)S(1)} %collective-permute-done.14.refs_0_, bf16[128,512]{1,0:T(8,128)(2,1)S(1)} %collective-permute-done.17.refs_1_, bf16[128,512]{1,0:T(8,128)(2,1)S(1)} %collective-permute-done.18.refs_2_), custom_call_target="tpu_custom_call" | custom-call | tf_op jit(solution)/shard_map/final/pallas_call | solution.py:212
  (3 shorter events, 0.1 us)
Async XLA Ops:
  0.0 0.7 %copy-start.2 = (s32[128]{0:T(128)S(1)}, s32[128]{0:T(128)}, u32[]{:S(2)}) copy-start(s32[128]{0:T(128)} %param.4) | copy-start | bytes 1540
  0.0 0.7 %copy-start.3 = (s32[128]{0:T(128)S(1)}, s32[128]{0:T(128)}, u32[]{:S(2)}) copy-start(s32[128]{0:T(128)} %param.5) | copy-start | bytes 1540
  0.7 0.9 %copy-start = (f32[128,512]{1,0:T(8,128)S(1)}, f32[128,512]{1,0:T(8,128)}, u32[]{:S(2)}) copy-start(f32[128,512]{1,0:T(8,128)} %emb.1) | copy-start | bytes 786436
  1.8 5.4 %collective-permute-start.6 = (bf16[528,128]{1,0:T(8,128)(2,1)S(1)}, bf16[528,128]{1,0:T(8,128)(2,1)S(1)}, u32[]{:S(2)}, u32[]{:S(2)}) collective-permute-start(bf16[528,128]{1,0:T(8,128)(2,1)S(1)} %pack.1.refs_0_), channel_id=1, source_target_pairs={{0,8},{1,201},{8,0},{9,65},{64,72},{65,9},{72,64},{73,129},{128,13... | collective-permute-start | bytes 405512 | tf_op jit(solution)/shard_map/ppermute | solution.py:46
  3.7 5.9 %collective-permute-start = (bf16[528,128]{1,0:T(8,128)(2,1)S(1)}, bf16[528,128]{1,0:T(8,128)(2,1)S(1)}, u32[]{:S(2)}, u32[]{:S(2)}) collective-permute-start(bf16[528,128]{1,0:T(8,128)(2,1)S(1)} %pack.1.refs_0_), channel_id=1, source_target_pairs={{0,16},{1,49},{8,24},{9,57},{64,80},{65,113},{72,88},{73,121},{128... | collective-permute-start | bytes 405512 | tf_op jit(solution)/shard_map/ppermute | solution.py:46
  3.7 5.9 %collective-permute-start.1 = (bf16[528,128]{1,0:T(8,128)(2,1)S(1)}, bf16[528,128]{1,0:T(8,128)(2,1)S(1)}, u32[]{:S(2)}, u32[]{:S(2)}) collective-permute-start(bf16[528,128]{1,0:T(8,128)(2,1)S(1)} %pack.1.refs_0_), channel_id=1, source_target_pairs={{0,2},{1,7},{8,10},{9,15},{64,66},{65,71},{72,74},{73,79},{128,130... | collective-permute-start | bytes 405512 | tf_op jit(solution)/shard_map/ppermute | solution.py:46
  5.1 5.9 %collective-permute-start.2 = (bf16[528,128]{1,0:T(8,128)(2,1)S(1)}, bf16[528,128]{1,0:T(8,128)(2,1)S(1)}, u32[]{:S(2)}, u32[]{:S(2)}) collective-permute-start(bf16[528,128]{1,0:T(8,128)(2,1)S(1)} %pack.1.refs_0_), channel_id=1, source_target_pairs={{0,18},{1,55},{8,26},{9,63},{64,82},{65,119},{72,90},{73,127},{128... | collective-permute-start | bytes 405512 | tf_op jit(solution)/shard_map/ppermute | solution.py:46
  7.6 10.1 %collective-permute-start.7 = (bf16[1056,128]{1,0:T(8,128)(2,1)S(1)}, bf16[1056,128]{1,0:T(8,128)(2,1)S(1)}, u32[]{:S(2)}, u32[]{:S(2)}) collective-permute-start(bf16[1056,128]{1,0:T(8,128)(2,1)S(1)} %join.3), channel_id=1, source_target_pairs={{0,200},{1,9},{8,64},{9,1},{64,8},{65,73},{72,128},{73,65},{128,72... | collective-permute-start | bytes 811016 | tf_op jit(solution)/shard_map/ppermute | solution.py:46
  11.7 18.4 %collective-permute-start.3 = (bf16[2112,128]{1,0:T(8,128)(2,1)S(1)}, bf16[2112,128]{1,0:T(8,128)(2,1)S(1)}, u32[]{:S(2)}, u32[]{:S(2)}) collective-permute-start(bf16[2112,128]{1,0:T(8,128)(2,1)S(1)} %join.2), channel_id=1, source_target_pairs={{0,48},{1,17},{8,56},{9,25},{64,112},{65,81},{72,120},{73,89},{128... | collective-permute-start | bytes 1622024 | tf_op jit(solution)/shard_map/ppermute | solution.py:46
  13.9 19.1 %collective-permute-start.4 = (bf16[2112,128]{1,0:T(8,128)(2,1)S(1)}, bf16[2112,128]{1,0:T(8,128)(2,1)S(1)}, u32[]{:S(2)}, u32[]{:S(2)}) collective-permute-start(bf16[2112,128]{1,0:T(8,128)(2,1)S(1)} %join.2), channel_id=1, source_target_pairs={{0,6},{1,3},{8,14},{9,11},{64,70},{65,67},{72,78},{73,75},{128,134... | collective-permute-start | bytes 1622024 | tf_op jit(solution)/shard_map/ppermute | solution.py:46
  16.3 16.7 %collective-permute-start.5 = (bf16[2112,128]{1,0:T(8,128)(2,1)S(1)}, bf16[2112,128]{1,0:T(8,128)(2,1)S(1)}, u32[]{:S(2)}, u32[]{:S(2)}) collective-permute-start(bf16[2112,128]{1,0:T(8,128)(2,1)S(1)} %join.2), channel_id=1, source_target_pairs={{0,54},{1,19},{8,62},{9,27},{64,118},{65,83},{72,126},{73,91},{128... | collective-permute-start | bytes 1622024 | tf_op jit(solution)/shard_map/ppermute | solution.py:46
  17.7 12.4 %collective-permute-start.9 = (bf16[1056,128]{1,0:T(8,128)(2,1)S(1)}, bf16[1056,128]{1,0:T(8,128)(2,1)S(1)}, u32[]{:S(2)}, u32[]{:S(2)}) collective-permute-start(bf16[1056,128]{1,0:T(8,128)(2,1)S(1)} %collective-permute-done.7), channel_id=1, source_target_pairs={{0,64},{1,193},{8,200},{9,73},{64,128},{65,1},{72,8},{73,137},{128... | collective-permute-start | bytes 811016 | tf_op jit(solution)/shard_map/ppermute | solution.py:54
  24.0 9.0 %collective-permute-start.8 = (bf16[1056,128]{1,0:T(8,128)(2,1)S(1)}, bf16[1056,128]{1,0:T(8,128)(2,1)S(1)}, u32[]{:S(2)}, u32[]{:S(2)}) collective-permute-start(bf16[1056,128]{1,0:T(8,128)(2,1)S(1)} %collective-permute-done.7), channel_id=1, source_target_pairs={{0,8},{1,201},{8,0},{9,65},{64,72},{65,9},{72,64},{73,129},{128,13... | collective-permute-start | bytes 811016 | tf_op jit(solution)/shard_map/ppermute | solution.py:46
  30.1 3.5 %collective-permute-start.10 = (bf16[2112,128]{1,0:T(8,128)(2,1)S(1)}, bf16[2112,128]{1,0:T(8,128)(2,1)S(1)}, u32[]{:S(2)}, u32[]{:S(2)}) collective-permute-start(bf16[2112,128]{1,0:T(8,128)(2,1)S(1)} %join.2), channel_id=1, source_target_pairs={{0,1},{1,0},{2,3},{3,2},{4,5},{5,4},{6,7},{7,6},{8,9},{9,8},{10,11... | collective-permute-start | bytes 1622024 | tf_op jit(solution)/shard_map/ppermute | solution.py:58
  33.0 1.9 %collective-permute-start.11 = (bf16[2112,128]{1,0:T(8,128)(2,1)S(1)}, bf16[2112,128]{1,0:T(8,128)(2,1)S(1)}, u32[]{:S(2)}, u32[]{:S(2)}) collective-permute-start(bf16[2112,128]{1,0:T(8,128)(2,1)S(1)} %collective-permute-done.3), channel_id=1, source_target_pairs={{0,1},{1,0},{2,3},{3,2},{4,5},{5,4},{6,7},{7,6},{8,9},{9,8},{10,11... | collective-permute-start | bytes 1622024 | tf_op jit(solution)/shard_map/ppermute | solution.py:58
  33.0 3.2 %collective-permute-start.12 = (bf16[2112,128]{1,0:T(8,128)(2,1)S(1)}, bf16[2112,128]{1,0:T(8,128)(2,1)S(1)}, u32[]{:S(2)}, u32[]{:S(2)}) collective-permute-start(bf16[2112,128]{1,0:T(8,128)(2,1)S(1)} %collective-permute-done.4), channel_id=1, source_target_pairs={{0,1},{1,0},{2,3},{3,2},{4,5},{5,4},{6,7},{7,6},{8,9},{9,8},{10,11... | collective-permute-start | bytes 1622024 | tf_op jit(solution)/shard_map/ppermute | solution.py:58
  33.5 3.0 %collective-permute-start.13 = (bf16[2112,128]{1,0:T(8,128)(2,1)S(1)}, bf16[2112,128]{1,0:T(8,128)(2,1)S(1)}, u32[]{:S(2)}, u32[]{:S(2)}) collective-permute-start(bf16[2112,128]{1,0:T(8,128)(2,1)S(1)} %collective-permute-done.5), channel_id=1, source_target_pairs={{0,1},{1,0},{2,3},{3,2},{4,5},{5,4},{6,7},{7,6},{8,9},{9,8},{10,11... | collective-permute-start | bytes 1622024 | tf_op jit(solution)/shard_map/ppermute | solution.py:58
  37.2 6.6 %collective-permute-start.15 = (bf16[256,512]{1,0:T(8,128)(2,1)S(1)}, bf16[256,512]{1,0:T(8,128)(2,1)S(1)}, u32[]{:S(2)}, u32[]{:S(2)}) collective-permute-start(bf16[256,512]{1,0:T(8,128)(2,1)S(1)} %pair.9), channel_id=1, source_target_pairs={{0,200},{1,9},{8,64},{9,1},{64,8},{65,73},{72,128},{73,65},{128,72... | collective-permute-start | bytes 786440 | tf_op jit(solution)/shard_map/ppermute | solution.py:46
  43.9 8.1 %collective-permute-start.16 = (bf16[256,512]{1,0:T(8,128)(2,1)S(1)}, bf16[256,512]{1,0:T(8,128)(2,1)S(1)}, u32[]{:S(2)}, u32[]{:S(2)}) collective-permute-start(bf16[256,512]{1,0:T(8,128)(2,1)S(1)} %add_convert_fusion.1), channel_id=1, source_target_pairs={{0,8},{1,201},{8,0},{9,65},{64,72},{65,9},{72,64},{73,129},{128,13... | collective-permute-start | bytes 786440 | tf_op jit(solution)/shard_map/ppermute | solution.py:46
  47.7 8.7 %collective-permute-start.14 = (bf16[128,512]{1,0:T(8,128)(2,1)S(1)}, bf16[128,512]{1,0:T(8,128)(2,1)S(1)}, u32[]{:S(2)}, u32[]{:S(2)}) collective-permute-start(bf16[128,512]{1,0:T(8,128)(2,1)S(1)} %slice.21), channel_id=1, source_target_pairs={{0,8},{1,201},{8,0},{9,65},{64,72},{65,9},{72,64},{73,129},{128,13... | collective-permute-start | bytes 393224 | tf_op jit(solution)/shard_map/ppermute | solution.py:46
  52.2 6.3 %collective-permute-start.17 = (bf16[128,512]{1,0:T(8,128)(2,1)S(1)}, bf16[128,512]{1,0:T(8,128)(2,1)S(1)}, u32[]{:S(2)}, u32[]{:S(2)}) collective-permute-start(bf16[128,512]{1,0:T(8,128)(2,1)S(1)} %get-tuple-element.20), channel_id=1, source_target_pairs={{0,200},{1,9},{8,64},{9,1},{64,8},{65,73},{72,128},{73,65},{128,72... | collective-permute-start | bytes 393224 | tf_op jit(solution)/shard_map/ppermute | solution.py:46
  53.4 8.3 %copy-start.1 = (f32[128,512]{1,0:T(8,128)S(1)}, f32[128,512]{1,0:T(8,128)}, u32[]{:S(2)}) copy-start(f32[128,512]{1,0:T(8,128)} %emb.1) | copy-start | bytes 786436
  53.4 8.3 %collective-permute-start.18 = (bf16[128,512]{1,0:T(8,128)(2,1)S(1)}, bf16[128,512]{1,0:T(8,128)(2,1)S(1)}, u32[]{:S(2)}, u32[]{:S(2)}) collective-permute-start(bf16[128,512]{1,0:T(8,128)(2,1)S(1)} %get-tuple-element.19), channel_id=1, source_target_pairs={{0,192},{1,65},{8,72},{9,201},{64,0},{65,129},{72,136},{73,9},{128... | collective-permute-start | bytes 393224 | tf_op jit(solution)/shard_map/ppermute | solution.py:54

commit v6 on v5

--- a/solution.py
+++ b/solution.py
@@ -187,15 +187,15 @@
     whole = pack(embeddings, margin, group)
 
     near = swap(whole, "za", "zb")
-    square = [swap(whole, a, b) for a, b in (("xa", "xb"), ("ya", "yb"), ("xaya", "xbyb"))]
+    square = [swap(whole, a, b) for a, b in (("xaya", "xbyb"), ("xa", "xb"), ("ya", "yb"))]
     (both,) = join(((0, 1),), whole, near)
     back = swap(both, "zb", "za")
-    (c0,) = join(((0, 1, 2, 3),), whole, *square)
+    (c0,) = join(((3, 0, 1, 2),), *square, whole)
     far, ahead = shift(back, 1), swap(back, "za", "zb")
     c3, c1, c2 = (swap(c0, b, a) for a, b in (("xaya", "xbyb"), ("xa", "xb"), ("ya", "yb")))
     e0 = swap_cores(c0)
     (p_far,) = pair([far], [c0, c1], F32)
-    c1, c2, c3, ahead, p_far = lax.optimization_barrier((c1, c2, c3, ahead, p_far))
+    c2, c3, ahead, p_far = lax.optimization_barrier((c2, c3, ahead, p_far))
     e1, e2, e3 = swap_cores(c1), swap_cores(c2), swap_cores(c3)
     cols = [c0, c1, c2, c3, e0, e1, e2, e3]
     (p_far,) = pair([far], [c2, c3, e0, e1], F32, [p_far])
@@ -206,7 +206,7 @@
     q = swap((p_ahead + q).astype(BF), "za", "zb")
     (p_back,) = pair([back], cols, F32)
     p_back = (p_back + q).astype(BF)
-    arrived = (q_near, swap(p_back[:CPD], "zb", "za"), shift(p_back[CPD:], -1))
+    arrived = (q_near, shift(p_back[CPD:], -1), swap(p_back[:CPD], "zb", "za"))
 
     rate = D * math.sqrt(D) / (3.0 * math.sqrt(classes))
     return pl.pallas_call(

time: 62.7 us -> 61.3 us (0.978)
  the two profiles are of different devices: /device:TPU:32 before, /device:TPU:1 now
where the time goes in v6:
time: 61.3 us; the launch traced here: 61.2 us
  starting transfers between devices  24.6 us (40%)
  waiting for transfers between devices  22.7 us (37%)
  Pallas kernels  11.9 us (19%)
  local copies, waits for them, and re-layouts  1.68 us (3%)
    ppermute x13, starting transfers between devices, swap(): return lax.ppermute(block, AXES, pairs)  21.8 us
    ppermute x2, waiting for transfers between devices, shift(): return lax.ppermute(block, AXES, pairs)  11 us
    ppermute x13, waiting for transfers between devices, swap(): return lax.ppermute(block, AXES, pairs)  10.7 us
    pallas_call x5, Pallas kernels, pair(): pl.pallas_call(functools.partial(pair_kernel, len(r_in), len(c_in), len(s...  9.76 us
    ppermute x4, starting transfers between devices, swap_cores(): return lax.ppermute(block, AXES, [(i, i ^ 1) for i in range(256)])  1.76 us
    unnamed x8, local copies, waits for them, and re-layouts  1.62 us
  transfers between devices with their start and end apart: 19, of which 12 were waited for; matrix products, arithmetic and copies ran while one was open for 0% of the time, Pallas kernels for 16%

profile of v6, /device:TPU:1, one launch (start us, length us, event | category | flops | bytes accessed | tf_op | source)
XLA Modules:
  0.0 61.2 jit_solution(7287239401115124819)
XLA Ops:
  0.0 0.0 copy-start.2
  0.0 0.0 copy-start.3
  0.0 0.7 %copy-done.2 = s32[128]{0:T(128)S(1)} copy-done((s32[128]{0:T(128)S(1)}, s32[128]{0:T(128)}, u32[]{:S(2)}) %copy-start.2) | copy-done | bytes 536
  0.7 0.0 copy-done.3
  0.7 0.0 copy-start
  0.7 0.9 %copy-done = f32[128,512]{1,0:T(8,128)S(1)} copy-done((f32[128,512]{1,0:T(8,128)S(1)}, f32[128,512]{1,0:T(8,128)}, u32[]{:S(2)}) %copy-start) | copy-done | bytes 262168
  1.6 0.2 pack.1.refs_3_.refs_0_
  1.8 6.5 %collective-permute-start.5 = (bf16[528,128]{1,0:T(8,128)(2,1)S(1)}, bf16[528,128]{1,0:T(8,128)(2,1)S(1)}, u32[]{:S(2)}, u32[]{:S(2)}) collective-permute-start(bf16[528,128]{1,0:T(8,128)(2,1)S(1)} %pack.1.refs_3_.refs_0_), channel_id=1, source_target_pairs={{0,8},{1,201},{8,0},{9,65},{64,72},{65,9},{72,64},{73,129},{128,13... | collective-permute-start | bytes 405512 | tf_op jit(solution)/shard_map/ppermute | solution.py:46
  8.3 4.9 %collective-permute-start = (bf16[528,128]{1,0:T(8,128)(2,1)S(1)}, bf16[528,128]{1,0:T(8,128)(2,1)S(1)}, u32[]{:S(2)}, u32[]{:S(2)}) collective-permute-start(bf16[528,128]{1,0:T(8,128)(2,1)S(1)} %pack.1.refs_3_.refs_0_), channel_id=1, source_target_pairs={{0,18},{1,55},{8,26},{9,63},{64,82},{65,119},{72,90},{73,127},{128... | collective-permute-start | bytes 405512 | tf_op jit(solution)/shard_map/ppermute | solution.py:46
  13.2 0.2 collective-permute-start.1
  13.4 0.1 collective-permute-start.2
  13.5 0.0 collective-permute-done.5.refs_1_
  13.5 0.3 join.3
  13.9 0.1 collective-permute-start.6
  14.0 1.7 %collective-permute-done.refs_0_ = bf16[528,128]{1,0:T(8,128)(2,1)S(1)} collective-permute-done((bf16[528,128]{1,0:T(8,128)(2,1)S(1)}, bf16[528,128]{1,0:T(8,128)(2,1)S(1)}, u32[]{:S(2)}, u32[]{:S(2)}) %collective-permute-start) | collective-permute-done | bytes 135200 | tf_op jit(solution)/shard_map/ppermute | solution.py:46
  15.6 3.0 %collective-permute-done.1.refs_1_ = bf16[528,128]{1,0:T(8,128)(2,1)S(1)} collective-permute-done((bf16[528,128]{1,0:T(8,128)(2,1)S(1)}, bf16[528,128]{1,0:T(8,128)(2,1)S(1)}, u32[]{:S(2)}, u32[]{:S(2)}) %collective-permute-start.1) | collective-permute-done | bytes 135200 | tf_op jit(solution)/shard_map/ppermute | solution.py:46
  18.6 0.1 collective-permute-done.2.refs_2_
  18.7 0.7 %join.2 = bf16[2112,128]{1,0:T(8,128)(2,1)S(1)} custom-call(bf16[528,128]{1,0:T(8,128)(2,1)S(1)} %collective-permute-done.refs_0_, bf16[528,128]{1,0:T(8,128)(2,1)S(1)} %collective-permute-done.1.refs_1_, bf16[528,128]{1,0:T(8,128)(2,1)S(1)} %collective-permute-done.2.refs_2_, bf16[528,128]{1,0:T(8,128)(2,1)S(1)} %pack.1.refs_3_.refs_0_), custom_call_target="tpu_custom_call" | custom-call | tf_op jit(solution)/shard_map/join/pallas_call | solution.py:164
  19.5 0.1 collective-permute-start.9
  19.6 0.1 collective-permute-start.3
  19.7 2.5 %collective-permute-start.4 = (bf16[2112,128]{1,0:T(8,128)(2,1)S(1)}, bf16[2112,128]{1,0:T(8,128)(2,1)S(1)}, u32[]{:S(2)}, u32[]{:S(2)}) collective-permute-start(bf16[2112,128]{1,0:T(8,128)(2,1)S(1)} %join.2), channel_id=1, source_target_pairs={{0,54},{1,19},{8,62},{9,27},{64,118},{65,83},{72,126},{73,91},{128... | collective-permute-start | bytes 1622024 | tf_op jit(solution)/shard_map/ppermute | solution.py:46
  22.2 0.0 collective-permute-done.6
  22.2 0.9 %collective-permute-start.8 = (bf16[1056,128]{1,0:T(8,128)(2,1)S(1)}, bf16[1056,128]{1,0:T(8,128)(2,1)S(1)}, u32[]{:S(2)}, u32[]{:S(2)}) collective-permute-start(bf16[1056,128]{1,0:T(8,128)(2,1)S(1)} %collective-permute-done.6), channel_id=1, source_target_pairs={{0,64},{1,193},{8,200},{9,73},{64,128},{65,1},{72,8},{73,137},{128... | collective-permute-start | bytes 811016 | tf_op jit(solution)/shard_map/ppermute | solution.py:54
  23.1 0.0 collective-permute-start.7
  23.1 8.2 %collective-permute-done.8 = bf16[1056,128]{1,0:T(8,128)(2,1)S(1)} collective-permute-done((bf16[1056,128]{1,0:T(8,128)(2,1)S(1)}, bf16[1056,128]{1,0:T(8,128)(2,1)S(1)}, u32[]{:S(2)}, u32[]{:S(2)}) %collective-permute-start.8) | collective-permute-done | bytes 270368 | tf_op jit(solution)/shard_map/ppermute | solution.py:54
  31.3 0.7 %collective-permute-start.10 = (bf16[2112,128]{1,0:T(8,128)(2,1)S(1)}, bf16[2112,128]{1,0:T(8,128)(2,1)S(1)}, u32[]{:S(2)}, u32[]{:S(2)}) collective-permute-start(bf16[2112,128]{1,0:T(8,128)(2,1)S(1)} %join.2), channel_id=1, source_target_pairs={{0,1},{1,0},{2,3},{3,2},{4,5},{5,4},{6,7},{7,6},{8,9},{9,8},{10,11... | collective-permute-start | bytes 1622024 | tf_op jit(solution)/shard_map/ppermute | solution.py:58
  32.0 0.0 collective-permute-done.9
  32.0 0.0 collective-permute-start.11
  32.0 0.7 %pair.5.refs_5_ = f32[256,512]{1,0:T(8,128)S(1)} custom-call(bf16[2,528,128]{2,1,0:T(8,128)(2,1)S(1)} %bitcast.24, bf16[4,528,128]{2,1,0:T(8,128)(2,1)S(1)} %bitcast.14, bf16[4,528,128]{2,1,0:T(8,128)(2,1)S(1)} %bitcast.29), custom_call_target="tpu_custom_call" | custom-call | flops 536870912 | bytes 1310720 | tf_op jit(solution)/shard_map/pair/pallas_call | solution.py:135
  32.7 0.1 collective-permute-done.7
  32.8 1.1 %collective-permute-done.3 = bf16[2112,128]{1,0:T(8,128)(2,1)S(1)} collective-permute-done((bf16[2112,128]{1,0:T(8,128)(2,1)S(1)}, bf16[2112,128]{1,0:T(8,128)(2,1)S(1)}, u32[]{:S(2)}, u32[]{:S(2)}) %collective-permute-start.3) | collective-permute-done | bytes 540704 | tf_op jit(solution)/shard_map/ppermute | solution.py:46
  33.9 0.0 collective-permute-done.4
  34.0 1.0 %collective-permute-start.12 = (bf16[2112,128]{1,0:T(8,128)(2,1)S(1)}, bf16[2112,128]{1,0:T(8,128)(2,1)S(1)}, u32[]{:S(2)}, u32[]{:S(2)}) collective-permute-start(bf16[2112,128]{1,0:T(8,128)(2,1)S(1)} %collective-permute-done.3), channel_id=1, source_target_pairs={{0,1},{1,0},{2,3},{3,2},{4,5},{5,4},{6,7},{7,6},{8,9},{9,8},{10,11... | collective-permute-start | bytes 1622024 | tf_op jit(solution)/shard_map/ppermute | solution.py:58
  35.0 0.1 collective-permute-start.13
  35.0 0.0 collective-permute-done.10
  35.1 0.0 collective-permute-done.11
  35.1 1.3 %pair.8.refs_3_ = f32[256,512]{1,0:T(8,128)S(1)} custom-call(bf16[2,528,128]{2,1,0:T(8,128)(2,1)S(1)} %bitcast.25, bf16[4,528,128]{2,1,0:T(8,128)(2,1)S(1)} %bitcast.32, bf16[4,528,128]{2,1,0:T(8,128)(2,1)S(1)} %bitcast.35, bf16[4,528,128]{2,1,0:T(8,128)(2,1)S(1)} %bitcast.38, bf16[4,528,128]{2,1,0:T(8,128)(2,1)S(1)} %bitcast.41, f32[256,512]{1,0:T(8,128)S(1)} %pair.5.refs_5_), custom_call_target="tpu_custom_call" | custom-call | flops 1073741824 | bytes 2359296 | tf_op jit(solution)/shard_map/pair/pallas_call | solution.py:135
  36.4 0.2 collective-permute-done.12
  36.5 0.8 %collective-permute-done.13 = bf16[2112,128]{1,0:T(8,128)(2,1)S(1)} collective-permute-done((bf16[2112,128]{1,0:T(8,128)(2,1)S(1)}, bf16[2112,128]{1,0:T(8,128)(2,1)S(1)}, u32[]{:S(2)}, u32[]{:S(2)}) %collective-permute-start.13) | collective-permute-done | bytes 540704 | tf_op jit(solution)/shard_map/ppermute | solution.py:58
  37.3 0.7 %pair.9 = bf16[256,512]{1,0:T(8,128)(2,1)S(1)} custom-call(bf16[2,528,128]{2,1,0:T(8,128)(2,1)S(1)} %bitcast.26, bf16[4,528,128]{2,1,0:T(8,128)(2,1)S(1)} %bitcast.17, bf16[4,528,128]{2,1,0:T(8,128)(2,1)S(1)} %bitcast.20, f32[256,512]{1,0:T(8,128)S(1)} %pair.8.refs_3_), custom_call_target="tpu_custom_call" | custom-call | flops 536870912 | bytes 1310720 | tf_op jit(solution)/shard_map/pair/pallas_call | solution.py:135
  38.0 0.3 collective-permute-start.15
  38.3 4.6 %pair.6 = (f32[256,512]{1,0:T(8,128)S(1)}, f32[256,512]{1,0:T(8,128)S(1)}) custom-call(bf16[2,528,128]{2,1,0:T(8,128)(2,1)S(1)} %bitcast.45, bf16[2,528,128]{2,1,0:T(8,128)(2,1)S(1)} %bitcast.23, bf16[4,528,128]{2,1,0:T(8,128)(2,1)S(1)} %bitcast.15, bf16[4,528,128]{2,1,0:T(8,128)(2,1)S(1)} %bitcast.30, bf16[4,528,128]{2,1,0:T(8,128)(2,1)S(1)} %bitcast.33, ...), custom_call_target="tpu_custom_call" | custom-call | flops 4294967296 | bytes 4718592 | tf_op jit(solution)/shard_map/pair/pallas_call | solution.py:135
  42.9 0.9 %collective-permute-done.15 = bf16[256,512]{1,0:T(8,128)(2,1)S(1)} collective-permute-done((bf16[256,512]{1,0:T(8,128)(2,1)S(1)}, bf16[256,512]{1,0:T(8,128)(2,1)S(1)}, u32[]{:S(2)}, u32[]{:S(2)}) %collective-permute-start.15) | collective-permute-done | bytes 262176 | tf_op jit(solution)/shard_map/ppermute | solution.py:46
  43.8 0.1 add_convert_fusion.1
  43.9 3.1 %collective-permute-start.16 = (bf16[256,512]{1,0:T(8,128)(2,1)S(1)}, bf16[256,512]{1,0:T(8,128)(2,1)S(1)}, u32[]{:S(2)}, u32[]{:S(2)}) collective-permute-start(bf16[256,512]{1,0:T(8,128)(2,1)S(1)} %add_convert_fusion.1), channel_id=1, source_target_pairs={{0,8},{1,201},{8,0},{9,65},{64,72},{65,9},{72,64},{73,129},{128,13... | collective-permute-start | bytes 786440 | tf_op jit(solution)/shard_map/ppermute | solution.py:46
  47.0 0.1 collective-permute-start.14
  47.1 2.4 %pair.7 = f32[256,512]{1,0:T(8,128)S(1)} custom-call(bf16[2,528,128]{2,1,0:T(8,128)(2,1)S(1)} %bitcast.44, bf16[4,528,128]{2,1,0:T(8,128)(2,1)S(1)} %bitcast.16, bf16[4,528,128]{2,1,0:T(8,128)(2,1)S(1)} %bitcast.31, bf16[4,528,128]{2,1,0:T(8,128)(2,1)S(1)} %bitcast.34, bf16[4,528,128]{2,1,0:T(8,128)(2,1)S(1)} %bitcast.37, bf16[4,528,128]{2,1,0:T(8,128)(2,1)S(1)} %bitcast.40, ...), custom_call_target="tpu_custom_call" | custom-call | flops 2147483648 | bytes 4456448 | tf_op jit(solution)/shard_map/pair/pallas_call | solution.py:135
  49.5 1.2 %collective-permute-done.16 = bf16[256,512]{1,0:T(8,128)(2,1)S(1)} collective-permute-done((bf16[256,512]{1,0:T(8,128)(2,1)S(1)}, bf16[256,512]{1,0:T(8,128)(2,1)S(1)}, u32[]{:S(2)}, u32[]{:S(2)}) %collective-permute-start.16) | collective-permute-done | bytes 262176 | tf_op jit(solution)/shard_map/ppermute | solution.py:46
  50.8 0.1 add_convert_fusion
  50.9 0.2 collective-permute-start.17
  51.0 0.0 copy-start.1
  51.0 3.8 %collective-permute-start.18 = (bf16[128,512]{1,0:T(8,128)(2,1)S(1)}, bf16[128,512]{1,0:T(8,128)(2,1)S(1)}, u32[]{:S(2)}, u32[]{:S(2)}) collective-permute-start(bf16[128,512]{1,0:T(8,128)(2,1)S(1)} %get-tuple-element.17), channel_id=1, source_target_pairs={{0,200},{1,9},{8,64},{9,1},{64,8},{65,73},{72,128},{73,65},{128,72... | collective-permute-start | bytes 393224 | tf_op jit(solution)/shard_map/ppermute | solution.py:46
  54.8 0.0 collective-permute-done.14.refs_0_
  54.8 2.9 %collective-permute-done.17.refs_1_ = bf16[128,512]{1,0:T(8,128)(2,1)S(1)} collective-permute-done((bf16[128,512]{1,0:T(8,128)(2,1)S(1)}, bf16[128,512]{1,0:T(8,128)(2,1)S(1)}, u32[]{:S(2)}, u32[]{:S(2)}) %collective-permute-start.17) | collective-permute-done | bytes 131104 | tf_op jit(solution)/shard_map/ppermute | solution.py:54
  57.7 2.5 %collective-permute-done.18.refs_2_ = bf16[128,512]{1,0:T(8,128)(2,1)S(1)} collective-permute-done((bf16[128,512]{1,0:T(8,128)(2,1)S(1)}, bf16[128,512]{1,0:T(8,128)(2,1)S(1)}, u32[]{:S(2)}, u32[]{:S(2)}) %collective-permute-start.18) | collective-permute-done | bytes 131104 | tf_op jit(solution)/shard_map/ppermute | solution.py:46
  60.3 0.0 copy-done.1
  60.3 0.9 %final.1 = f32[128,512]{1,0:T(8,128)} custom-call(f32[128,512]{1,0:T(8,128)S(1)} %copy-done.1, f32[128,512]{1,0:T(8,128)S(1)} %slice.13.own, bf16[128,512]{1,0:T(8,128)(2,1)S(1)} %collective-permute-done.14.refs_0_, bf16[128,512]{1,0:T(8,128)(2,1)S(1)} %collective-permute-done.17.refs_1_, bf16[128,512]{1,0:T(8,128)(2,1)S(1)} %collective-permute-done.18.refs_2_), custom_call_target="tpu_custom_call" | custom-call | tf_op jit(solution)/shard_map/final/pallas_call | solution.py:212
  (3 shorter events, 0.1 us)
Async XLA Ops:
  0.0 0.7 %copy-start.2 = (s32[128]{0:T(128)S(1)}, s32[128]{0:T(128)}, u32[]{:S(2)}) copy-start(s32[128]{0:T(128)} %param.4) | copy-start | bytes 1540
  0.0 0.7 %copy-start.3 = (s32[128]{0:T(128)S(1)}, s32[128]{0:T(128)}, u32[]{:S(2)}) copy-start(s32[128]{0:T(128)} %param.5) | copy-start | bytes 1540
  0.7 0.9 %copy-start = (f32[128,512]{1,0:T(8,128)S(1)}, f32[128,512]{1,0:T(8,128)}, u32[]{:S(2)}) copy-start(f32[128,512]{1,0:T(8,128)} %emb.1) | copy-start | bytes 786436
  1.8 11.7 %collective-permute-start.5 = (bf16[528,128]{1,0:T(8,128)(2,1)S(1)}, bf16[528,128]{1,0:T(8,128)(2,1)S(1)}, u32[]{:S(2)}, u32[]{:S(2)}) collective-permute-start(bf16[528,128]{1,0:T(8,128)(2,1)S(1)} %pack.1.refs_3_.refs_0_), channel_id=1, source_target_pairs={{0,8},{1,201},{8,0},{9,65},{64,72},{65,9},{72,64},{73,129},{128,13... | collective-permute-start | bytes 405512 | tf_op jit(solution)/shard_map/ppermute | solution.py:46
  8.3 7.3 %collective-permute-start = (bf16[528,128]{1,0:T(8,128)(2,1)S(1)}, bf16[528,128]{1,0:T(8,128)(2,1)S(1)}, u32[]{:S(2)}, u32[]{:S(2)}) collective-permute-start(bf16[528,128]{1,0:T(8,128)(2,1)S(1)} %pack.1.refs_3_.refs_0_), channel_id=1, source_target_pairs={{0,18},{1,55},{8,26},{9,63},{64,82},{65,119},{72,90},{73,127},{128... | collective-permute-start | bytes 405512 | tf_op jit(solution)/shard_map/ppermute | solution.py:46
  13.2 5.4 %collective-permute-start.1 = (bf16[528,128]{1,0:T(8,128)(2,1)S(1)}, bf16[528,128]{1,0:T(8,128)(2,1)S(1)}, u32[]{:S(2)}, u32[]{:S(2)}) collective-permute-start(bf16[528,128]{1,0:T(8,128)(2,1)S(1)} %pack.1.refs_3_.refs_0_), channel_id=1, source_target_pairs={{0,16},{1,49},{8,24},{9,57},{64,80},{65,113},{72,88},{73,121},{128... | collective-permute-start | bytes 405512 | tf_op jit(solution)/shard_map/ppermute | solution.py:46
  13.4 5.3 %collective-permute-start.2 = (bf16[528,128]{1,0:T(8,128)(2,1)S(1)}, bf16[528,128]{1,0:T(8,128)(2,1)S(1)}, u32[]{:S(2)}, u32[]{:S(2)}) collective-permute-start(bf16[528,128]{1,0:T(8,128)(2,1)S(1)} %pack.1.refs_3_.refs_0_), channel_id=1, source_target_pairs={{0,2},{1,7},{8,10},{9,15},{64,66},{65,71},{72,74},{73,79},{128,130... | collective-permute-start | bytes 405512 | tf_op jit(solution)/shard_map/ppermute | solution.py:46
  13.9 8.3 %collective-permute-start.6 = (bf16[1056,128]{1,0:T(8,128)(2,1)S(1)}, bf16[1056,128]{1,0:T(8,128)(2,1)S(1)}, u32[]{:S(2)}, u32[]{:S(2)}) collective-permute-start(bf16[1056,128]{1,0:T(8,128)(2,1)S(1)} %join.3), channel_id=1, source_target_pairs={{0,200},{1,9},{8,64},{9,1},{64,8},{65,73},{72,128},{73,65},{128,72... | collective-permute-start | bytes 811016 | tf_op jit(solution)/shard_map/ppermute | solution.py:46
  19.5 12.5 %collective-permute-start.9 = (bf16[2112,128]{1,0:T(8,128)(2,1)S(1)}, bf16[2112,128]{1,0:T(8,128)(2,1)S(1)}, u32[]{:S(2)}, u32[]{:S(2)}) collective-permute-start(bf16[2112,128]{1,0:T(8,128)(2,1)S(1)} %join.2), channel_id=1, source_target_pairs={{0,48},{1,17},{8,56},{9,25},{64,112},{65,81},{72,120},{73,89},{128... | collective-permute-start | bytes 1622024 | tf_op jit(solution)/shard_map/ppermute | solution.py:46
  19.6 14.3 %collective-permute-start.3 = (bf16[2112,128]{1,0:T(8,128)(2,1)S(1)}, bf16[2112,128]{1,0:T(8,128)(2,1)S(1)}, u32[]{:S(2)}, u32[]{:S(2)}) collective-permute-start(bf16[2112,128]{1,0:T(8,128)(2,1)S(1)} %join.2), channel_id=1, source_target_pairs={{0,6},{1,3},{8,14},{9,11},{64,70},{65,67},{72,78},{73,75},{128,134... | collective-permute-start | bytes 1622024 | tf_op jit(solution)/shard_map/ppermute | solution.py:46
  19.7 14.3 %collective-permute-start.4 = (bf16[2112,128]{1,0:T(8,128)(2,1)S(1)}, bf16[2112,128]{1,0:T(8,128)(2,1)S(1)}, u32[]{:S(2)}, u32[]{:S(2)}) collective-permute-start(bf16[2112,128]{1,0:T(8,128)(2,1)S(1)} %join.2), channel_id=1, source_target_pairs={{0,54},{1,19},{8,62},{9,27},{64,118},{65,83},{72,126},{73,91},{128... | collective-permute-start | bytes 1622024 | tf_op jit(solution)/shard_map/ppermute | solution.py:46
  22.2 9.1 %collective-permute-start.8 = (bf16[1056,128]{1,0:T(8,128)(2,1)S(1)}, bf16[1056,128]{1,0:T(8,128)(2,1)S(1)}, u32[]{:S(2)}, u32[]{:S(2)}) collective-permute-start(bf16[1056,128]{1,0:T(8,128)(2,1)S(1)} %collective-permute-done.6), channel_id=1, source_target_pairs={{0,64},{1,193},{8,200},{9,73},{64,128},{65,1},{72,8},{73,137},{128... | collective-permute-start | bytes 811016 | tf_op jit(solution)/shard_map/ppermute | solution.py:54
  23.1 9.7 %collective-permute-start.7 = (bf16[1056,128]{1,0:T(8,128)(2,1)S(1)}, bf16[1056,128]{1,0:T(8,128)(2,1)S(1)}, u32[]{:S(2)}, u32[]{:S(2)}) collective-permute-start(bf16[1056,128]{1,0:T(8,128)(2,1)S(1)} %collective-permute-done.6), channel_id=1, source_target_pairs={{0,8},{1,201},{8,0},{9,65},{64,72},{65,9},{72,64},{73,129},{128,13... | collective-permute-start | bytes 811016 | tf_op jit(solution)/shard_map/ppermute | solution.py:46
  31.3 3.7 %collective-permute-start.10 = (bf16[2112,128]{1,0:T(8,128)(2,1)S(1)}, bf16[2112,128]{1,0:T(8,128)(2,1)S(1)}, u32[]{:S(2)}, u32[]{:S(2)}) collective-permute-start(bf16[2112,128]{1,0:T(8,128)(2,1)S(1)} %join.2), channel_id=1, source_target_pairs={{0,1},{1,0},{2,3},{3,2},{4,5},{5,4},{6,7},{7,6},{8,9},{9,8},{10,11... | collective-permute-start | bytes 1622024 | tf_op jit(solution)/shard_map/ppermute | solution.py:58
  32.0 3.1 %collective-permute-start.11 = (bf16[2112,128]{1,0:T(8,128)(2,1)S(1)}, bf16[2112,128]{1,0:T(8,128)(2,1)S(1)}, u32[]{:S(2)}, u32[]{:S(2)}) collective-permute-start(bf16[2112,128]{1,0:T(8,128)(2,1)S(1)} %collective-permute-done.9), channel_id=1, source_target_pairs={{0,1},{1,0},{2,3},{3,2},{4,5},{5,4},{6,7},{7,6},{8,9},{9,8},{10,11... | collective-permute-start | bytes 1622024 | tf_op jit(solution)/shard_map/ppermute | solution.py:58
  34.0 2.6 %collective-permute-start.12 = (bf16[2112,128]{1,0:T(8,128)(2,1)S(1)}, bf16[2112,128]{1,0:T(8,128)(2,1)S(1)}, u32[]{:S(2)}, u32[]{:S(2)}) collective-permute-start(bf16[2112,128]{1,0:T(8,128)(2,1)S(1)} %collective-permute-done.3), channel_id=1, source_target_pairs={{0,1},{1,0},{2,3},{3,2},{4,5},{5,4},{6,7},{7,6},{8,9},{9,8},{10,11... | collective-permute-start | bytes 1622024 | tf_op jit(solution)/shard_map/ppermute | solution.py:58
  35.0 2.3 %collective-permute-start.13 = (bf16[2112,128]{1,0:T(8,128)(2,1)S(1)}, bf16[2112,128]{1,0:T(8,128)(2,1)S(1)}, u32[]{:S(2)}, u32[]{:S(2)}) collective-permute-start(bf16[2112,128]{1,0:T(8,128)(2,1)S(1)} %collective-permute-done.4), channel_id=1, source_target_pairs={{0,1},{1,0},{2,3},{3,2},{4,5},{5,4},{6,7},{7,6},{8,9},{9,8},{10,11... | collective-permute-start | bytes 1622024 | tf_op jit(solution)/shard_map/ppermute | solution.py:58
  38.0 5.8 %collective-permute-start.15 = (bf16[256,512]{1,0:T(8,128)(2,1)S(1)}, bf16[256,512]{1,0:T(8,128)(2,1)S(1)}, u32[]{:S(2)}, u32[]{:S(2)}) collective-permute-start(bf16[256,512]{1,0:T(8,128)(2,1)S(1)} %pair.9), channel_id=1, source_target_pairs={{0,200},{1,9},{8,64},{9,1},{64,8},{65,73},{72,128},{73,65},{128,72... | collective-permute-start | bytes 786440 | tf_op jit(solution)/shard_map/ppermute | solution.py:46
  43.9 6.9 %collective-permute-start.16 = (bf16[256,512]{1,0:T(8,128)(2,1)S(1)}, bf16[256,512]{1,0:T(8,128)(2,1)S(1)}, u32[]{:S(2)}, u32[]{:S(2)}) collective-permute-start(bf16[256,512]{1,0:T(8,128)(2,1)S(1)} %add_convert_fusion.1), channel_id=1, source_target_pairs={{0,8},{1,201},{8,0},{9,65},{64,72},{65,9},{72,64},{73,129},{128,13... | collective-permute-start | bytes 786440 | tf_op jit(solution)/shard_map/ppermute | solution.py:46
  47.0 7.8 %collective-permute-start.14 = (bf16[128,512]{1,0:T(8,128)(2,1)S(1)}, bf16[128,512]{1,0:T(8,128)(2,1)S(1)}, u32[]{:S(2)}, u32[]{:S(2)}) collective-permute-start(bf16[128,512]{1,0:T(8,128)(2,1)S(1)} %slice.21), channel_id=1, source_target_pairs={{0,8},{1,201},{8,0},{9,65},{64,72},{65,9},{72,64},{73,129},{128,13... | collective-permute-start | bytes 393224 | tf_op jit(solution)/shard_map/ppermute | solution.py:46
  50.9 6.8 %collective-permute-start.17 = (bf16[128,512]{1,0:T(8,128)(2,1)S(1)}, bf16[128,512]{1,0:T(8,128)(2,1)S(1)}, u32[]{:S(2)}, u32[]{:S(2)}) collective-permute-start(bf16[128,512]{1,0:T(8,128)(2,1)S(1)} %get-tuple-element.18), channel_id=1, source_target_pairs={{0,192},{1,65},{8,72},{9,201},{64,0},{65,129},{72,136},{73,9},{128... | collective-permute-start | bytes 393224 | tf_op jit(solution)/shard_map/ppermute | solution.py:54
  51.0 9.2 %copy-start.1 = (f32[128,512]{1,0:T(8,128)S(1)}, f32[128,512]{1,0:T(8,128)}, u32[]{:S(2)}) copy-start(f32[128,512]{1,0:T(8,128)} %emb.1) | copy-start | bytes 786436
  51.0 9.2 %collective-permute-start.18 = (bf16[128,512]{1,0:T(8,128)(2,1)S(1)}, bf16[128,512]{1,0:T(8,128)(2,1)S(1)}, u32[]{:S(2)}, u32[]{:S(2)}) collective-permute-start(bf16[128,512]{1,0:T(8,128)(2,1)S(1)} %get-tuple-element.17), channel_id=1, source_target_pairs={{0,200},{1,9},{8,64},{9,1},{64,8},{65,73},{72,128},{73,65},{128,72... | collective-permute-start | bytes 393224 | tf_op jit(solution)/shard_map/ppermute | solution.py:46

commit v7 on v6

--- a/solution.py
+++ b/solution.py
@@ -20,7 +20,6 @@
 SMALL = 6 << 20
 AXES = ("row", "col")
 VMEM = pl.BlockSpec(memory_space=pltpu.VMEM)
-ANY = pl.BlockSpec(memory_space=pl.ANY)
 
 
 def _flat(x, y, z, core):
@@ -58,37 +57,38 @@
     return lax.ppermute(block, AXES, [(i, i ^ 1) for i in range(256)])
 
 
-def pack_kernel(emb_hbm, margin_hbm, group_hbm, whole, emb, margin, group, sem):
-    pairs = ((emb_hbm, emb), (margin_hbm, margin), (group_hbm, group))
-    copies = [pltpu.make_async_copy(src, dst, sem.at[i]) for i, (src, dst) in enumerate(pairs)]
-    for c in copies:
-        c.start()
-    for c in copies:
-        c.wait()
+def units_kernel(emb, out):
     e = emb[...]
     unit = (e / jnp.sqrt(jnp.sum(e * e, axis=1, keepdims=True) + 1e-06)).astype(BF)
+    for f in range(CHUNKS):
+        out[f * CPD : (f + 1) * CPD, :] = unit[:, f * LANES : (f + 1) * LANES]
+
+
+def pack_kernel(unit, margin, group, whole):
     row = lax.broadcasted_iota(jnp.int32, (META, LANES), 0)
     meta = jnp.where(row == 0, margin[...], jnp.where(row == 1, group[...], 0)).astype(F32).astype(BF)
-    for f in range(CHUNKS):
-        whole[f * CPD : (f + 1) * CPD, :] = unit[:, f * LANES : (f + 1) * LANES]
+    whole[: CHUNKS * CPD, :] = unit[...]
     whole[CHUNKS * CPD :, :] = meta
 
 
 def pack(embeddings, margin, group):
+    params = pltpu.CompilerParams(vmem_limit_bytes=SMALL)
+    unit = pl.pallas_call(
+        units_kernel,
+        out_shape=jax.ShapeDtypeStruct((CHUNKS * CPD, LANES), BF),
+        in_specs=[VMEM],
+        out_specs=VMEM,
+        compiler_params=params,
+        name="units",
+    )(embeddings)
     return pl.pallas_call(
         pack_kernel,
         out_shape=jax.ShapeDtypeStruct((PACKED, LANES), BF),
-        in_specs=[pl.BlockSpec(memory_space=pltpu.HBM)] * 3,
-        out_specs=VMEM,
-        scratch_shapes=[
-            pltpu.VMEM((CPD, D), F32),
-            pltpu.VMEM((1, CPD), jnp.int32),
-            pltpu.VMEM((1, CPD), jnp.int32),
-            pltpu.SemaphoreType.DMA((3,)),
-        ],
-        compiler_params=pltpu.CompilerParams(vmem_limit_bytes=SMALL),
+        in_specs=[VMEM] * 3,
+        out_specs=VMEM,
+        compiler_params=params,
         name="pack",
-    )(embeddings, margin.reshape(1, CPD), group.reshape(1, CPD))
+    )(unit, margin.reshape(1, CPD), group.reshape(1, CPD))
 
 
 TB = 8
@@ -145,28 +145,21 @@
     )(*r_in, *c_in, *sums)
 
 
-def join_kernel(pieces, n_in, *refs):
-    ins, outs, sem = refs[:n_in], refs[n_in:-1], refs[-1]
-    copies = []
-    for out, which in zip(outs, pieces, strict=True):
-        at = 0
-        for i in which:
-            n = ins[i].shape[0]
-            copies.append(pltpu.make_async_copy(ins[i], out.at[at : at + n], sem.at[len(copies)]))
-            at += n
-    for c in copies:
-        c.start()
-    for c in copies:
-        c.wait()
-
-
-def join(pieces, *ins):
-    return pl.pallas_call(
-        functools.partial(join_kernel, pieces, len(ins)),
-        out_shape=[jax.ShapeDtypeStruct((sum(ins[i].shape[0] for i in p), LANES), BF) for p in pieces],
-        in_specs=[ANY] * len(ins),
-        out_specs=[VMEM] * len(pieces),
-        scratch_shapes=[pltpu.SemaphoreType.DMA((sum(map(len, pieces)),))],
+def join_kernel(*refs):
+    ins, out = refs[:-1], refs[-1]
+    at = 0
+    for ref in ins:
+        n = ref.shape[0]
+        out[at : at + n, :] = ref[...]
+        at += n
+
+
+def join(*ins):
+    return pl.pallas_call(
+        join_kernel,
+        out_shape=jax.ShapeDtypeStruct((sum(a.shape[0] for a in ins), LANES), BF),
+        in_specs=[VMEM] * len(ins),
+        out_specs=VMEM,
         compiler_params=pltpu.CompilerParams(vmem_limit_bytes=SMALL),
         name="join",
     )(*ins)
@@ -188,9 +181,9 @@
 
     near = swap(whole, "za", "zb")
     square = [swap(whole, a, b) for a, b in (("xaya", "xbyb"), ("xa", "xb"), ("ya", "yb"))]
-    (both,) = join(((0, 1),), whole, near)
+    both = join(whole, near)
     back = swap(both, "zb", "za")
-    (c0,) = join(((3, 0, 1, 2),), *square, whole)
+    c0 = join(*square, whole)
     far, ahead = shift(back, 1), swap(back, "za", "zb")
     c3, c1, c2 = (swap(c0, b, a) for a, b in (("xaya", "xbyb"), ("xa", "xb"), ("ya", "yb")))
     e0 = swap_cores(c0)

time: 61.3 us -> 60.6 us (0.989)
  Pallas kernels: 11.9 us -> 11 us
    pallas_call x2 -> x3, Pallas kernels: 1.05 us -> 0.18 us  [the longest x1 0.12 us: pack(): pl.pallas_call(units_kernel, out_shape=jax.ShapeDtypeStruct((CHUNKS * CPD...]
  transfers between devices with their start and end apart: 19 -> 19, of which waited for: 12 -> 12; matrix products, arithmetic and copies ran while one was open for 0% -> 0% of each run, Pallas kernels for 16% -> 15%
where the time goes in v7:
time: 60.6 us; the launch traced here: 60.5 us
  starting transfers between devices  25.1 us (41%)
  waiting for transfers between devices  22.4 us (37%)
  Pallas kernels  11 us (18%)
  local copies, waits for them, and re-layouts  1.67 us (3%)
    ppermute x13, starting transfers between devices, swap(): return lax.ppermute(block, AXES, pairs)  22 us
    ppermute x2, waiting for transfers between devices, shift(): return lax.ppermute(block, AXES, pairs)  10.8 us
    ppermute x13, waiting for transfers between devices, swap(): return lax.ppermute(block, AXES, pairs)  10.7 us
    pallas_call x5, Pallas kernels, pair(): pl.pallas_call(functools.partial(pair_kernel, len(r_in), len(c_in), len(s...  9.82 us
    ppermute x4, starting transfers between devices, swap_cores(): return lax.ppermute(block, AXES, [(i, i ^ 1) for i in range(256)])  1.8 us
    unnamed x8, local copies, waits for them, and re-layouts  1.61 us
    ppermute x2, starting transfers between devices, shift(): return lax.ppermute(block, AXES, pairs)  1.33 us
  transfers between devices with their start and end apart: 19, of which 12 were waited for; matrix products, arithmetic and copies ran while one was open for 0% of the time, Pallas kernels for 15%

profile of v7, /device:TPU:1, one launch (start us, length us, event | category | flops | bytes accessed | tf_op | source)
XLA Modules:
  0.0 60.5 jit_solution(10661436079866024663)
XLA Ops:
  0.0 0.0 copy-start
  0.0 0.9 %copy-done = f32[128,512]{1,0:T(8,128)S(1)} copy-done((f32[128,512]{1,0:T(8,128)S(1)}, f32[128,512]{1,0:T(8,128)}, u32[]{:S(2)}) %copy-start) | copy-done | bytes 262168
  1.0 0.1 units.1.unit
  1.1 0.0 copy-start.2
  1.1 0.0 copy-start.3
  1.1 0.6 %copy-done.2 = s32[128]{0:T(128)S(1)} copy-done((s32[128]{0:T(128)S(1)}, s32[128]{0:T(128)}, u32[]{:S(2)}) %copy-start.2) | copy-done | bytes 536
  1.7 0.0 copy-done.3
  1.8 6.5 %collective-permute-start.5 = (bf16[528,128]{1,0:T(8,128)(2,1)S(1)}, bf16[528,128]{1,0:T(8,128)(2,1)S(1)}, u32[]{:S(2)}, u32[]{:S(2)}) collective-permute-start(bf16[528,128]{1,0:T(8,128)(2,1)S(1)} %pack.1.refs_3_.refs_0_), channel_id=1, source_target_pairs={{0,8},{1,201},{8,0},{9,65},{64,72},{65,9},{72,64},{73,129},{128,13... | collective-permute-start | bytes 405512 | tf_op jit(solution)/shard_map/ppermute | solution.py:45
  8.3 4.9 %collective-permute-start = (bf16[528,128]{1,0:T(8,128)(2,1)S(1)}, bf16[528,128]{1,0:T(8,128)(2,1)S(1)}, u32[]{:S(2)}, u32[]{:S(2)}) collective-permute-start(bf16[528,128]{1,0:T(8,128)(2,1)S(1)} %pack.1.refs_3_.refs_0_), channel_id=1, source_target_pairs={{0,18},{1,55},{8,26},{9,63},{64,82},{65,119},{72,90},{73,127},{128... | collective-permute-start | bytes 405512 | tf_op jit(solution)/shard_map/ppermute | solution.py:45
  13.2 0.2 collective-permute-start.1
  13.4 0.1 collective-permute-start.2
  13.5 0.0 collective-permute-done.5.refs_1_
  13.5 0.1 collective-permute-start.6
  13.6 2.0 %collective-permute-done.refs_0_ = bf16[528,128]{1,0:T(8,128)(2,1)S(1)} collective-permute-done((bf16[528,128]{1,0:T(8,128)(2,1)S(1)}, bf16[528,128]{1,0:T(8,128)(2,1)S(1)}, u32[]{:S(2)}, u32[]{:S(2)}) %collective-permute-start) | collective-permute-done | bytes 135200 | tf_op jit(solution)/shard_map/ppermute | solution.py:45
  15.6 2.8 %collective-permute-done.1.refs_1_ = bf16[528,128]{1,0:T(8,128)(2,1)S(1)} collective-permute-done((bf16[528,128]{1,0:T(8,128)(2,1)S(1)}, bf16[528,128]{1,0:T(8,128)(2,1)S(1)}, u32[]{:S(2)}, u32[]{:S(2)}) %collective-permute-start.1) | collective-permute-done | bytes 135200 | tf_op jit(solution)/shard_map/ppermute | solution.py:45
  18.4 0.1 collective-permute-done.2.refs_2_
  18.5 0.4 collective-permute-start.9
  18.9 0.0 collective-permute-start.3
  18.9 2.4 %collective-permute-start.4 = (bf16[2112,128]{1,0:T(8,128)(2,1)S(1)}, bf16[2112,128]{1,0:T(8,128)(2,1)S(1)}, u32[]{:S(2)}, u32[]{:S(2)}) collective-permute-start(bf16[2112,128]{1,0:T(8,128)(2,1)S(1)} %join.2), channel_id=1, source_target_pairs={{0,54},{1,19},{8,62},{9,27},{64,118},{65,83},{72,126},{73,91},{128... | collective-permute-start | bytes 1622024 | tf_op jit(solution)/shard_map/ppermute | solution.py:45
  21.2 0.0 collective-permute-done.6
  21.2 1.2 %collective-permute-start.8 = (bf16[1056,128]{1,0:T(8,128)(2,1)S(1)}, bf16[1056,128]{1,0:T(8,128)(2,1)S(1)}, u32[]{:S(2)}, u32[]{:S(2)}) collective-permute-start(bf16[1056,128]{1,0:T(8,128)(2,1)S(1)} %collective-permute-done.6), channel_id=1, source_target_pairs={{0,64},{1,193},{8,200},{9,73},{64,128},{65,1},{72,8},{73,137},{128... | collective-permute-start | bytes 811016 | tf_op jit(solution)/shard_map/ppermute | solution.py:53
  22.4 0.0 collective-permute-start.7
  22.4 7.9 %collective-permute-done.8 = bf16[1056,128]{1,0:T(8,128)(2,1)S(1)} collective-permute-done((bf16[1056,128]{1,0:T(8,128)(2,1)S(1)}, bf16[1056,128]{1,0:T(8,128)(2,1)S(1)}, u32[]{:S(2)}, u32[]{:S(2)}) %collective-permute-start.8) | collective-permute-done | bytes 270368 | tf_op jit(solution)/shard_map/ppermute | solution.py:53
  30.4 0.9 %collective-permute-start.10 = (bf16[2112,128]{1,0:T(8,128)(2,1)S(1)}, bf16[2112,128]{1,0:T(8,128)(2,1)S(1)}, u32[]{:S(2)}, u32[]{:S(2)}) collective-permute-start(bf16[2112,128]{1,0:T(8,128)(2,1)S(1)} %join.2), channel_id=1, source_target_pairs={{0,1},{1,0},{2,3},{3,2},{4,5},{5,4},{6,7},{7,6},{8,9},{9,8},{10,11... | collective-permute-start | bytes 1622024 | tf_op jit(solution)/shard_map/ppermute | solution.py:57
  31.3 0.0 collective-permute-done.9
  31.3 0.0 collective-permute-start.11
  31.3 0.7 %pair.5.refs_5_ = f32[256,512]{1,0:T(8,128)S(1)} custom-call(bf16[2,528,128]{2,1,0:T(8,128)(2,1)S(1)} %bitcast.24, bf16[4,528,128]{2,1,0:T(8,128)(2,1)S(1)} %bitcast.14, bf16[4,528,128]{2,1,0:T(8,128)(2,1)S(1)} %bitcast.29), custom_call_target="tpu_custom_call" | custom-call | flops 536870912 | bytes 1310720 | tf_op jit(solution)/shard_map/pair/pallas_call | solution.py:135
  32.0 0.1 collective-permute-done.7
  32.1 1.1 %collective-permute-done.3 = bf16[2112,128]{1,0:T(8,128)(2,1)S(1)} collective-permute-done((bf16[2112,128]{1,0:T(8,128)(2,1)S(1)}, bf16[2112,128]{1,0:T(8,128)(2,1)S(1)}, u32[]{:S(2)}, u32[]{:S(2)}) %collective-permute-start.3) | collective-permute-done | bytes 540704 | tf_op jit(solution)/shard_map/ppermute | solution.py:45
  33.2 0.0 collective-permute-done.4
  33.2 0.8 %collective-permute-start.12 = (bf16[2112,128]{1,0:T(8,128)(2,1)S(1)}, bf16[2112,128]{1,0:T(8,128)(2,1)S(1)}, u32[]{:S(2)}, u32[]{:S(2)}) collective-permute-start(bf16[2112,128]{1,0:T(8,128)(2,1)S(1)} %collective-permute-done.3), channel_id=1, source_target_pairs={{0,1},{1,0},{2,3},{3,2},{4,5},{5,4},{6,7},{7,6},{8,9},{9,8},{10,11... | collective-permute-start | bytes 1622024 | tf_op jit(solution)/shard_map/ppermute | solution.py:57
  34.0 0.1 collective-permute-start.13
  34.1 0.0 collective-permute-done.10
  34.1 0.0 collective-permute-done.11
  34.1 1.3 %pair.8.refs_3_ = f32[256,512]{1,0:T(8,128)S(1)} custom-call(bf16[2,528,128]{2,1,0:T(8,128)(2,1)S(1)} %bitcast.25, bf16[4,528,128]{2,1,0:T(8,128)(2,1)S(1)} %bitcast.32, bf16[4,528,128]{2,1,0:T(8,128)(2,1)S(1)} %bitcast.35, bf16[4,528,128]{2,1,0:T(8,128)(2,1)S(1)} %bitcast.38, bf16[4,528,128]{2,1,0:T(8,128)(2,1)S(1)} %bitcast.41, f32[256,512]{1,0:T(8,128)S(1)} %pair.5.refs_5_), custom_call_target="tpu_custom_call" | custom-call | flops 1073741824 | bytes 2359296 | tf_op jit(solution)/shard_map/pair/pallas_call | solution.py:135
  35.4 0.2 collective-permute-done.12
  35.5 0.8 %collective-permute-done.13 = bf16[2112,128]{1,0:T(8,128)(2,1)S(1)} collective-permute-done((bf16[2112,128]{1,0:T(8,128)(2,1)S(1)}, bf16[2112,128]{1,0:T(8,128)(2,1)S(1)}, u32[]{:S(2)}, u32[]{:S(2)}) %collective-permute-start.13) | collective-permute-done | bytes 540704 | tf_op jit(solution)/shard_map/ppermute | solution.py:57
  36.3 0.8 %pair.9 = bf16[256,512]{1,0:T(8,128)(2,1)S(1)} custom-call(bf16[2,528,128]{2,1,0:T(8,128)(2,1)S(1)} %bitcast.26, bf16[4,528,128]{2,1,0:T(8,128)(2,1)S(1)} %bitcast.17, bf16[4,528,128]{2,1,0:T(8,128)(2,1)S(1)} %bitcast.20, f32[256,512]{1,0:T(8,128)S(1)} %pair.8.refs_3_), custom_call_target="tpu_custom_call" | custom-call | flops 536870912 | bytes 1310720 | tf_op jit(solution)/shard_map/pair/pallas_call | solution.py:135
  37.1 0.3 collective-permute-start.15
  37.4 4.6 %pair.6 = (f32[256,512]{1,0:T(8,128)S(1)}, f32[256,512]{1,0:T(8,128)S(1)}) custom-call(bf16[2,528,128]{2,1,0:T(8,128)(2,1)S(1)} %bitcast.45, bf16[2,528,128]{2,1,0:T(8,128)(2,1)S(1)} %bitcast.23, bf16[4,528,128]{2,1,0:T(8,128)(2,1)S(1)} %bitcast.15, bf16[4,528,128]{2,1,0:T(8,128)(2,1)S(1)} %bitcast.30, bf16[4,528,128]{2,1,0:T(8,128)(2,1)S(1)} %bitcast.33, ...), custom_call_target="tpu_custom_call" | custom-call | flops 4294967296 | bytes 4718592 | tf_op jit(solution)/shard_map/pair/pallas_call | solution.py:135
  42.0 0.9 %collective-permute-done.15 = bf16[256,512]{1,0:T(8,128)(2,1)S(1)} collective-permute-done((bf16[256,512]{1,0:T(8,128)(2,1)S(1)}, bf16[256,512]{1,0:T(8,128)(2,1)S(1)}, u32[]{:S(2)}, u32[]{:S(2)}) %collective-permute-start.15) | collective-permute-done | bytes 262176 | tf_op jit(solution)/shard_map/ppermute | solution.py:45
  42.9 0.1 add_convert_fusion.1
  43.0 3.3 %collective-permute-start.16 = (bf16[256,512]{1,0:T(8,128)(2,1)S(1)}, bf16[256,512]{1,0:T(8,128)(2,1)S(1)}, u32[]{:S(2)}, u32[]{:S(2)}) collective-permute-start(bf16[256,512]{1,0:T(8,128)(2,1)S(1)} %add_convert_fusion.1), channel_id=1, source_target_pairs={{0,8},{1,201},{8,0},{9,65},{64,72},{65,9},{72,64},{73,129},{128,13... | collective-permute-start | bytes 786440 | tf_op jit(solution)/shard_map/ppermute | solution.py:45
  46.3 0.1 collective-permute-start.14
  46.4 2.4 %pair.7 = f32[256,512]{1,0:T(8,128)S(1)} custom-call(bf16[2,528,128]{2,1,0:T(8,128)(2,1)S(1)} %bitcast.44, bf16[4,528,128]{2,1,0:T(8,128)(2,1)S(1)} %bitcast.16, bf16[4,528,128]{2,1,0:T(8,128)(2,1)S(1)} %bitcast.31, bf16[4,528,128]{2,1,0:T(8,128)(2,1)S(1)} %bitcast.34, bf16[4,528,128]{2,1,0:T(8,128)(2,1)S(1)} %bitcast.37, bf16[4,528,128]{2,1,0:T(8,128)(2,1)S(1)} %bitcast.40, ...), custom_call_target="tpu_custom_call" | custom-call | flops 2147483648 | bytes 4456448 | tf_op jit(solution)/shard_map/pair/pallas_call | solution.py:135
  48.8 1.2 %collective-permute-done.16 = bf16[256,512]{1,0:T(8,128)(2,1)S(1)} collective-permute-done((bf16[256,512]{1,0:T(8,128)(2,1)S(1)}, bf16[256,512]{1,0:T(8,128)(2,1)S(1)}, u32[]{:S(2)}, u32[]{:S(2)}) %collective-permute-start.16) | collective-permute-done | bytes 262176 | tf_op jit(solution)/shard_map/ppermute | solution.py:45
  50.0 0.1 add_convert_fusion
  50.1 0.2 collective-permute-start.17
  50.3 0.0 copy-start.1
  50.3 3.8 %collective-permute-start.18 = (bf16[128,512]{1,0:T(8,128)(2,1)S(1)}, bf16[128,512]{1,0:T(8,128)(2,1)S(1)}, u32[]{:S(2)}, u32[]{:S(2)}) collective-permute-start(bf16[128,512]{1,0:T(8,128)(2,1)S(1)} %get-tuple-element.17), channel_id=1, source_target_pairs={{0,200},{1,9},{8,64},{9,1},{64,8},{65,73},{72,128},{73,65},{128,72... | collective-permute-start | bytes 393224 | tf_op jit(solution)/shard_map/ppermute | solution.py:45
  54.1 0.0 collective-permute-done.14.refs_0_
  54.1 2.9 %collective-permute-done.17.refs_1_ = bf16[128,512]{1,0:T(8,128)(2,1)S(1)} collective-permute-done((bf16[128,512]{1,0:T(8,128)(2,1)S(1)}, bf16[128,512]{1,0:T(8,128)(2,1)S(1)}, u32[]{:S(2)}, u32[]{:S(2)}) %collective-permute-start.17) | collective-permute-done | bytes 131104 | tf_op jit(solution)/shard_map/ppermute | solution.py:53
  57.0 2.5 %collective-permute-done.18.refs_2_ = bf16[128,512]{1,0:T(8,128)(2,1)S(1)} collective-permute-done((bf16[128,512]{1,0:T(8,128)(2,1)S(1)}, bf16[128,512]{1,0:T(8,128)(2,1)S(1)}, u32[]{:S(2)}, u32[]{:S(2)}) %collective-permute-start.18) | collective-permute-done | bytes 131104 | tf_op jit(solution)/shard_map/ppermute | solution.py:45
  59.5 0.0 copy-done.1
  59.5 0.9 %final.1 = f32[128,512]{1,0:T(8,128)} custom-call(f32[128,512]{1,0:T(8,128)S(1)} %copy-done.1, f32[128,512]{1,0:T(8,128)S(1)} %slice.13.own, bf16[128,512]{1,0:T(8,128)(2,1)S(1)} %collective-permute-done.14.refs_0_, bf16[128,512]{1,0:T(8,128)(2,1)S(1)} %collective-permute-done.17.refs_1_, bf16[128,512]{1,0:T(8,128)(2,1)S(1)} %collective-permute-done.18.refs_2_), custom_call_target="tpu_custom_call" | custom-call | tf_op jit(solution)/shard_map/final/pallas_call | solution.py:205
  (6 shorter events, 0.1 us)
Async XLA Ops:
  0.0 0.9 %copy-start = (f32[128,512]{1,0:T(8,128)S(1)}, f32[128,512]{1,0:T(8,128)}, u32[]{:S(2)}) copy-start(f32[128,512]{1,0:T(8,128)} %emb.3) | copy-start | bytes 786436
  1.1 0.7 %copy-start.2 = (s32[128]{0:T(128)S(1)}, s32[128]{0:T(128)}, u32[]{:S(2)}) copy-start(s32[128]{0:T(128)} %param.4) | copy-start | bytes 1540
  1.1 0.7 %copy-start.3 = (s32[128]{0:T(128)S(1)}, s32[128]{0:T(128)}, u32[]{:S(2)}) copy-start(s32[128]{0:T(128)} %param.5) | copy-start | bytes 1540
  1.8 11.7 %collective-permute-start.5 = (bf16[528,128]{1,0:T(8,128)(2,1)S(1)}, bf16[528,128]{1,0:T(8,128)(2,1)S(1)}, u32[]{:S(2)}, u32[]{:S(2)}) collective-permute-start(bf16[528,128]{1,0:T(8,128)(2,1)S(1)} %pack.1.refs_3_.refs_0_), channel_id=1, source_target_pairs={{0,8},{1,201},{8,0},{9,65},{64,72},{65,9},{72,64},{73,129},{128,13... | collective-permute-start | bytes 405512 | tf_op jit(solution)/shard_map/ppermute | solution.py:45
  8.3 7.3 %collective-permute-start = (bf16[528,128]{1,0:T(8,128)(2,1)S(1)}, bf16[528,128]{1,0:T(8,128)(2,1)S(1)}, u32[]{:S(2)}, u32[]{:S(2)}) collective-permute-start(bf16[528,128]{1,0:T(8,128)(2,1)S(1)} %pack.1.refs_3_.refs_0_), channel_id=1, source_target_pairs={{0,18},{1,55},{8,26},{9,63},{64,82},{65,119},{72,90},{73,127},{128... | collective-permute-start | bytes 405512 | tf_op jit(solution)/shard_map/ppermute | solution.py:45
  13.2 5.2 %collective-permute-start.1 = (bf16[528,128]{1,0:T(8,128)(2,1)S(1)}, bf16[528,128]{1,0:T(8,128)(2,1)S(1)}, u32[]{:S(2)}, u32[]{:S(2)}) collective-permute-start(bf16[528,128]{1,0:T(8,128)(2,1)S(1)} %pack.1.refs_3_.refs_0_), channel_id=1, source_target_pairs={{0,16},{1,49},{8,24},{9,57},{64,80},{65,113},{72,88},{73,121},{128... | collective-permute-start | bytes 405512 | tf_op jit(solution)/shard_map/ppermute | solution.py:45
  13.4 5.1 %collective-permute-start.2 = (bf16[528,128]{1,0:T(8,128)(2,1)S(1)}, bf16[528,128]{1,0:T(8,128)(2,1)S(1)}, u32[]{:S(2)}, u32[]{:S(2)}) collective-permute-start(bf16[528,128]{1,0:T(8,128)(2,1)S(1)} %pack.1.refs_3_.refs_0_), channel_id=1, source_target_pairs={{0,2},{1,7},{8,10},{9,15},{64,66},{65,71},{72,74},{73,79},{128,130... | collective-permute-start | bytes 405512 | tf_op jit(solution)/shard_map/ppermute | solution.py:45
  13.5 7.7 %collective-permute-start.6 = (bf16[1056,128]{1,0:T(8,128)(2,1)S(1)}, bf16[1056,128]{1,0:T(8,128)(2,1)S(1)}, u32[]{:S(2)}, u32[]{:S(2)}) collective-permute-start(bf16[1056,128]{1,0:T(8,128)(2,1)S(1)} %join.3), channel_id=1, source_target_pairs={{0,200},{1,9},{8,64},{9,1},{64,8},{65,73},{72,128},{73,65},{128,72... | collective-permute-start | bytes 811016 | tf_op jit(solution)/shard_map/ppermute | solution.py:45
  18.5 12.8 %collective-permute-start.9 = (bf16[2112,128]{1,0:T(8,128)(2,1)S(1)}, bf16[2112,128]{1,0:T(8,128)(2,1)S(1)}, u32[]{:S(2)}, u32[]{:S(2)}) collective-permute-start(bf16[2112,128]{1,0:T(8,128)(2,1)S(1)} %join.2), channel_id=1, source_target_pairs={{0,48},{1,17},{8,56},{9,25},{64,112},{65,81},{72,120},{73,89},{128... | collective-permute-start | bytes 1622024 | tf_op jit(solution)/shard_map/ppermute | solution.py:45
  18.9 14.3 %collective-permute-start.3 = (bf16[2112,128]{1,0:T(8,128)(2,1)S(1)}, bf16[2112,128]{1,0:T(8,128)(2,1)S(1)}, u32[]{:S(2)}, u32[]{:S(2)}) collective-permute-start(bf16[2112,128]{1,0:T(8,128)(2,1)S(1)} %join.2), channel_id=1, source_target_pairs={{0,6},{1,3},{8,14},{9,11},{64,70},{65,67},{72,78},{73,75},{128,134... | collective-permute-start | bytes 1622024 | tf_op jit(solution)/shard_map/ppermute | solution.py:45
  18.9 14.3 %collective-permute-start.4 = (bf16[2112,128]{1,0:T(8,128)(2,1)S(1)}, bf16[2112,128]{1,0:T(8,128)(2,1)S(1)}, u32[]{:S(2)}, u32[]{:S(2)}) collective-permute-start(bf16[2112,128]{1,0:T(8,128)(2,1)S(1)} %join.2), channel_id=1, source_target_pairs={{0,54},{1,19},{8,62},{9,27},{64,118},{65,83},{72,126},{73,91},{128... | collective-permute-start | bytes 1622024 | tf_op jit(solution)/shard_map/ppermute | solution.py:45
  21.2 9.1 %collective-permute-start.8 = (bf16[1056,128]{1,0:T(8,128)(2,1)S(1)}, bf16[1056,128]{1,0:T(8,128)(2,1)S(1)}, u32[]{:S(2)}, u32[]{:S(2)}) collective-permute-start(bf16[1056,128]{1,0:T(8,128)(2,1)S(1)} %collective-permute-done.6), channel_id=1, source_target_pairs={{0,64},{1,193},{8,200},{9,73},{64,128},{65,1},{72,8},{73,137},{128... | collective-permute-start | bytes 811016 | tf_op jit(solution)/shard_map/ppermute | solution.py:53
  22.4 9.7 %collective-permute-start.7 = (bf16[1056,128]{1,0:T(8,128)(2,1)S(1)}, bf16[1056,128]{1,0:T(8,128)(2,1)S(1)}, u32[]{:S(2)}, u32[]{:S(2)}) collective-permute-start(bf16[1056,128]{1,0:T(8,128)(2,1)S(1)} %collective-permute-done.6), channel_id=1, source_target_pairs={{0,8},{1,201},{8,0},{9,65},{64,72},{65,9},{72,64},{73,129},{128,13... | collective-permute-start | bytes 811016 | tf_op jit(solution)/shard_map/ppermute | solution.py:45
  30.4 3.7 %collective-permute-start.10 = (bf16[2112,128]{1,0:T(8,128)(2,1)S(1)}, bf16[2112,128]{1,0:T(8,128)(2,1)S(1)}, u32[]{:S(2)}, u32[]{:S(2)}) collective-permute-start(bf16[2112,128]{1,0:T(8,128)(2,1)S(1)} %join.2), channel_id=1, source_target_pairs={{0,1},{1,0},{2,3},{3,2},{4,5},{5,4},{6,7},{7,6},{8,9},{9,8},{10,11... | collective-permute-start | bytes 1622024 | tf_op jit(solution)/shard_map/ppermute | solution.py:57
  31.3 2.8 %collective-permute-start.11 = (bf16[2112,128]{1,0:T(8,128)(2,1)S(1)}, bf16[2112,128]{1,0:T(8,128)(2,1)S(1)}, u32[]{:S(2)}, u32[]{:S(2)}) collective-permute-start(bf16[2112,128]{1,0:T(8,128)(2,1)S(1)} %collective-permute-done.9), channel_id=1, source_target_pairs={{0,1},{1,0},{2,3},{3,2},{4,5},{5,4},{6,7},{7,6},{8,9},{9,8},{10,11... | collective-permute-start | bytes 1622024 | tf_op jit(solution)/shard_map/ppermute | solution.py:57
  33.2 2.4 %collective-permute-start.12 = (bf16[2112,128]{1,0:T(8,128)(2,1)S(1)}, bf16[2112,128]{1,0:T(8,128)(2,1)S(1)}, u32[]{:S(2)}, u32[]{:S(2)}) collective-permute-start(bf16[2112,128]{1,0:T(8,128)(2,1)S(1)} %collective-permute-done.3), channel_id=1, source_target_pairs={{0,1},{1,0},{2,3},{3,2},{4,5},{5,4},{6,7},{7,6},{8,9},{9,8},{10,11... | collective-permute-start | bytes 1622024 | tf_op jit(solution)/shard_map/ppermute | solution.py:57
  34.0 2.3 %collective-permute-start.13 = (bf16[2112,128]{1,0:T(8,128)(2,1)S(1)}, bf16[2112,128]{1,0:T(8,128)(2,1)S(1)}, u32[]{:S(2)}, u32[]{:S(2)}) collective-permute-start(bf16[2112,128]{1,0:T(8,128)(2,1)S(1)} %collective-permute-done.4), channel_id=1, source_target_pairs={{0,1},{1,0},{2,3},{3,2},{4,5},{5,4},{6,7},{7,6},{8,9},{9,8},{10,11... | collective-permute-start | bytes 1622024 | tf_op jit(solution)/shard_map/ppermute | solution.py:57
  37.1 5.8 %collective-permute-start.15 = (bf16[256,512]{1,0:T(8,128)(2,1)S(1)}, bf16[256,512]{1,0:T(8,128)(2,1)S(1)}, u32[]{:S(2)}, u32[]{:S(2)}) collective-permute-start(bf16[256,512]{1,0:T(8,128)(2,1)S(1)} %pair.9), channel_id=1, source_target_pairs={{0,200},{1,9},{8,64},{9,1},{64,8},{65,73},{72,128},{73,65},{128,72... | collective-permute-start | bytes 786440 | tf_op jit(solution)/shard_map/ppermute | solution.py:45
  43.0 7.1 %collective-permute-start.16 = (bf16[256,512]{1,0:T(8,128)(2,1)S(1)}, bf16[256,512]{1,0:T(8,128)(2,1)S(1)}, u32[]{:S(2)}, u32[]{:S(2)}) collective-permute-start(bf16[256,512]{1,0:T(8,128)(2,1)S(1)} %add_convert_fusion.1), channel_id=1, source_target_pairs={{0,8},{1,201},{8,0},{9,65},{64,72},{65,9},{72,64},{73,129},{128,13... | collective-permute-start | bytes 786440 | tf_op jit(solution)/shard_map/ppermute | solution.py:45
  46.3 7.8 %collective-permute-start.14 = (bf16[128,512]{1,0:T(8,128)(2,1)S(1)}, bf16[128,512]{1,0:T(8,128)(2,1)S(1)}, u32[]{:S(2)}, u32[]{:S(2)}) collective-permute-start(bf16[128,512]{1,0:T(8,128)(2,1)S(1)} %slice.21), channel_id=1, source_target_pairs={{0,8},{1,201},{8,0},{9,65},{64,72},{65,9},{72,64},{73,129},{128,13... | collective-permute-start | bytes 393224 | tf_op jit(solution)/shard_map/ppermute | solution.py:45
  50.1 6.8 %collective-permute-start.17 = (bf16[128,512]{1,0:T(8,128)(2,1)S(1)}, bf16[128,512]{1,0:T(8,128)(2,1)S(1)}, u32[]{:S(2)}, u32[]{:S(2)}) collective-permute-start(bf16[128,512]{1,0:T(8,128)(2,1)S(1)} %get-tuple-element.18), channel_id=1, source_target_pairs={{0,192},{1,65},{8,72},{9,201},{64,0},{65,129},{72,136},{73,9},{128... | collective-permute-start | bytes 393224 | tf_op jit(solution)/shard_map/ppermute | solution.py:53
  50.3 9.2 %copy-start.1 = (f32[128,512]{1,0:T(8,128)S(1)}, f32[128,512]{1,0:T(8,128)}, u32[]{:S(2)}) copy-start(f32[128,512]{1,0:T(8,128)} %emb.3) | copy-start | bytes 786436
  50.3 9.2 %collective-permute-start.18 = (bf16[128,512]{1,0:T(8,128)(2,1)S(1)}, bf16[128,512]{1,0:T(8,128)(2,1)S(1)}, u32[]{:S(2)}, u32[]{:S(2)}) collective-permute-start(bf16[128,512]{1,0:T(8,128)(2,1)S(1)} %get-tuple-element.17), channel_id=1, source_target_pairs={{0,200},{1,9},{8,64},{9,1},{64,8},{65,73},{72,128},{73,65},{128,72... | collective-permute-start | bytes 393224 | tf_op jit(solution)/shard_map/ppermute | solution.py:45

commit v8 on v7

--- a/solution.py
+++ b/solution.py
@@ -16,7 +16,7 @@
 META = 16
 LANES = 128
 CHUNKS = D // LANES
-PACKED = CHUNKS * CPD + META
+UNITS = CHUNKS * CPD
 SMALL = 6 << 20
 AXES = ("row", "col")
 VMEM = pl.BlockSpec(memory_space=pltpu.VMEM)
@@ -67,15 +67,15 @@
 def pack_kernel(unit, margin, group, whole):
     row = lax.broadcasted_iota(jnp.int32, (META, LANES), 0)
     meta = jnp.where(row == 0, margin[...], jnp.where(row == 1, group[...], 0)).astype(F32).astype(BF)
-    whole[: CHUNKS * CPD, :] = unit[...]
-    whole[CHUNKS * CPD :, :] = meta
+    whole[:UNITS, :] = unit[...]
+    whole[UNITS:, :] = meta
 
 
 def pack(embeddings, margin, group):
     params = pltpu.CompilerParams(vmem_limit_bytes=SMALL)
     unit = pl.pallas_call(
         units_kernel,
-        out_shape=jax.ShapeDtypeStruct((CHUNKS * CPD, LANES), BF),
+        out_shape=jax.ShapeDtypeStruct((UNITS, LANES), BF),
         in_specs=[VMEM],
         out_specs=VMEM,
         compiler_params=params,
@@ -83,7 +83,7 @@
     )(embeddings)
     return pl.pallas_call(
         pack_kernel,
-        out_shape=jax.ShapeDtypeStruct((PACKED, LANES), BF),
+        out_shape=jax.ShapeDtypeStruct((UNITS + META, LANES), BF),
         in_specs=[VMEM] * 3,
         out_specs=VMEM,
         compiler_params=params,
@@ -95,33 +95,43 @@
 
 
 def units(ref, k):
-    return jnp.concatenate([ref[k, f * CPD : (f + 1) * CPD, :] for f in range(CHUNKS)], axis=1)
+    at = k * UNITS
+    return jnp.concatenate([ref[at + f * CPD : at + (f + 1) * CPD, :] for f in range(CHUNKS)], axis=1)
+
+
+def marks(ref, k):
+    meta = ref[ref.shape[0] - META :, :].astype(F32)
+    return meta[2 * k : 2 * k + 1], meta[2 * k + 1 : 2 * k + 2]
+
+
+def blocks(ref):
+    return (ref.shape[0] - META) // UNITS
 
 
 def pair_kernel(n_r, n_c, n_sum, *refs):
     r_in, c_in, rest = refs[:n_r], refs[n_r : n_r + n_c], refs[n_r + n_c :]
     sums, outs = rest[:n_sum], rest[n_sum:]
-    r_blocks, c_blocks = ([(ref, k) for ref in v for k in range(ref.shape[0])] for v in (r_in, c_in))
+    r_blocks, c_blocks = ([(ref, k) for ref in v for k in range(blocks(ref))] for v in (r_in, c_in))
     acc, r_margin, r_group = [], [], []
     for i in range(0, len(r_blocks), 2):
-        meta = [ref[k, CHUNKS * CPD :, :].astype(F32) for ref, k in r_blocks[i : i + 2]]
-        r_margin.append(jnp.concatenate([jnp.broadcast_to(m[0:1] * 0.0005, (CPD, CPD)).T for m in meta], axis=0))
-        r_group.append(jnp.concatenate([jnp.broadcast_to(m[1:2], (CPD, CPD)).T for m in meta], axis=0))
+        meta = [marks(ref, k) for ref, k in r_blocks[i : i + 2]]
+        r_margin.append(jnp.concatenate([jnp.broadcast_to(m * 0.0005, (CPD, CPD)).T for m, _ in meta], axis=0))
+        r_group.append(jnp.concatenate([jnp.broadcast_to(g, (CPD, CPD)).T for _, g in meta], axis=0))
         acc.append(None)
     halves = [(ref, o) for ref in sums for o in range(0, ref.shape[0], 2 * CPD)]
     for i, (ref, o) in enumerate(halves):
         acc[i] = ref[o : o + 2 * CPD, :]
     for t in range(0, len(c_blocks), TB):
         tile = c_blocks[t : t + TB]
-        meta = [ref[k, CHUNKS * CPD :, :].astype(F32) for ref, k in tile]
+        meta = [marks(ref, k) for ref, k in tile]
         ct = jnp.concatenate([units(ref, k) for ref, k in tile], axis=0)
         for i in range(len(acc)):
             rt = jnp.concatenate([units(ref, k) for ref, k in r_blocks[2 * i : 2 * i + 2]], axis=0)
             cos = lax.dot_general(rt, ct, (((1,), (1,)), ((), ())), preferred_element_type=F32)
             parts = []
-            for k, m in enumerate(meta):
-                over = jnp.maximum(cos[:, k * LANES : (k + 1) * LANES] - r_margin[i] - m[0:1] * 0.0005, 0.0)
-                parts.append(jnp.where(r_group[i] != m[1:2], over, 0.0).astype(BF))
+            for k, (m, g) in enumerate(meta):
+                over = jnp.maximum(cos[:, k * LANES : (k + 1) * LANES] - r_margin[i] - m * 0.0005, 0.0)
+                parts.append(jnp.where(r_group[i] != g, over, 0.0).astype(BF))
             part = jnp.dot(jnp.concatenate(parts, axis=1), ct, preferred_element_type=F32)
             acc[i] = part if acc[i] is None else acc[i] + part
     halves = [(ref, o) for ref in outs for o in range(0, ref.shape[0], 2 * CPD)]
@@ -130,11 +140,10 @@
 
 
 def pair(r_in, c_in, out_dtype, sums=()):
-    r_in, c_in = ([a.reshape(-1, PACKED, LANES) for a in v] for v in (r_in, c_in))
-    rows, cols = (sum(a.shape[0] for a in v) * CPD for v in (r_in, c_in))
+    rows, cols = (sum(blocks(a) for a in v) * CPD for v in (r_in, c_in))
     return pl.pallas_call(
         functools.partial(pair_kernel, len(r_in), len(c_in), len(sums)),
-        out_shape=[jax.ShapeDtypeStruct((a.shape[0] * CPD, D), out_dtype) for a in r_in],
+        out_shape=[jax.ShapeDtypeStruct((blocks(a) * CPD, D), out_dtype) for a in r_in],
         in_specs=[VMEM] * (len(r_in) + len(c_in) + len(sums)),
         out_specs=[VMEM] * len(r_in),
         compiler_params=pltpu.CompilerParams(vmem_limit_bytes=20 << 20),
@@ -147,17 +156,19 @@
 
 def join_kernel(*refs):
     ins, out = refs[:-1], refs[-1]
-    at = 0
-    for ref in ins:
-        n = ref.shape[0]
-        out[at : at + n, :] = ref[...]
-        at += n
+    row = lax.broadcasted_iota(jnp.int32, (META, LANES), 0)
+    meta = jnp.zeros((META, LANES), F32)
+    for i, ref in enumerate(ins):
+        out[i * UNITS : (i + 1) * UNITS, :] = ref[:UNITS, :]
+        margin, group = marks(ref, 0)
+        meta = jnp.where(row == 2 * i, margin, jnp.where(row == 2 * i + 1, group, meta))
+    out[len(ins) * UNITS :, :] = meta.astype(BF)
 
 
 def join(*ins):
     return pl.pallas_call(
         join_kernel,
-        out_shape=jax.ShapeDtypeStruct((sum(a.shape[0] for a in ins), LANES), BF),
+        out_shape=jax.ShapeDtypeStruct((len(ins) * UNITS + META, LANES), BF),
         in_specs=[VMEM] * len(ins),
         out_specs=VMEM,
         compiler_params=pltpu.CompilerParams(vmem_limit_bytes=SMALL),
@@ -194,10 +205,10 @@
     (p_far,) = pair([far], [c2, c3, e0, e1], F32, [p_far])
     (p_far,) = pair([far], [e2, e3], BF, [p_far])
     q = swap(p_far, "zb", "za")
-    p_ahead, p_own = pair([ahead, both], cols, F32)
+    p_ahead, p_back = pair([ahead, back], cols, F32)
+    q = swap((p_ahead + q).astype(BF), "za", "zb")
+    (p_own,) = pair([both], cols, F32)
     q_near = swap(p_own[CPD:].astype(BF), "za", "zb")
-    q = swap((p_ahead + q).astype(BF), "za", "zb")
-    (p_back,) = pair([back], cols, F32)
     p_back = (p_back + q).astype(BF)
     arrived = (q_near, shift(p_back[CPD:], -1), swap(p_back[:CPD], "zb", "za"))
 

time: 60.6 us -> 60.3 us (level)
    ppermute x2, waiting for transfers between devices: 10.8 us -> 6.16 us  [shift(): return lax.ppermute(block, AXES, pairs)]
    ppermute x13, waiting for transfers between devices: 10.7 us -> 15 us  [swap(): return lax.ppermute(block, AXES, pairs)]
where the time goes in v8:
time: 60.3 us; the launch traced here: 60.2 us
  starting transfers between devices  25.1 us (42%)
  waiting for transfers between devices  22.1 us (37%)
  Pallas kernels  11 us (18%)
  local copies, waits for them, and re-layouts  1.67 us (3%)
    ppermute x13, starting transfers between devices, swap(): return lax.ppermute(block, AXES, pairs)  21.9 us
    ppermute x13, waiting for transfers between devices, swap(): return lax.ppermute(block, AXES, pairs)  15 us
    pallas_call x5, Pallas kernels, pair(): pl.pallas_call(functools.partial(pair_kernel, len(r_in), len(c_in), len(s...  9.88 us
    ppermute x2, waiting for transfers between devices, shift(): return lax.ppermute(block, AXES, pairs)  6.16 us
    ppermute x4, starting transfers between devices, swap_cores(): return lax.ppermute(block, AXES, [(i, i ^ 1) for i in range(256)])  1.83 us
    unnamed x8, local copies, waits for them, and re-layouts  1.61 us
    ppermute x2, starting transfers between devices, shift(): return lax.ppermute(block, AXES, pairs)  1.33 us
  transfers between devices with their start and end apart: 19, of which 12 were waited for; matrix products, arithmetic and copies ran while one was open for 0% of the time, Pallas kernels for 15%

profile of v8, /device:TPU:1, one launch (start us, length us, event | category | flops | bytes accessed | tf_op | source)
XLA Modules:
  0.0 60.2 jit_solution(12994560388096904214)
XLA Ops:
  0.0 0.0 copy-start
  0.0 0.9 %copy-done = f32[128,512]{1,0:T(8,128)S(1)} copy-done((f32[128,512]{1,0:T(8,128)S(1)}, f32[128,512]{1,0:T(8,128)}, u32[]{:S(2)}) %copy-start) | copy-done | bytes 262168
  1.0 0.1 units.1.unit
  1.1 0.0 copy-start.2
  1.1 0.0 copy-start.3
  1.1 0.6 %copy-done.2 = s32[128]{0:T(128)S(1)} copy-done((s32[128]{0:T(128)S(1)}, s32[128]{0:T(128)}, u32[]{:S(2)}) %copy-start.2) | copy-done | bytes 536
  1.7 0.0 copy-done.3
  1.8 6.5 %collective-permute-start = (bf16[528,128]{1,0:T(8,128)(2,1)S(1)}, bf16[528,128]{1,0:T(8,128)(2,1)S(1)}, u32[]{:S(2)}, u32[]{:S(2)}) collective-permute-start(bf16[528,128]{1,0:T(8,128)(2,1)S(1)} %pack.1.refs_0_.refs_3_), channel_id=1, source_target_pairs={{0,8},{1,201},{8,0},{9,65},{64,72},{65,9},{72,64},{73,129},{128,13... | collective-permute-start | bytes 405512 | tf_op jit(solution)/shard_map/ppermute | solution.py:45
  8.3 4.9 %collective-permute-start.1 = (bf16[528,128]{1,0:T(8,128)(2,1)S(1)}, bf16[528,128]{1,0:T(8,128)(2,1)S(1)}, u32[]{:S(2)}, u32[]{:S(2)}) collective-permute-start(bf16[528,128]{1,0:T(8,128)(2,1)S(1)} %pack.1.refs_0_.refs_3_), channel_id=1, source_target_pairs={{0,18},{1,55},{8,26},{9,63},{64,82},{65,119},{72,90},{73,127},{128... | collective-permute-start | bytes 405512 | tf_op jit(solution)/shard_map/ppermute | solution.py:45
  13.2 0.2 collective-permute-start.2
  13.4 0.1 collective-permute-start.3
  13.5 0.0 collective-permute-done.refs_1_
  13.5 0.1 collective-permute-start.7
  13.6 2.0 %collective-permute-done.1.refs_0_ = bf16[528,128]{1,0:T(8,128)(2,1)S(1)} collective-permute-done((bf16[528,128]{1,0:T(8,128)(2,1)S(1)}, bf16[528,128]{1,0:T(8,128)(2,1)S(1)}, u32[]{:S(2)}, u32[]{:S(2)}) %collective-permute-start.1) | collective-permute-done | bytes 135200 | tf_op jit(solution)/shard_map/ppermute | solution.py:45
  15.6 2.8 %collective-permute-done.2.refs_1_ = bf16[528,128]{1,0:T(8,128)(2,1)S(1)} collective-permute-done((bf16[528,128]{1,0:T(8,128)(2,1)S(1)}, bf16[528,128]{1,0:T(8,128)(2,1)S(1)}, u32[]{:S(2)}, u32[]{:S(2)}) %collective-permute-start.2) | collective-permute-done | bytes 135200 | tf_op jit(solution)/shard_map/ppermute | solution.py:45
  18.3 0.1 collective-permute-done.3.refs_2_
  18.5 0.4 collective-permute-start.4
  18.9 0.0 collective-permute-start.5
  18.9 2.4 %collective-permute-start.6 = (bf16[2064,128]{1,0:T(8,128)(2,1)S(1)}, bf16[2064,128]{1,0:T(8,128)(2,1)S(1)}, u32[]{:S(2)}, u32[]{:S(2)}) collective-permute-start(bf16[2064,128]{1,0:T(8,128)(2,1)S(1)} %join.3.refs_1_.refs_2_), channel_id=1, source_target_pairs={{0,54},{1,19},{8,62},{9,27},{64,118},{65,83},{72,126},{73,91},{128... | collective-permute-start | bytes 1585160 | tf_op jit(solution)/shard_map/ppermute | solution.py:45
  21.2 0.0 collective-permute-done.7.refs_1_
  21.2 1.2 %collective-permute-start.9 = (bf16[1040,128]{1,0:T(8,128)(2,1)S(1)}, bf16[1040,128]{1,0:T(8,128)(2,1)S(1)}, u32[]{:S(2)}, u32[]{:S(2)}) collective-permute-start(bf16[1040,128]{1,0:T(8,128)(2,1)S(1)} %collective-permute-done.7.refs_1_), channel_id=1, source_target_pairs={{0,64},{1,193},{8,200},{9,73},{64,128},{65,1},{72,8},{73,137},{128... | collective-permute-start | bytes 798728 | tf_op jit(solution)/shard_map/ppermute | solution.py:53
  22.4 0.0 collective-permute-start.8
  22.4 4.5 %collective-permute-done.4.refs_2_.refs_3_ = bf16[2064,128]{1,0:T(8,128)(2,1)S(1)} collective-permute-done((bf16[2064,128]{1,0:T(8,128)(2,1)S(1)}, bf16[2064,128]{1,0:T(8,128)(2,1)S(1)}, u32[]{:S(2)}, u32[]{:S(2)}) %collective-permute-start.4) | collective-permute-done | bytes 528416 | tf_op jit(solution)/shard_map/ppermute | solution.py:45
  27.0 0.0 collective-permute-start.10
  27.0 3.3 %collective-permute-done.9.refs_0_ = bf16[1040,128]{1,0:T(8,128)(2,1)S(1)} collective-permute-done((bf16[1040,128]{1,0:T(8,128)(2,1)S(1)}, bf16[1040,128]{1,0:T(8,128)(2,1)S(1)}, u32[]{:S(2)}, u32[]{:S(2)}) %collective-permute-start.9) | collective-permute-done | bytes 266272 | tf_op jit(solution)/shard_map/ppermute | solution.py:53
  30.3 0.9 %collective-permute-start.11 = (bf16[2064,128]{1,0:T(8,128)(2,1)S(1)}, bf16[2064,128]{1,0:T(8,128)(2,1)S(1)}, u32[]{:S(2)}, u32[]{:S(2)}) collective-permute-start(bf16[2064,128]{1,0:T(8,128)(2,1)S(1)} %collective-permute-done.4.refs_2_.refs_3_), channel_id=1, source_target_pairs={{0,1},{1,0},{2,3},{3,2},{4,5},{5,4},{6,7},{7,6},{8,9},{9,8},{10,11... | collective-permute-start | bytes 1585160 | tf_op jit(solution)/shard_map/ppermute | solution.py:57
  31.2 0.8 %pair.5.refs_5_ = f32[256,512]{1,0:T(8,128)S(1)} custom-call(bf16[1040,128]{1,0:T(8,128)(2,1)S(1)} %collective-permute-done.9.refs_0_, bf16[2064,128]{1,0:T(8,128)(2,1)S(1)} %join.3.refs_1_.refs_2_, bf16[2064,128]{1,0:T(8,128)(2,1)S(1)} %collective-permute-done.4.refs_2_.refs_3_), custom_call_target="tpu_custom_call" | custom-call | flops 536870912 | bytes 1310720 | tf_op jit(solution)/shard_map/pair/pallas_call | solution.py:144
  31.9 1.0 %collective-permute-done.5.refs_3_.refs_4_.refs_1_ = bf16[2064,128]{1,0:T(8,128)(2,1)S(1)} collective-permute-done((bf16[2064,128]{1,0:T(8,128)(2,1)S(1)}, bf16[2064,128]{1,0:T(8,128)(2,1)S(1)}, u32[]{:S(2)}, u32[]{:S(2)}) %collective-permute-start.5) | collective-permute-done | bytes 528416 | tf_op jit(solution)/shard_map/ppermute | solution.py:45
  32.9 0.0 collective-permute-done.6.refs_4_.refs_5_.refs_2_
  32.9 0.0 collective-permute-done.8.refs_0_
  32.9 0.9 %collective-permute-start.12 = (bf16[2064,128]{1,0:T(8,128)(2,1)S(1)}, bf16[2064,128]{1,0:T(8,128)(2,1)S(1)}, u32[]{:S(2)}, u32[]{:S(2)}) collective-permute-start(bf16[2064,128]{1,0:T(8,128)(2,1)S(1)} %collective-permute-done.5.refs_3_.refs_4_.refs_1_), channel_id=1, source_target_pairs={{0,1},{1,0},{2,3},{3,2},{4,5},{5,4},{6,7},{7,6},{8,9},{9,8},{10,11... | collective-permute-start | bytes 1585160 | tf_op jit(solution)/shard_map/ppermute | solution.py:57
  33.9 0.0 collective-permute-start.13
  33.9 0.0 collective-permute-done.10.refs_5_.refs_6_.refs_3_
  33.9 0.0 collective-permute-done.11.refs_6_.refs_7_.refs_4_
  33.9 1.3 %pair.8.refs_3_ = f32[256,512]{1,0:T(8,128)S(1)} custom-call(bf16[1040,128]{1,0:T(8,128)(2,1)S(1)} %collective-permute-done.9.refs_0_, bf16[2064,128]{1,0:T(8,128)(2,1)S(1)} %collective-permute-done.5.refs_3_.refs_4_.refs_1_, bf16[2064,128]{1,0:T(8,128)(2,1)S(1)} %collective-permute-done.6.refs_4_.refs_5_.refs_2_, ...), custom_call_target="tpu_custom_call" | custom-call | flops 1073741824 | bytes 2359296 | tf_op jit(solution)/shard_map/pair/pallas_call | solution.py:144
  35.2 0.2 collective-permute-done.12.refs_7_.refs_8_.refs_1_
  35.4 0.8 %collective-permute-done.13.refs_8_.refs_9_.refs_2_ = bf16[2064,128]{1,0:T(8,128)(2,1)S(1)} collective-permute-done((bf16[2064,128]{1,0:T(8,128)(2,1)S(1)}, bf16[2064,128]{1,0:T(8,128)(2,1)S(1)}, u32[]{:S(2)}, u32[]{:S(2)}) %collective-permute-start.13) | collective-permute-done | bytes 528416 | tf_op jit(solution)/shard_map/ppermute | solution.py:57
  36.2 0.8 %pair.9 = bf16[256,512]{1,0:T(8,128)(2,1)S(1)} custom-call(bf16[1040,128]{1,0:T(8,128)(2,1)S(1)} %collective-permute-done.9.refs_0_, bf16[2064,128]{1,0:T(8,128)(2,1)S(1)} %collective-permute-done.12.refs_7_.refs_8_.refs_1_, bf16[2064,128]{1,0:T(8,128)(2,1)S(1)} %collective-permute-done.13.refs_8_.refs_9_.refs_2_, f32[256,512]{1,0:T(8,128)S(1)} %pair.8.refs_3_), custom_call_target="tpu_custom_call" | custom-call | flops 536870912 | bytes 1310720 | tf_op jit(solution)/shard_map/pair/pallas_call | solution.py:144
  36.9 0.3 collective-permute-start.15
  37.2 4.6 %pair.7 = (f32[256,512]{1,0:T(8,128)S(1)}, f32[256,512]{1,0:T(8,128)S(1)}) custom-call(bf16[1040,128]{1,0:T(8,128)(2,1)S(1)} %collective-permute-done.8.refs_0_, bf16[1040,128]{1,0:T(8,128)(2,1)S(1)} %collective-permute-done.7.refs_1_, bf16[2064,128]{1,0:T(8,128)(2,1)S(1)} %join.3.refs_1_.refs_2_, ...), custom_call_target="tpu_custom_call" | custom-call | flops 4294967296 | bytes 4718592 | tf_op jit(solution)/shard_map/pair/pallas_call | solution.py:144
  41.8 0.9 %collective-permute-done.15 = bf16[256,512]{1,0:T(8,128)(2,1)S(1)} collective-permute-done((bf16[256,512]{1,0:T(8,128)(2,1)S(1)}, bf16[256,512]{1,0:T(8,128)(2,1)S(1)}, u32[]{:S(2)}, u32[]{:S(2)}) %collective-permute-start.15) | collective-permute-done | bytes 262176 | tf_op jit(solution)/shard_map/ppermute | solution.py:45
  42.7 0.1 add_convert_fusion.1
  42.8 3.2 %collective-permute-start.16 = (bf16[256,512]{1,0:T(8,128)(2,1)S(1)}, bf16[256,512]{1,0:T(8,128)(2,1)S(1)}, u32[]{:S(2)}, u32[]{:S(2)}) collective-permute-start(bf16[256,512]{1,0:T(8,128)(2,1)S(1)} %add_convert_fusion.1), channel_id=1, source_target_pairs={{0,8},{1,201},{8,0},{9,65},{64,72},{65,9},{72,64},{73,129},{128,13... | collective-permute-start | bytes 786440 | tf_op jit(solution)/shard_map/ppermute | solution.py:45
  46.0 2.4 %pair.6 = f32[256,512]{1,0:T(8,128)S(1)} custom-call(bf16[1040,128]{1,0:T(8,128)(2,1)S(1)} %join.2.refs_0_, bf16[2064,128]{1,0:T(8,128)(2,1)S(1)} %join.3.refs_1_.refs_2_, bf16[2064,128]{1,0:T(8,128)(2,1)S(1)} %collective-permute-done.4.refs_2_.refs_3_, bf16[2064,128]{1,0:T(8,128)(2,1)S(1)} %collective-permute-done.5.refs_3_.refs_4_.refs_1_, ...), custom_call_target="tpu_custom_call" | custom-call | flops 2147483648 | bytes 4456448 | tf_op jit(solution)/shard_map/pair/pallas_call | solution.py:144
  48.5 0.1 collective-permute-start.14
  48.6 1.2 %collective-permute-done.16 = bf16[256,512]{1,0:T(8,128)(2,1)S(1)} collective-permute-done((bf16[256,512]{1,0:T(8,128)(2,1)S(1)}, bf16[256,512]{1,0:T(8,128)(2,1)S(1)}, u32[]{:S(2)}, u32[]{:S(2)}) %collective-permute-start.16) | collective-permute-done | bytes 262176 | tf_op jit(solution)/shard_map/ppermute | solution.py:45
  49.8 0.1 add_convert_fusion
  49.9 0.2 collective-permute-start.17
  50.0 0.0 copy-start.1
  50.0 3.8 %collective-permute-start.18 = (bf16[128,512]{1,0:T(8,128)(2,1)S(1)}, bf16[128,512]{1,0:T(8,128)(2,1)S(1)}, u32[]{:S(2)}, u32[]{:S(2)}) collective-permute-start(bf16[128,512]{1,0:T(8,128)(2,1)S(1)} %get-tuple-element.17), channel_id=1, source_target_pairs={{0,200},{1,9},{8,64},{9,1},{64,8},{65,73},{72,128},{73,65},{128,72... | collective-permute-start | bytes 393224 | tf_op jit(solution)/shard_map/ppermute | solution.py:45
  53.8 0.0 collective-permute-done.14.refs_0_
  53.8 2.9 %collective-permute-done.17.refs_1_ = bf16[128,512]{1,0:T(8,128)(2,1)S(1)} collective-permute-done((bf16[128,512]{1,0:T(8,128)(2,1)S(1)}, bf16[128,512]{1,0:T(8,128)(2,1)S(1)}, u32[]{:S(2)}, u32[]{:S(2)}) %collective-permute-start.17) | collective-permute-done | bytes 131104 | tf_op jit(solution)/shard_map/ppermute | solution.py:53
  56.7 2.6 %collective-permute-done.18.refs_2_ = bf16[128,512]{1,0:T(8,128)(2,1)S(1)} collective-permute-done((bf16[128,512]{1,0:T(8,128)(2,1)S(1)}, bf16[128,512]{1,0:T(8,128)(2,1)S(1)}, u32[]{:S(2)}, u32[]{:S(2)}) %collective-permute-start.18) | collective-permute-done | bytes 131104 | tf_op jit(solution)/shard_map/ppermute | solution.py:45
  59.3 0.0 copy-done.1
  59.3 0.9 %final.1 = f32[128,512]{1,0:T(8,128)} custom-call(f32[128,512]{1,0:T(8,128)S(1)} %copy-done.1, f32[128,512]{1,0:T(8,128)S(1)} %slice.17.own, bf16[128,512]{1,0:T(8,128)(2,1)S(1)} %collective-permute-done.14.refs_0_, bf16[128,512]{1,0:T(8,128)(2,1)S(1)} %collective-permute-done.17.refs_1_, bf16[128,512]{1,0:T(8,128)(2,1)S(1)} %collective-permute-done.18.refs_2_), custom_call_target="tpu_custom_call" | custom-call | tf_op jit(solution)/shard_map/final/pallas_call | solution.py:216
  (6 shorter events, 0.1 us)
Async XLA Ops:
  0.0 0.9 %copy-start = (f32[128,512]{1,0:T(8,128)S(1)}, f32[128,512]{1,0:T(8,128)}, u32[]{:S(2)}) copy-start(f32[128,512]{1,0:T(8,128)} %emb.3) | copy-start | bytes 786436
  1.1 0.7 %copy-start.2 = (s32[128]{0:T(128)S(1)}, s32[128]{0:T(128)}, u32[]{:S(2)}) copy-start(s32[128]{0:T(128)} %param.4) | copy-start | bytes 1540
  1.1 0.7 %copy-start.3 = (s32[128]{0:T(128)S(1)}, s32[128]{0:T(128)}, u32[]{:S(2)}) copy-start(s32[128]{0:T(128)} %param.5) | copy-start | bytes 1540
  1.8 11.7 %collective-permute-start = (bf16[528,128]{1,0:T(8,128)(2,1)S(1)}, bf16[528,128]{1,0:T(8,128)(2,1)S(1)}, u32[]{:S(2)}, u32[]{:S(2)}) collective-permute-start(bf16[528,128]{1,0:T(8,128)(2,1)S(1)} %pack.1.refs_0_.refs_3_), channel_id=1, source_target_pairs={{0,8},{1,201},{8,0},{9,65},{64,72},{65,9},{72,64},{73,129},{128,13... | collective-permute-start | bytes 405512 | tf_op jit(solution)/shard_map/ppermute | solution.py:45
  8.3 7.3 %collective-permute-start.1 = (bf16[528,128]{1,0:T(8,128)(2,1)S(1)}, bf16[528,128]{1,0:T(8,128)(2,1)S(1)}, u32[]{:S(2)}, u32[]{:S(2)}) collective-permute-start(bf16[528,128]{1,0:T(8,128)(2,1)S(1)} %pack.1.refs_0_.refs_3_), channel_id=1, source_target_pairs={{0,18},{1,55},{8,26},{9,63},{64,82},{65,119},{72,90},{73,127},{128... | collective-permute-start | bytes 405512 | tf_op jit(solution)/shard_map/ppermute | solution.py:45
  13.2 5.2 %collective-permute-start.2 = (bf16[528,128]{1,0:T(8,128)(2,1)S(1)}, bf16[528,128]{1,0:T(8,128)(2,1)S(1)}, u32[]{:S(2)}, u32[]{:S(2)}) collective-permute-start(bf16[528,128]{1,0:T(8,128)(2,1)S(1)} %pack.1.refs_0_.refs_3_), channel_id=1, source_target_pairs={{0,16},{1,49},{8,24},{9,57},{64,80},{65,113},{72,88},{73,121},{128... | collective-permute-start | bytes 405512 | tf_op jit(solution)/shard_map/ppermute | solution.py:45
  13.4 5.1 %collective-permute-start.3 = (bf16[528,128]{1,0:T(8,128)(2,1)S(1)}, bf16[528,128]{1,0:T(8,128)(2,1)S(1)}, u32[]{:S(2)}, u32[]{:S(2)}) collective-permute-start(bf16[528,128]{1,0:T(8,128)(2,1)S(1)} %pack.1.refs_0_.refs_3_), channel_id=1, source_target_pairs={{0,2},{1,7},{8,10},{9,15},{64,66},{65,71},{72,74},{73,79},{128,130... | collective-permute-start | bytes 405512 | tf_op jit(solution)/shard_map/ppermute | solution.py:45
  13.5 7.7 %collective-permute-start.7 = (bf16[1040,128]{1,0:T(8,128)(2,1)S(1)}, bf16[1040,128]{1,0:T(8,128)(2,1)S(1)}, u32[]{:S(2)}, u32[]{:S(2)}) collective-permute-start(bf16[1040,128]{1,0:T(8,128)(2,1)S(1)} %join.2.refs_0_), channel_id=1, source_target_pairs={{0,200},{1,9},{8,64},{9,1},{64,8},{65,73},{72,128},{73,65},{128,72... | collective-permute-start | bytes 798728 | tf_op jit(solution)/shard_map/ppermute | solution.py:45
  18.5 8.5 %collective-permute-start.4 = (bf16[2064,128]{1,0:T(8,128)(2,1)S(1)}, bf16[2064,128]{1,0:T(8,128)(2,1)S(1)}, u32[]{:S(2)}, u32[]{:S(2)}) collective-permute-start(bf16[2064,128]{1,0:T(8,128)(2,1)S(1)} %join.3.refs_1_.refs_2_), channel_id=1, source_target_pairs={{0,48},{1,17},{8,56},{9,25},{64,112},{65,81},{72,120},{73,89},{128... | collective-permute-start | bytes 1585160 | tf_op jit(solution)/shard_map/ppermute | solution.py:45
  18.9 14.0 %collective-permute-start.5 = (bf16[2064,128]{1,0:T(8,128)(2,1)S(1)}, bf16[2064,128]{1,0:T(8,128)(2,1)S(1)}, u32[]{:S(2)}, u32[]{:S(2)}) collective-permute-start(bf16[2064,128]{1,0:T(8,128)(2,1)S(1)} %join.3.refs_1_.refs_2_), channel_id=1, source_target_pairs={{0,6},{1,3},{8,14},{9,11},{64,70},{65,67},{72,78},{73,75},{128,134... | collective-permute-start | bytes 1585160 | tf_op jit(solution)/shard_map/ppermute | solution.py:45
  18.9 14.0 %collective-permute-start.6 = (bf16[2064,128]{1,0:T(8,128)(2,1)S(1)}, bf16[2064,128]{1,0:T(8,128)(2,1)S(1)}, u32[]{:S(2)}, u32[]{:S(2)}) collective-permute-start(bf16[2064,128]{1,0:T(8,128)(2,1)S(1)} %join.3.refs_1_.refs_2_), channel_id=1, source_target_pairs={{0,54},{1,19},{8,62},{9,27},{64,118},{65,83},{72,126},{73,91},{128... | collective-permute-start | bytes 1585160 | tf_op jit(solution)/shard_map/ppermute | solution.py:45
  21.2 9.0 %collective-permute-start.9 = (bf16[1040,128]{1,0:T(8,128)(2,1)S(1)}, bf16[1040,128]{1,0:T(8,128)(2,1)S(1)}, u32[]{:S(2)}, u32[]{:S(2)}) collective-permute-start(bf16[1040,128]{1,0:T(8,128)(2,1)S(1)} %collective-permute-done.7.refs_1_), channel_id=1, source_target_pairs={{0,64},{1,193},{8,200},{9,73},{64,128},{65,1},{72,8},{73,137},{128... | collective-permute-start | bytes 798728 | tf_op jit(solution)/shard_map/ppermute | solution.py:53
  22.4 10.5 %collective-permute-start.8 = (bf16[1040,128]{1,0:T(8,128)(2,1)S(1)}, bf16[1040,128]{1,0:T(8,128)(2,1)S(1)}, u32[]{:S(2)}, u32[]{:S(2)}) collective-permute-start(bf16[1040,128]{1,0:T(8,128)(2,1)S(1)} %collective-permute-done.7.refs_1_), channel_id=1, source_target_pairs={{0,8},{1,201},{8,0},{9,65},{64,72},{65,9},{72,64},{73,129},{128,13... | collective-permute-start | bytes 798728 | tf_op jit(solution)/shard_map/ppermute | solution.py:45
  27.0 6.9 %collective-permute-start.10 = (bf16[2064,128]{1,0:T(8,128)(2,1)S(1)}, bf16[2064,128]{1,0:T(8,128)(2,1)S(1)}, u32[]{:S(2)}, u32[]{:S(2)}) collective-permute-start(bf16[2064,128]{1,0:T(8,128)(2,1)S(1)} %join.3.refs_1_.refs_2_), channel_id=1, source_target_pairs={{0,1},{1,0},{2,3},{3,2},{4,5},{5,4},{6,7},{7,6},{8,9},{9,8},{10,11... | collective-permute-start | bytes 1585160 | tf_op jit(solution)/shard_map/ppermute | solution.py:57
  30.3 3.6 %collective-permute-start.11 = (bf16[2064,128]{1,0:T(8,128)(2,1)S(1)}, bf16[2064,128]{1,0:T(8,128)(2,1)S(1)}, u32[]{:S(2)}, u32[]{:S(2)}) collective-permute-start(bf16[2064,128]{1,0:T(8,128)(2,1)S(1)} %collective-permute-done.4.refs_2_.refs_3_), channel_id=1, source_target_pairs={{0,1},{1,0},{2,3},{3,2},{4,5},{5,4},{6,7},{7,6},{8,9},{9,8},{10,11... | collective-permute-start | bytes 1585160 | tf_op jit(solution)/shard_map/ppermute | solution.py:57
  32.9 2.5 %collective-permute-start.12 = (bf16[2064,128]{1,0:T(8,128)(2,1)S(1)}, bf16[2064,128]{1,0:T(8,128)(2,1)S(1)}, u32[]{:S(2)}, u32[]{:S(2)}) collective-permute-start(bf16[2064,128]{1,0:T(8,128)(2,1)S(1)} %collective-permute-done.5.refs_3_.refs_4_.refs_1_), channel_id=1, source_target_pairs={{0,1},{1,0},{2,3},{3,2},{4,5},{5,4},{6,7},{7,6},{8,9},{9,8},{10,11... | collective-permute-start | bytes 1585160 | tf_op jit(solution)/shard_map/ppermute | solution.py:57
  33.9 2.3 %collective-permute-start.13 = (bf16[2064,128]{1,0:T(8,128)(2,1)S(1)}, bf16[2064,128]{1,0:T(8,128)(2,1)S(1)}, u32[]{:S(2)}, u32[]{:S(2)}) collective-permute-start(bf16[2064,128]{1,0:T(8,128)(2,1)S(1)} %collective-permute-done.6.refs_4_.refs_5_.refs_2_), channel_id=1, source_target_pairs={{0,1},{1,0},{2,3},{3,2},{4,5},{5,4},{6,7},{7,6},{8,9},{9,8},{10,11... | collective-permute-start | bytes 1585160 | tf_op jit(solution)/shard_map/ppermute | solution.py:57
  36.9 5.8 %collective-permute-start.15 = (bf16[256,512]{1,0:T(8,128)(2,1)S(1)}, bf16[256,512]{1,0:T(8,128)(2,1)S(1)}, u32[]{:S(2)}, u32[]{:S(2)}) collective-permute-start(bf16[256,512]{1,0:T(8,128)(2,1)S(1)} %pair.9), channel_id=1, source_target_pairs={{0,200},{1,9},{8,64},{9,1},{64,8},{65,73},{72,128},{73,65},{128,72... | collective-permute-start | bytes 786440 | tf_op jit(solution)/shard_map/ppermute | solution.py:45
  42.8 7.0 %collective-permute-start.16 = (bf16[256,512]{1,0:T(8,128)(2,1)S(1)}, bf16[256,512]{1,0:T(8,128)(2,1)S(1)}, u32[]{:S(2)}, u32[]{:S(2)}) collective-permute-start(bf16[256,512]{1,0:T(8,128)(2,1)S(1)} %add_convert_fusion.1), channel_id=1, source_target_pairs={{0,8},{1,201},{8,0},{9,65},{64,72},{65,9},{72,64},{73,129},{128,13... | collective-permute-start | bytes 786440 | tf_op jit(solution)/shard_map/ppermute | solution.py:45
  48.5 5.4 %collective-permute-start.14 = (bf16[128,512]{1,0:T(8,128)(2,1)S(1)}, bf16[128,512]{1,0:T(8,128)(2,1)S(1)}, u32[]{:S(2)}, u32[]{:S(2)}) collective-permute-start(bf16[128,512]{1,0:T(8,128)(2,1)S(1)} %slice.22), channel_id=1, source_target_pairs={{0,8},{1,201},{8,0},{9,65},{64,72},{65,9},{72,64},{73,129},{128,13... | collective-permute-start | bytes 393224 | tf_op jit(solution)/shard_map/ppermute | solution.py:45
  49.9 6.8 %collective-permute-start.17 = (bf16[128,512]{1,0:T(8,128)(2,1)S(1)}, bf16[128,512]{1,0:T(8,128)(2,1)S(1)}, u32[]{:S(2)}, u32[]{:S(2)}) collective-permute-start(bf16[128,512]{1,0:T(8,128)(2,1)S(1)} %get-tuple-element.18), channel_id=1, source_target_pairs={{0,192},{1,65},{8,72},{9,201},{64,0},{65,129},{72,136},{73,9},{128... | collective-permute-start | bytes 393224 | tf_op jit(solution)/shard_map/ppermute | solution.py:53
  50.0 9.2 %copy-start.1 = (f32[128,512]{1,0:T(8,128)S(1)}, f32[128,512]{1,0:T(8,128)}, u32[]{:S(2)}) copy-start(f32[128,512]{1,0:T(8,128)} %emb.3) | copy-start | bytes 786436
  50.0 9.2 %collective-permute-start.18 = (bf16[128,512]{1,0:T(8,128)(2,1)S(1)}, bf16[128,512]{1,0:T(8,128)(2,1)S(1)}, u32[]{:S(2)}, u32[]{:S(2)}) collective-permute-start(bf16[128,512]{1,0:T(8,128)(2,1)S(1)} %get-tuple-element.17), channel_id=1, source_target_pairs={{0,200},{1,9},{8,64},{9,1},{64,8},{65,73},{72,128},{73,65},{128,72... | collective-permute-start | bytes 393224 | tf_op jit(solution)/shard_map/ppermute | solution.py:45

commit v9 on v8

--- a/solution.py
+++ b/solution.py
@@ -29,8 +29,8 @@
 LINKS = {
     "xa": lambda x, y, z: (x ^ 1, y, z),
     "xb": lambda x, y, z: (3 - x, y, z),
-    "xaya": lambda x, y, z: (x ^ 1, y ^ 1, z),
-    "xbyb": lambda x, y, z: (3 - x, 3 - y, z),
+    "xayb": lambda x, y, z: (x ^ 1, 3 - y, z),
+    "xbya": lambda x, y, z: (3 - x, y ^ 1, z),
     "ya": lambda x, y, z: (x, y ^ 1, z),
     "yb": lambda x, y, z: (x, 3 - y, z),
     "za": lambda x, y, z: (x, y, z ^ 1),
@@ -191,12 +191,12 @@
     whole = pack(embeddings, margin, group)
 
     near = swap(whole, "za", "zb")
-    square = [swap(whole, a, b) for a, b in (("xaya", "xbyb"), ("xa", "xb"), ("ya", "yb"))]
+    square = [swap(whole, a, b) for a, b in (("xbya", "xayb"), ("xb", "xa"), ("ya", "yb"))]
     both = join(whole, near)
     back = swap(both, "zb", "za")
     c0 = join(*square, whole)
     far, ahead = shift(back, 1), swap(back, "za", "zb")
-    c3, c1, c2 = (swap(c0, b, a) for a, b in (("xaya", "xbyb"), ("xa", "xb"), ("ya", "yb")))
+    c3, c1, c2 = (swap(c0, b, a) for a, b in (("xbya", "xayb"), ("xb", "xa"), ("ya", "yb")))
     e0 = swap_cores(c0)
     (p_far,) = pair([far], [c0, c1], F32)
     c2, c3, ahead, p_far = lax.optimization_barrier((c2, c3, ahead, p_far))

time: 60.3 us -> 60.2 us (level)
  starting transfers between devices: 25.1 us -> 22.9 us
  waiting for transfers between devices: 22.1 us -> 23.9 us
    ppermute x13, waiting for transfers between devices: 15 us -> 16.8 us  [swap(): return lax.ppermute(block, AXES, pairs)]
    ppermute x13, starting transfers between devices: 21.9 us -> 20.5 us  [swap(): return lax.ppermute(block, AXES, pairs)]
    ppermute x4, starting transfers between devices: 1.83 us -> 0.89 us  [swap_cores(): return lax.ppermute(block, AXES, [(i, i ^ 1) for i in range(256)])]
where the time goes in v9:
time: 60.2 us; the launch traced here: 59.8 us
  waiting for transfers between devices  23.9 us (40%)
  starting transfers between devices  22.9 us (38%)
  Pallas kernels  11 us (18%)
  local copies, waits for them, and re-layouts  1.67 us (3%)
    ppermute x13, starting transfers between devices, swap(): return lax.ppermute(block, AXES, pairs)  20.5 us
    ppermute x13, waiting for transfers between devices, swap(): return lax.ppermute(block, AXES, pairs)  16.8 us
    pallas_call x5, Pallas kernels, pair(): pl.pallas_call(functools.partial(pair_kernel, len(r_in), len(c_in), len(s...  9.88 us
    ppermute x2, waiting for transfers between devices, shift(): return lax.ppermute(block, AXES, pairs)  6.26 us
    unnamed x8, local copies, waits for them, and re-layouts  1.61 us
    ppermute x2, starting transfers between devices, shift(): return lax.ppermute(block, AXES, pairs)  1.47 us
  transfers between devices with their start and end apart: 19, of which 12 were waited for; matrix products, arithmetic and copies ran while one was open for 0% of the time, Pallas kernels for 15%

profile of v9, /device:TPU:1, one launch (start us, length us, event | category | flops | bytes accessed | tf_op | source)
XLA Modules:
  0.0 59.8 jit_solution(3916126345986799519)
XLA Ops:
  0.0 0.0 copy-start
  0.0 0.9 %copy-done = f32[128,512]{1,0:T(8,128)S(1)} copy-done((f32[128,512]{1,0:T(8,128)S(1)}, f32[128,512]{1,0:T(8,128)}, u32[]{:S(2)}) %copy-start) | copy-done | bytes 262168
  1.0 0.1 units.1.unit
  1.1 0.0 copy-start.2
  1.1 0.0 copy-start.3
  1.1 0.6 %copy-done.2 = s32[128]{0:T(128)S(1)} copy-done((s32[128]{0:T(128)S(1)}, s32[128]{0:T(128)}, u32[]{:S(2)}) %copy-start.2) | copy-done | bytes 536
  1.7 0.0 copy-done.3
  1.8 6.5 %collective-permute-start = (bf16[528,128]{1,0:T(8,128)(2,1)S(1)}, bf16[528,128]{1,0:T(8,128)(2,1)S(1)}, u32[]{:S(2)}, u32[]{:S(2)}) collective-permute-start(bf16[528,128]{1,0:T(8,128)(2,1)S(1)} %pack.1.refs_0_.refs_3_), channel_id=1, source_target_pairs={{0,8},{1,201},{8,0},{9,65},{64,72},{65,9},{72,64},{73,129},{128,13... | collective-permute-start | bytes 405512 | tf_op jit(solution)/shard_map/ppermute | solution.py:45
  8.3 3.7 %collective-permute-start.1 = (bf16[528,128]{1,0:T(8,128)(2,1)S(1)}, bf16[528,128]{1,0:T(8,128)(2,1)S(1)}, u32[]{:S(2)}, u32[]{:S(2)}) collective-permute-start(bf16[528,128]{1,0:T(8,128)(2,1)S(1)} %pack.1.refs_0_.refs_3_), channel_id=1, source_target_pairs={{0,50},{1,23},{8,58},{9,31},{64,114},{65,87},{72,122},{73,95},{128... | collective-permute-start | bytes 405512 | tf_op jit(solution)/shard_map/ppermute | solution.py:45
  11.9 0.3 collective-permute-start.2
  12.2 0.0 collective-permute-start.3
  12.2 0.0 collective-permute-done.refs_1_
  12.2 0.1 collective-permute-start.7
  12.3 2.0 %collective-permute-done.1.refs_0_ = bf16[528,128]{1,0:T(8,128)(2,1)S(1)} collective-permute-done((bf16[528,128]{1,0:T(8,128)(2,1)S(1)}, bf16[528,128]{1,0:T(8,128)(2,1)S(1)}, u32[]{:S(2)}, u32[]{:S(2)}) %collective-permute-start.1) | collective-permute-done | bytes 135200 | tf_op jit(solution)/shard_map/ppermute | solution.py:45
  14.3 2.0 %collective-permute-done.2.refs_1_ = bf16[528,128]{1,0:T(8,128)(2,1)S(1)} collective-permute-done((bf16[528,128]{1,0:T(8,128)(2,1)S(1)}, bf16[528,128]{1,0:T(8,128)(2,1)S(1)}, u32[]{:S(2)}, u32[]{:S(2)}) %collective-permute-start.2) | collective-permute-done | bytes 135200 | tf_op jit(solution)/shard_map/ppermute | solution.py:45
  16.3 1.2 %collective-permute-done.3.refs_2_ = bf16[528,128]{1,0:T(8,128)(2,1)S(1)} collective-permute-done((bf16[528,128]{1,0:T(8,128)(2,1)S(1)}, bf16[528,128]{1,0:T(8,128)(2,1)S(1)}, u32[]{:S(2)}, u32[]{:S(2)}) %collective-permute-start.3) | collective-permute-done | bytes 135200 | tf_op jit(solution)/shard_map/ppermute | solution.py:45
  17.6 2.6 %collective-permute-start.4 = (bf16[2064,128]{1,0:T(8,128)(2,1)S(1)}, bf16[2064,128]{1,0:T(8,128)(2,1)S(1)}, u32[]{:S(2)}, u32[]{:S(2)}) collective-permute-start(bf16[2064,128]{1,0:T(8,128)(2,1)S(1)} %join.3.refs_1_.refs_2_), channel_id=1, source_target_pairs={{0,16},{1,49},{8,24},{9,57},{64,80},{65,113},{72,88},{73,121},{128... | collective-permute-start | bytes 1585160 | tf_op jit(solution)/shard_map/ppermute | solution.py:45
  20.2 0.0 collective-permute-start.5
  20.2 1.4 %collective-permute-start.6 = (bf16[2064,128]{1,0:T(8,128)(2,1)S(1)}, bf16[2064,128]{1,0:T(8,128)(2,1)S(1)}, u32[]{:S(2)}, u32[]{:S(2)}) collective-permute-start(bf16[2064,128]{1,0:T(8,128)(2,1)S(1)} %join.3.refs_1_.refs_2_), channel_id=1, source_target_pairs={{0,22},{1,51},{8,30},{9,59},{64,86},{65,115},{72,94},{73,123},{128... | collective-permute-start | bytes 1585160 | tf_op jit(solution)/shard_map/ppermute | solution.py:45
  21.5 0.0 collective-permute-done.7.refs_1_
  21.5 1.2 %collective-permute-start.9 = (bf16[1040,128]{1,0:T(8,128)(2,1)S(1)}, bf16[1040,128]{1,0:T(8,128)(2,1)S(1)}, u32[]{:S(2)}, u32[]{:S(2)}) collective-permute-start(bf16[1040,128]{1,0:T(8,128)(2,1)S(1)} %collective-permute-done.7.refs_1_), channel_id=1, source_target_pairs={{0,64},{1,193},{8,200},{9,73},{64,128},{65,1},{72,8},{73,137},{128... | collective-permute-start | bytes 798728 | tf_op jit(solution)/shard_map/ppermute | solution.py:53
  22.7 0.0 collective-permute-start.8
  22.7 4.5 %collective-permute-done.4.refs_2_.refs_3_ = bf16[2064,128]{1,0:T(8,128)(2,1)S(1)} collective-permute-done((bf16[2064,128]{1,0:T(8,128)(2,1)S(1)}, bf16[2064,128]{1,0:T(8,128)(2,1)S(1)}, u32[]{:S(2)}, u32[]{:S(2)}) %collective-permute-start.4) | collective-permute-done | bytes 528416 | tf_op jit(solution)/shard_map/ppermute | solution.py:45
  27.3 0.0 collective-permute-start.10
  27.3 3.4 %collective-permute-done.9.refs_0_ = bf16[1040,128]{1,0:T(8,128)(2,1)S(1)} collective-permute-done((bf16[1040,128]{1,0:T(8,128)(2,1)S(1)}, bf16[1040,128]{1,0:T(8,128)(2,1)S(1)}, u32[]{:S(2)}, u32[]{:S(2)}) %collective-permute-start.9) | collective-permute-done | bytes 266272 | tf_op jit(solution)/shard_map/ppermute | solution.py:53
  30.7 0.4 collective-permute-start.11
  31.1 0.8 %pair.5.refs_5_ = f32[256,512]{1,0:T(8,128)S(1)} custom-call(bf16[1040,128]{1,0:T(8,128)(2,1)S(1)} %collective-permute-done.9.refs_0_, bf16[2064,128]{1,0:T(8,128)(2,1)S(1)} %join.3.refs_1_.refs_2_, bf16[2064,128]{1,0:T(8,128)(2,1)S(1)} %collective-permute-done.4.refs_2_.refs_3_), custom_call_target="tpu_custom_call" | custom-call | flops 536870912 | bytes 1310720 | tf_op jit(solution)/shard_map/pair/pallas_call | solution.py:144
  31.8 2.4 %collective-permute-done.5.refs_3_.refs_4_.refs_1_ = bf16[2064,128]{1,0:T(8,128)(2,1)S(1)} collective-permute-done((bf16[2064,128]{1,0:T(8,128)(2,1)S(1)}, bf16[2064,128]{1,0:T(8,128)(2,1)S(1)}, u32[]{:S(2)}, u32[]{:S(2)}) %collective-permute-start.5) | collective-permute-done | bytes 528416 | tf_op jit(solution)/shard_map/ppermute | solution.py:45
  34.2 0.0 collective-permute-done.6.refs_4_.refs_5_.refs_2_
  34.2 0.0 collective-permute-done.8.refs_0_
  34.2 0.4 collective-permute-start.12
  34.6 0.1 collective-permute-start.13
  34.7 0.0 collective-permute-done.10.refs_5_.refs_6_.refs_3_
  34.7 0.0 collective-permute-done.11.refs_6_.refs_7_.refs_4_
  34.7 1.3 %pair.8.refs_3_ = f32[256,512]{1,0:T(8,128)S(1)} custom-call(bf16[1040,128]{1,0:T(8,128)(2,1)S(1)} %collective-permute-done.9.refs_0_, bf16[2064,128]{1,0:T(8,128)(2,1)S(1)} %collective-permute-done.5.refs_3_.refs_4_.refs_1_, bf16[2064,128]{1,0:T(8,128)(2,1)S(1)} %collective-permute-done.6.refs_4_.refs_5_.refs_2_, ...), custom_call_target="tpu_custom_call" | custom-call | flops 1073741824 | bytes 2359296 | tf_op jit(solution)/shard_map/pair/pallas_call | solution.py:144
  36.0 0.1 collective-permute-done.12.refs_7_.refs_8_.refs_1_
  36.2 0.8 %collective-permute-done.13.refs_8_.refs_9_.refs_2_ = bf16[2064,128]{1,0:T(8,128)(2,1)S(1)} collective-permute-done((bf16[2064,128]{1,0:T(8,128)(2,1)S(1)}, bf16[2064,128]{1,0:T(8,128)(2,1)S(1)}, u32[]{:S(2)}, u32[]{:S(2)}) %collective-permute-start.13) | collective-permute-done | bytes 528416 | tf_op jit(solution)/shard_map/ppermute | solution.py:57
  36.9 0.7 %pair.9 = bf16[256,512]{1,0:T(8,128)(2,1)S(1)} custom-call(bf16[1040,128]{1,0:T(8,128)(2,1)S(1)} %collective-permute-done.9.refs_0_, bf16[2064,128]{1,0:T(8,128)(2,1)S(1)} %collective-permute-done.12.refs_7_.refs_8_.refs_1_, bf16[2064,128]{1,0:T(8,128)(2,1)S(1)} %collective-permute-done.13.refs_8_.refs_9_.refs_2_, f32[256,512]{1,0:T(8,128)S(1)} %pair.8.refs_3_), custom_call_target="tpu_custom_call" | custom-call | flops 536870912 | bytes 1310720 | tf_op jit(solution)/shard_map/pair/pallas_call | solution.py:144
  37.7 0.3 collective-permute-start.15
  38.0 4.6 %pair.7 = (f32[256,512]{1,0:T(8,128)S(1)}, f32[256,512]{1,0:T(8,128)S(1)}) custom-call(bf16[1040,128]{1,0:T(8,128)(2,1)S(1)} %collective-permute-done.8.refs_0_, bf16[1040,128]{1,0:T(8,128)(2,1)S(1)} %collective-permute-done.7.refs_1_, bf16[2064,128]{1,0:T(8,128)(2,1)S(1)} %join.3.refs_1_.refs_2_, ...), custom_call_target="tpu_custom_call" | custom-call | flops 4294967296 | bytes 4718592 | tf_op jit(solution)/shard_map/pair/pallas_call | solution.py:144
  42.6 0.9 %collective-permute-done.15 = bf16[256,512]{1,0:T(8,128)(2,1)S(1)} collective-permute-done((bf16[256,512]{1,0:T(8,128)(2,1)S(1)}, bf16[256,512]{1,0:T(8,128)(2,1)S(1)}, u32[]{:S(2)}, u32[]{:S(2)}) %collective-permute-start.15) | collective-permute-done | bytes 262176 | tf_op jit(solution)/shard_map/ppermute | solution.py:45
  43.5 0.1 add_convert_fusion.1
  43.6 2.0 %collective-permute-start.16 = (bf16[256,512]{1,0:T(8,128)(2,1)S(1)}, bf16[256,512]{1,0:T(8,128)(2,1)S(1)}, u32[]{:S(2)}, u32[]{:S(2)}) collective-permute-start(bf16[256,512]{1,0:T(8,128)(2,1)S(1)} %add_convert_fusion.1), channel_id=1, source_target_pairs={{0,8},{1,201},{8,0},{9,65},{64,72},{65,9},{72,64},{73,129},{128,13... | collective-permute-start | bytes 786440 | tf_op jit(solution)/shard_map/ppermute | solution.py:45
  45.6 2.4 %pair.6 = f32[256,512]{1,0:T(8,128)S(1)} custom-call(bf16[1040,128]{1,0:T(8,128)(2,1)S(1)} %join.2.refs_0_, bf16[2064,128]{1,0:T(8,128)(2,1)S(1)} %join.3.refs_1_.refs_2_, bf16[2064,128]{1,0:T(8,128)(2,1)S(1)} %collective-permute-done.4.refs_2_.refs_3_, bf16[2064,128]{1,0:T(8,128)(2,1)S(1)} %collective-permute-done.5.refs_3_.refs_4_.refs_1_, ...), custom_call_target="tpu_custom_call" | custom-call | flops 2147483648 | bytes 4456448 | tf_op jit(solution)/shard_map/pair/pallas_call | solution.py:144
  48.0 0.8 %collective-permute-start.14 = (bf16[128,512]{1,0:T(8,128)(2,1)S(1)}, bf16[128,512]{1,0:T(8,128)(2,1)S(1)}, u32[]{:S(2)}, u32[]{:S(2)}) collective-permute-start(bf16[128,512]{1,0:T(8,128)(2,1)S(1)} %slice.22), channel_id=1, source_target_pairs={{0,8},{1,201},{8,0},{9,65},{64,72},{65,9},{72,64},{73,129},{128,13... | collective-permute-start | bytes 393224 | tf_op jit(solution)/shard_map/ppermute | solution.py:45
  48.9 1.2 %collective-permute-done.16 = bf16[256,512]{1,0:T(8,128)(2,1)S(1)} collective-permute-done((bf16[256,512]{1,0:T(8,128)(2,1)S(1)}, bf16[256,512]{1,0:T(8,128)(2,1)S(1)}, u32[]{:S(2)}, u32[]{:S(2)}) %collective-permute-start.16) | collective-permute-done | bytes 262176 | tf_op jit(solution)/shard_map/ppermute | solution.py:45
  50.1 0.1 add_convert_fusion
  50.2 0.3 collective-permute-start.17
  50.5 0.0 copy-start.1
  50.5 2.9 %collective-permute-start.18 = (bf16[128,512]{1,0:T(8,128)(2,1)S(1)}, bf16[128,512]{1,0:T(8,128)(2,1)S(1)}, u32[]{:S(2)}, u32[]{:S(2)}) collective-permute-start(bf16[128,512]{1,0:T(8,128)(2,1)S(1)} %get-tuple-element.17), channel_id=1, source_target_pairs={{0,200},{1,9},{8,64},{9,1},{64,8},{65,73},{72,128},{73,65},{128,72... | collective-permute-start | bytes 393224 | tf_op jit(solution)/shard_map/ppermute | solution.py:45
  53.4 0.0 collective-permute-done.14.refs_0_
  53.4 2.8 %collective-permute-done.17.refs_1_ = bf16[128,512]{1,0:T(8,128)(2,1)S(1)} collective-permute-done((bf16[128,512]{1,0:T(8,128)(2,1)S(1)}, bf16[128,512]{1,0:T(8,128)(2,1)S(1)}, u32[]{:S(2)}, u32[]{:S(2)}) %collective-permute-start.17) | collective-permute-done | bytes 131104 | tf_op jit(solution)/shard_map/ppermute | solution.py:53
  56.3 2.6 %collective-permute-done.18.refs_2_ = bf16[128,512]{1,0:T(8,128)(2,1)S(1)} collective-permute-done((bf16[128,512]{1,0:T(8,128)(2,1)S(1)}, bf16[128,512]{1,0:T(8,128)(2,1)S(1)}, u32[]{:S(2)}, u32[]{:S(2)}) %collective-permute-start.18) | collective-permute-done | bytes 131104 | tf_op jit(solution)/shard_map/ppermute | solution.py:45
  58.9 0.0 copy-done.1
  58.9 0.9 %final.1 = f32[128,512]{1,0:T(8,128)} custom-call(f32[128,512]{1,0:T(8,128)S(1)} %copy-done.1, f32[128,512]{1,0:T(8,128)S(1)} %slice.17.own, bf16[128,512]{1,0:T(8,128)(2,1)S(1)} %collective-permute-done.14.refs_0_, bf16[128,512]{1,0:T(8,128)(2,1)S(1)} %collective-permute-done.17.refs_1_, bf16[128,512]{1,0:T(8,128)(2,1)S(1)} %collective-permute-done.18.refs_2_), custom_call_target="tpu_custom_call" | custom-call | tf_op jit(solution)/shard_map/final/pallas_call | solution.py:216
  (6 shorter events, 0.1 us)
Async XLA Ops:
  0.0 0.9 %copy-start = (f32[128,512]{1,0:T(8,128)S(1)}, f32[128,512]{1,0:T(8,128)}, u32[]{:S(2)}) copy-start(f32[128,512]{1,0:T(8,128)} %emb.3) | copy-start | bytes 786436
  1.1 0.7 %copy-start.2 = (s32[128]{0:T(128)S(1)}, s32[128]{0:T(128)}, u32[]{:S(2)}) copy-start(s32[128]{0:T(128)} %param.4) | copy-start | bytes 1540
  1.1 0.7 %copy-start.3 = (s32[128]{0:T(128)S(1)}, s32[128]{0:T(128)}, u32[]{:S(2)}) copy-start(s32[128]{0:T(128)} %param.5) | copy-start | bytes 1540
  1.8 10.4 %collective-permute-start = (bf16[528,128]{1,0:T(8,128)(2,1)S(1)}, bf16[528,128]{1,0:T(8,128)(2,1)S(1)}, u32[]{:S(2)}, u32[]{:S(2)}) collective-permute-start(bf16[528,128]{1,0:T(8,128)(2,1)S(1)} %pack.1.refs_0_.refs_3_), channel_id=1, source_target_pairs={{0,8},{1,201},{8,0},{9,65},{64,72},{65,9},{72,64},{73,129},{128,13... | collective-permute-start | bytes 405512 | tf_op jit(solution)/shard_map/ppermute | solution.py:45
  8.3 6.1 %collective-permute-start.1 = (bf16[528,128]{1,0:T(8,128)(2,1)S(1)}, bf16[528,128]{1,0:T(8,128)(2,1)S(1)}, u32[]{:S(2)}, u32[]{:S(2)}) collective-permute-start(bf16[528,128]{1,0:T(8,128)(2,1)S(1)} %pack.1.refs_0_.refs_3_), channel_id=1, source_target_pairs={{0,50},{1,23},{8,58},{9,31},{64,114},{65,87},{72,122},{73,95},{128... | collective-permute-start | bytes 405512 | tf_op jit(solution)/shard_map/ppermute | solution.py:45
  11.9 4.4 %collective-permute-start.2 = (bf16[528,128]{1,0:T(8,128)(2,1)S(1)}, bf16[528,128]{1,0:T(8,128)(2,1)S(1)}, u32[]{:S(2)}, u32[]{:S(2)}) collective-permute-start(bf16[528,128]{1,0:T(8,128)(2,1)S(1)} %pack.1.refs_0_.refs_3_), channel_id=1, source_target_pairs={{0,48},{1,17},{8,56},{9,25},{64,112},{65,81},{72,120},{73,89},{128... | collective-permute-start | bytes 405512 | tf_op jit(solution)/shard_map/ppermute | solution.py:45
  12.2 5.4 %collective-permute-start.3 = (bf16[528,128]{1,0:T(8,128)(2,1)S(1)}, bf16[528,128]{1,0:T(8,128)(2,1)S(1)}, u32[]{:S(2)}, u32[]{:S(2)}) collective-permute-start(bf16[528,128]{1,0:T(8,128)(2,1)S(1)} %pack.1.refs_0_.refs_3_), channel_id=1, source_target_pairs={{0,2},{1,7},{8,10},{9,15},{64,66},{65,71},{72,74},{73,79},{128,130... | collective-permute-start | bytes 405512 | tf_op jit(solution)/shard_map/ppermute | solution.py:45
  12.2 9.3 %collective-permute-start.7 = (bf16[1040,128]{1,0:T(8,128)(2,1)S(1)}, bf16[1040,128]{1,0:T(8,128)(2,1)S(1)}, u32[]{:S(2)}, u32[]{:S(2)}) collective-permute-start(bf16[1040,128]{1,0:T(8,128)(2,1)S(1)} %join.2.refs_0_), channel_id=1, source_target_pairs={{0,200},{1,9},{8,64},{9,1},{64,8},{65,73},{72,128},{73,65},{128,72... | collective-permute-start | bytes 798728 | tf_op jit(solution)/shard_map/ppermute | solution.py:45
  17.6 9.7 %collective-permute-start.4 = (bf16[2064,128]{1,0:T(8,128)(2,1)S(1)}, bf16[2064,128]{1,0:T(8,128)(2,1)S(1)}, u32[]{:S(2)}, u32[]{:S(2)}) collective-permute-start(bf16[2064,128]{1,0:T(8,128)(2,1)S(1)} %join.3.refs_1_.refs_2_), channel_id=1, source_target_pairs={{0,16},{1,49},{8,24},{9,57},{64,80},{65,113},{72,88},{73,121},{128... | collective-permute-start | bytes 1585160 | tf_op jit(solution)/shard_map/ppermute | solution.py:45
  20.2 14.0 %collective-permute-start.5 = (bf16[2064,128]{1,0:T(8,128)(2,1)S(1)}, bf16[2064,128]{1,0:T(8,128)(2,1)S(1)}, u32[]{:S(2)}, u32[]{:S(2)}) collective-permute-start(bf16[2064,128]{1,0:T(8,128)(2,1)S(1)} %join.3.refs_1_.refs_2_), channel_id=1, source_target_pairs={{0,6},{1,3},{8,14},{9,11},{64,70},{65,67},{72,78},{73,75},{128,134... | collective-permute-start | bytes 1585160 | tf_op jit(solution)/shard_map/ppermute | solution.py:45
  20.2 14.0 %collective-permute-start.6 = (bf16[2064,128]{1,0:T(8,128)(2,1)S(1)}, bf16[2064,128]{1,0:T(8,128)(2,1)S(1)}, u32[]{:S(2)}, u32[]{:S(2)}) collective-permute-start(bf16[2064,128]{1,0:T(8,128)(2,1)S(1)} %join.3.refs_1_.refs_2_), channel_id=1, source_target_pairs={{0,22},{1,51},{8,30},{9,59},{64,86},{65,115},{72,94},{73,123},{128... | collective-permute-start | bytes 1585160 | tf_op jit(solution)/shard_map/ppermute | solution.py:45
  21.5 9.2 %collective-permute-start.9 = (bf16[1040,128]{1,0:T(8,128)(2,1)S(1)}, bf16[1040,128]{1,0:T(8,128)(2,1)S(1)}, u32[]{:S(2)}, u32[]{:S(2)}) collective-permute-start(bf16[1040,128]{1,0:T(8,128)(2,1)S(1)} %collective-permute-done.7.refs_1_), channel_id=1, source_target_pairs={{0,64},{1,193},{8,200},{9,73},{64,128},{65,1},{72,8},{73,137},{128... | collective-permute-start | bytes 798728 | tf_op jit(solution)/shard_map/ppermute | solution.py:53
  22.7 11.5 %collective-permute-start.8 = (bf16[1040,128]{1,0:T(8,128)(2,1)S(1)}, bf16[1040,128]{1,0:T(8,128)(2,1)S(1)}, u32[]{:S(2)}, u32[]{:S(2)}) collective-permute-start(bf16[1040,128]{1,0:T(8,128)(2,1)S(1)} %collective-permute-done.7.refs_1_), channel_id=1, source_target_pairs={{0,8},{1,201},{8,0},{9,65},{64,72},{65,9},{72,64},{73,129},{128,13... | collective-permute-start | bytes 798728 | tf_op jit(solution)/shard_map/ppermute | solution.py:45
  27.3 7.5 %collective-permute-start.10 = (bf16[2064,128]{1,0:T(8,128)(2,1)S(1)}, bf16[2064,128]{1,0:T(8,128)(2,1)S(1)}, u32[]{:S(2)}, u32[]{:S(2)}) collective-permute-start(bf16[2064,128]{1,0:T(8,128)(2,1)S(1)} %join.3.refs_1_.refs_2_), channel_id=1, source_target_pairs={{0,1},{1,0},{2,3},{3,2},{4,5},{5,4},{6,7},{7,6},{8,9},{9,8},{10,11... | collective-permute-start | bytes 1585160 | tf_op jit(solution)/shard_map/ppermute | solution.py:57
  30.7 4.0 %collective-permute-start.11 = (bf16[2064,128]{1,0:T(8,128)(2,1)S(1)}, bf16[2064,128]{1,0:T(8,128)(2,1)S(1)}, u32[]{:S(2)}, u32[]{:S(2)}) collective-permute-start(bf16[2064,128]{1,0:T(8,128)(2,1)S(1)} %collective-permute-done.4.refs_2_.refs_3_), channel_id=1, source_target_pairs={{0,1},{1,0},{2,3},{3,2},{4,5},{5,4},{6,7},{7,6},{8,9},{9,8},{10,11... | collective-permute-start | bytes 1585160 | tf_op jit(solution)/shard_map/ppermute | solution.py:57
  34.2 2.0 %collective-permute-start.12 = (bf16[2064,128]{1,0:T(8,128)(2,1)S(1)}, bf16[2064,128]{1,0:T(8,128)(2,1)S(1)}, u32[]{:S(2)}, u32[]{:S(2)}) collective-permute-start(bf16[2064,128]{1,0:T(8,128)(2,1)S(1)} %collective-permute-done.5.refs_3_.refs_4_.refs_1_), channel_id=1, source_target_pairs={{0,1},{1,0},{2,3},{3,2},{4,5},{5,4},{6,7},{7,6},{8,9},{9,8},{10,11... | collective-permute-start | bytes 1585160 | tf_op jit(solution)/shard_map/ppermute | solution.py:57
  34.6 2.3 %collective-permute-start.13 = (bf16[2064,128]{1,0:T(8,128)(2,1)S(1)}, bf16[2064,128]{1,0:T(8,128)(2,1)S(1)}, u32[]{:S(2)}, u32[]{:S(2)}) collective-permute-start(bf16[2064,128]{1,0:T(8,128)(2,1)S(1)} %collective-permute-done.6.refs_4_.refs_5_.refs_2_), channel_id=1, source_target_pairs={{0,1},{1,0},{2,3},{3,2},{4,5},{5,4},{6,7},{7,6},{8,9},{9,8},{10,11... | collective-permute-start | bytes 1585160 | tf_op jit(solution)/shard_map/ppermute | solution.py:57
  37.7 5.8 %collective-permute-start.15 = (bf16[256,512]{1,0:T(8,128)(2,1)S(1)}, bf16[256,512]{1,0:T(8,128)(2,1)S(1)}, u32[]{:S(2)}, u32[]{:S(2)}) collective-permute-start(bf16[256,512]{1,0:T(8,128)(2,1)S(1)} %pair.9), channel_id=1, source_target_pairs={{0,200},{1,9},{8,64},{9,1},{64,8},{65,73},{72,128},{73,65},{128,72... | collective-permute-start | bytes 786440 | tf_op jit(solution)/shard_map/ppermute | solution.py:45
  43.6 6.5 %collective-permute-start.16 = (bf16[256,512]{1,0:T(8,128)(2,1)S(1)}, bf16[256,512]{1,0:T(8,128)(2,1)S(1)}, u32[]{:S(2)}, u32[]{:S(2)}) collective-permute-start(bf16[256,512]{1,0:T(8,128)(2,1)S(1)} %add_convert_fusion.1), channel_id=1, source_target_pairs={{0,8},{1,201},{8,0},{9,65},{64,72},{65,9},{72,64},{73,129},{128,13... | collective-permute-start | bytes 786440 | tf_op jit(solution)/shard_map/ppermute | solution.py:45
  48.0 5.4 %collective-permute-start.14 = (bf16[128,512]{1,0:T(8,128)(2,1)S(1)}, bf16[128,512]{1,0:T(8,128)(2,1)S(1)}, u32[]{:S(2)}, u32[]{:S(2)}) collective-permute-start(bf16[128,512]{1,0:T(8,128)(2,1)S(1)} %slice.22), channel_id=1, source_target_pairs={{0,8},{1,201},{8,0},{9,65},{64,72},{65,9},{72,64},{73,129},{128,13... | collective-permute-start | bytes 393224 | tf_op jit(solution)/shard_map/ppermute | solution.py:45
  50.2 6.1 %collective-permute-start.17 = (bf16[128,512]{1,0:T(8,128)(2,1)S(1)}, bf16[128,512]{1,0:T(8,128)(2,1)S(1)}, u32[]{:S(2)}, u32[]{:S(2)}) collective-permute-start(bf16[128,512]{1,0:T(8,128)(2,1)S(1)} %get-tuple-element.18), channel_id=1, source_target_pairs={{0,192},{1,65},{8,72},{9,201},{64,0},{65,129},{72,136},{73,9},{128... | collective-permute-start | bytes 393224 | tf_op jit(solution)/shard_map/ppermute | solution.py:53
  50.5 8.4 %copy-start.1 = (f32[128,512]{1,0:T(8,128)S(1)}, f32[128,512]{1,0:T(8,128)}, u32[]{:S(2)}) copy-start(f32[128,512]{1,0:T(8,128)} %emb.3) | copy-start | bytes 786436
  50.5 8.4 %collective-permute-start.18 = (bf16[128,512]{1,0:T(8,128)(2,1)S(1)}, bf16[128,512]{1,0:T(8,128)(2,1)S(1)}, u32[]{:S(2)}, u32[]{:S(2)}) collective-permute-start(bf16[128,512]{1,0:T(8,128)(2,1)S(1)} %get-tuple-element.17), channel_id=1, source_target_pairs={{0,200},{1,9},{8,64},{9,1},{64,8},{65,73},{72,128},{73,65},{128,72... | collective-permute-start | bytes 393224 | tf_op jit(solution)/shard_map/ppermute | solution.py:45

commit v10 on v8

--- a/solution.py
+++ b/solution.py
@@ -136,7 +136,7 @@
             acc[i] = part if acc[i] is None else acc[i] + part
     halves = [(ref, o) for ref in outs for o in range(0, ref.shape[0], 2 * CPD)]
     for i, (ref, o) in enumerate(halves):
-        ref[o : o + 2 * CPD, :] = acc[i].astype(ref.dtype)
+        ref[o : o + acc[i].shape[0], :] = acc[i].astype(ref.dtype)
 
 
 def pair(r_in, c_in, out_dtype, sums=()):
@@ -207,8 +207,9 @@
     q = swap(p_far, "zb", "za")
     p_ahead, p_back = pair([ahead, back], cols, F32)
     q = swap((p_ahead + q).astype(BF), "za", "zb")
-    (p_own,) = pair([both], cols, F32)
-    q_near = swap(p_own[CPD:].astype(BF), "za", "zb")
+    (p_near,) = pair([near], cols, BF)
+    q_near = swap(p_near, "za", "zb")
+    (p_own,) = pair([whole], cols, F32)
     p_back = (p_back + q).astype(BF)
     arrived = (q_near, shift(p_back[CPD:], -1), swap(p_back[:CPD], "zb", "za"))
 
@@ -220,7 +221,7 @@
         out_specs=VMEM,
         compiler_params=pltpu.CompilerParams(vmem_limit_bytes=SMALL),
         name="final",
-    )(embeddings, p_own[:CPD], *arrived)
+    )(embeddings, p_own, *arrived)
 
 
 def solution(mesh):

time: 60.3 us -> 60.3 us (level)
  Pallas kernels: 11 us -> 12.9 us
  waiting for transfers between devices: 22.1 us -> 20.3 us
    ppermute x2, waiting for transfers between devices: 6.16 us -> 4.04 us  [shift(): return lax.ppermute(block, AXES, pairs)]
    pallas_call x5 -> x6, Pallas kernels: 9.88 us -> 11.7 us  [pair(): pl.pallas_call(functools.partial(pair_kernel, len(r_in), len(c_in), len(s...]
  transfers between devices with their start and end apart: 19 -> 19, of which waited for: 12 -> 12; matrix products, arithmetic and copies ran while one was open for 0% -> 0% of each run, Pallas kernels for 15% -> 18%
where the time goes in v10:
time: 60.3 us; the launch traced here: 60.2 us
  starting transfers between devices  25.1 us (42%)
  waiting for transfers between devices  20.3 us (34%)
  Pallas kernels  12.9 us (21%)
  local copies, waits for them, and re-layouts  1.63 us (3%)
    ppermute x13, starting transfers between devices, swap(): return lax.ppermute(block, AXES, pairs)  21.9 us
    ppermute x13, waiting for transfers between devices, swap(): return lax.ppermute(block, AXES, pairs)  15.3 us
    pallas_call x6, Pallas kernels, pair(): pl.pallas_call(functools.partial(pair_kernel, len(r_in), len(c_in), len(s...  11.7 us
    ppermute x2, waiting for transfers between devices, shift(): return lax.ppermute(block, AXES, pairs)  4.04 us
    ppermute x4, starting transfers between devices, swap_cores(): return lax.ppermute(block, AXES, [(i, i ^ 1) for i in range(256)])  1.83 us
    unnamed x8, local copies, waits for them, and re-layouts  1.61 us
    ppermute x2, starting transfers between devices, shift(): return lax.ppermute(block, AXES, pairs)  1.33 us
  transfers between devices with their start and end apart: 19, of which 12 were waited for; matrix products, arithmetic and copies ran while one was open for 0% of the time, Pallas kernels for 18%

profile of v10, /device:TPU:1, one launch (start us, length us, event | category | flops | bytes accessed | tf_op | source)
XLA Modules:
  0.0 60.2 jit_solution(12119717610221711258)
XLA Ops:
  0.0 0.0 copy-start
  0.0 0.9 %copy-done = f32[128,512]{1,0:T(8,128)S(1)} copy-done((f32[128,512]{1,0:T(8,128)S(1)}, f32[128,512]{1,0:T(8,128)}, u32[]{:S(2)}) %copy-start) | copy-done | bytes 262168
  1.0 0.1 units.1.unit
  1.1 0.0 copy-start.2
  1.1 0.0 copy-start.3
  1.1 0.6 %copy-done.2 = s32[128]{0:T(128)S(1)} copy-done((s32[128]{0:T(128)S(1)}, s32[128]{0:T(128)}, u32[]{:S(2)}) %copy-start.2) | copy-done | bytes 536
  1.7 0.0 copy-done.3
  1.8 6.5 %collective-permute-start.6 = (bf16[528,128]{1,0:T(8,128)(2,1)S(1)}, bf16[528,128]{1,0:T(8,128)(2,1)S(1)}, u32[]{:S(2)}, u32[]{:S(2)}) collective-permute-start(bf16[528,128]{1,0:T(8,128)(2,1)S(1)} %pack.1.refs_3_.refs_0_), channel_id=1, source_target_pairs={{0,8},{1,201},{8,0},{9,65},{64,72},{65,9},{72,64},{73,129},{128,13... | collective-permute-start | bytes 405512 | tf_op jit(solution)/shard_map/ppermute | solution.py:45
  8.3 4.9 %collective-permute-start = (bf16[528,128]{1,0:T(8,128)(2,1)S(1)}, bf16[528,128]{1,0:T(8,128)(2,1)S(1)}, u32[]{:S(2)}, u32[]{:S(2)}) collective-permute-start(bf16[528,128]{1,0:T(8,128)(2,1)S(1)} %pack.1.refs_3_.refs_0_), channel_id=1, source_target_pairs={{0,18},{1,55},{8,26},{9,63},{64,82},{65,119},{72,90},{73,127},{128... | collective-permute-start | bytes 405512 | tf_op jit(solution)/shard_map/ppermute | solution.py:45
  13.2 0.2 collective-permute-start.1
  13.4 0.1 collective-permute-start.2
  13.5 0.0 collective-permute-done.6.refs_1_.refs_0_
  13.5 0.1 collective-permute-start.7
  13.6 2.0 %collective-permute-done.refs_0_ = bf16[528,128]{1,0:T(8,128)(2,1)S(1)} collective-permute-done((bf16[528,128]{1,0:T(8,128)(2,1)S(1)}, bf16[528,128]{1,0:T(8,128)(2,1)S(1)}, u32[]{:S(2)}, u32[]{:S(2)}) %collective-permute-start) | collective-permute-done | bytes 135200 | tf_op jit(solution)/shard_map/ppermute | solution.py:45
  15.6 2.8 %collective-permute-done.1.refs_1_ = bf16[528,128]{1,0:T(8,128)(2,1)S(1)} collective-permute-done((bf16[528,128]{1,0:T(8,128)(2,1)S(1)}, bf16[528,128]{1,0:T(8,128)(2,1)S(1)}, u32[]{:S(2)}, u32[]{:S(2)}) %collective-permute-start.1) | collective-permute-done | bytes 135200 | tf_op jit(solution)/shard_map/ppermute | solution.py:45
  18.3 0.1 collective-permute-done.2.refs_2_
  18.5 0.4 collective-permute-start.3
  18.9 0.0 collective-permute-start.4
  18.9 2.4 %collective-permute-start.5 = (bf16[2064,128]{1,0:T(8,128)(2,1)S(1)}, bf16[2064,128]{1,0:T(8,128)(2,1)S(1)}, u32[]{:S(2)}, u32[]{:S(2)}) collective-permute-start(bf16[2064,128]{1,0:T(8,128)(2,1)S(1)} %join.2.refs_1_.refs_2_), channel_id=1, source_target_pairs={{0,54},{1,19},{8,62},{9,27},{64,118},{65,83},{72,126},{73,91},{128... | collective-permute-start | bytes 1585160 | tf_op jit(solution)/shard_map/ppermute | solution.py:45
  21.2 0.0 collective-permute-done.7.refs_1_
  21.2 1.2 %collective-permute-start.9 = (bf16[1040,128]{1,0:T(8,128)(2,1)S(1)}, bf16[1040,128]{1,0:T(8,128)(2,1)S(1)}, u32[]{:S(2)}, u32[]{:S(2)}) collective-permute-start(bf16[1040,128]{1,0:T(8,128)(2,1)S(1)} %collective-permute-done.7.refs_1_), channel_id=1, source_target_pairs={{0,64},{1,193},{8,200},{9,73},{64,128},{65,1},{72,8},{73,137},{128... | collective-permute-start | bytes 798728 | tf_op jit(solution)/shard_map/ppermute | solution.py:53
  22.4 0.0 collective-permute-start.8
  22.4 4.5 %collective-permute-done.3.refs_2_.refs_3_ = bf16[2064,128]{1,0:T(8,128)(2,1)S(1)} collective-permute-done((bf16[2064,128]{1,0:T(8,128)(2,1)S(1)}, bf16[2064,128]{1,0:T(8,128)(2,1)S(1)}, u32[]{:S(2)}, u32[]{:S(2)}) %collective-permute-start.3) | collective-permute-done | bytes 528416 | tf_op jit(solution)/shard_map/ppermute | solution.py:45
  27.0 0.0 collective-permute-start.10
  27.0 3.3 %collective-permute-done.9.refs_0_ = bf16[1040,128]{1,0:T(8,128)(2,1)S(1)} collective-permute-done((bf16[1040,128]{1,0:T(8,128)(2,1)S(1)}, bf16[1040,128]{1,0:T(8,128)(2,1)S(1)}, u32[]{:S(2)}, u32[]{:S(2)}) %collective-permute-start.9) | collective-permute-done | bytes 266272 | tf_op jit(solution)/shard_map/ppermute | solution.py:53
  30.3 0.9 %collective-permute-start.11 = (bf16[2064,128]{1,0:T(8,128)(2,1)S(1)}, bf16[2064,128]{1,0:T(8,128)(2,1)S(1)}, u32[]{:S(2)}, u32[]{:S(2)}) collective-permute-start(bf16[2064,128]{1,0:T(8,128)(2,1)S(1)} %collective-permute-done.3.refs_2_.refs_3_), channel_id=1, source_target_pairs={{0,1},{1,0},{2,3},{3,2},{4,5},{5,4},{6,7},{7,6},{8,9},{9,8},{10,11... | collective-permute-start | bytes 1585160 | tf_op jit(solution)/shard_map/ppermute | solution.py:57
  31.2 0.8 %pair.6.refs_5_ = f32[256,512]{1,0:T(8,128)S(1)} custom-call(bf16[1040,128]{1,0:T(8,128)(2,1)S(1)} %collective-permute-done.9.refs_0_, bf16[2064,128]{1,0:T(8,128)(2,1)S(1)} %join.2.refs_1_.refs_2_, bf16[2064,128]{1,0:T(8,128)(2,1)S(1)} %collective-permute-done.3.refs_2_.refs_3_), custom_call_target="tpu_custom_call" | custom-call | flops 536870912 | bytes 1310720 | tf_op jit(solution)/shard_map/pair/pallas_call | solution.py:144
  31.9 1.0 %collective-permute-done.4.refs_3_.refs_4_.refs_1_ = bf16[2064,128]{1,0:T(8,128)(2,1)S(1)} collective-permute-done((bf16[2064,128]{1,0:T(8,128)(2,1)S(1)}, bf16[2064,128]{1,0:T(8,128)(2,1)S(1)}, u32[]{:S(2)}, u32[]{:S(2)}) %collective-permute-start.4) | collective-permute-done | bytes 528416 | tf_op jit(solution)/shard_map/ppermute | solution.py:45
  32.9 0.0 collective-permute-done.5.refs_4_.refs_5_.refs_2_
  32.9 0.0 collective-permute-done.8.refs_0_
  32.9 0.9 %collective-permute-start.12 = (bf16[2064,128]{1,0:T(8,128)(2,1)S(1)}, bf16[2064,128]{1,0:T(8,128)(2,1)S(1)}, u32[]{:S(2)}, u32[]{:S(2)}) collective-permute-start(bf16[2064,128]{1,0:T(8,128)(2,1)S(1)} %collective-permute-done.4.refs_3_.refs_4_.refs_1_), channel_id=1, source_target_pairs={{0,1},{1,0},{2,3},{3,2},{4,5},{5,4},{6,7},{7,6},{8,9},{9,8},{10,11... | collective-permute-start | bytes 1585160 | tf_op jit(solution)/shard_map/ppermute | solution.py:57
  33.9 0.0 collective-permute-start.13
  33.9 0.0 collective-permute-done.10.refs_5_.refs_6_.refs_3_
  33.9 0.0 collective-permute-done.11.refs_6_.refs_7_.refs_4_
  33.9 1.3 %pair.10.refs_3_ = f32[256,512]{1,0:T(8,128)S(1)} custom-call(bf16[1040,128]{1,0:T(8,128)(2,1)S(1)} %collective-permute-done.9.refs_0_, bf16[2064,128]{1,0:T(8,128)(2,1)S(1)} %collective-permute-done.4.refs_3_.refs_4_.refs_1_, bf16[2064,128]{1,0:T(8,128)(2,1)S(1)} %collective-permute-done.5.refs_4_.refs_5_.refs_2_, ...), custom_call_target="tpu_custom_call" | custom-call | flops 1073741824 | bytes 2359296 | tf_op jit(solution)/shard_map/pair/pallas_call | solution.py:144
  35.2 0.2 collective-permute-done.12.refs_7_.refs_8_.refs_1_
  35.4 0.8 %collective-permute-done.13.refs_8_.refs_9_.refs_2_ = bf16[2064,128]{1,0:T(8,128)(2,1)S(1)} collective-permute-done((bf16[2064,128]{1,0:T(8,128)(2,1)S(1)}, bf16[2064,128]{1,0:T(8,128)(2,1)S(1)}, u32[]{:S(2)}, u32[]{:S(2)}) %collective-permute-start.13) | collective-permute-done | bytes 528416 | tf_op jit(solution)/shard_map/ppermute | solution.py:57
  36.2 0.7 %pair.11 = bf16[256,512]{1,0:T(8,128)(2,1)S(1)} custom-call(bf16[1040,128]{1,0:T(8,128)(2,1)S(1)} %collective-permute-done.9.refs_0_, bf16[2064,128]{1,0:T(8,128)(2,1)S(1)} %collective-permute-done.12.refs_7_.refs_8_.refs_1_, bf16[2064,128]{1,0:T(8,128)(2,1)S(1)} %collective-permute-done.13.refs_8_.refs_9_.refs_2_, f32[256,512]{1,0:T(8,128)S(1)} %pair.10.refs_3_), custom_call_target="tpu_custom_call" | custom-call | flops 536870912 | bytes 1310720 | tf_op jit(solution)/shard_map/pair/pallas_call | solution.py:144
  36.9 0.3 collective-permute-start.15
  37.2 4.6 %pair.9 = (f32[256,512]{1,0:T(8,128)S(1)}, f32[256,512]{1,0:T(8,128)S(1)}) custom-call(bf16[1040,128]{1,0:T(8,128)(2,1)S(1)} %collective-permute-done.8.refs_0_, bf16[1040,128]{1,0:T(8,128)(2,1)S(1)} %collective-permute-done.7.refs_1_, bf16[2064,128]{1,0:T(8,128)(2,1)S(1)} %join.2.refs_1_.refs_2_, ...), custom_call_target="tpu_custom_call" | custom-call | flops 4294967296 | bytes 4718592 | tf_op jit(solution)/shard_map/pair/pallas_call | solution.py:144
  41.8 0.9 %collective-permute-done.15 = bf16[256,512]{1,0:T(8,128)(2,1)S(1)} collective-permute-done((bf16[256,512]{1,0:T(8,128)(2,1)S(1)}, bf16[256,512]{1,0:T(8,128)(2,1)S(1)}, u32[]{:S(2)}, u32[]{:S(2)}) %collective-permute-start.15) | collective-permute-done | bytes 262176 | tf_op jit(solution)/shard_map/ppermute | solution.py:45
  42.7 0.1 add_convert_fusion.1
  42.8 3.2 %collective-permute-start.16 = (bf16[256,512]{1,0:T(8,128)(2,1)S(1)}, bf16[256,512]{1,0:T(8,128)(2,1)S(1)}, u32[]{:S(2)}, u32[]{:S(2)}) collective-permute-start(bf16[256,512]{1,0:T(8,128)(2,1)S(1)} %add_convert_fusion.1), channel_id=1, source_target_pairs={{0,8},{1,201},{8,0},{9,65},{64,72},{65,9},{72,64},{73,129},{128,13... | collective-permute-start | bytes 786440 | tf_op jit(solution)/shard_map/ppermute | solution.py:45
  46.0 2.2 %pair.8 = bf16[128,512]{1,0:T(8,128)(2,1)S(1)} custom-call(bf16[528,128]{1,0:T(8,128)(2,1)S(1)} %collective-permute-done.6.refs_1_.refs_0_, bf16[2064,128]{1,0:T(8,128)(2,1)S(1)} %join.2.refs_1_.refs_2_, bf16[2064,128]{1,0:T(8,128)(2,1)S(1)} %collective-permute-done.3.refs_2_.refs_3_, bf16[2064,128]{1,0:T(8,128)(2,1)S(1)} %collective-permute-done.4.refs_3_.refs_4_.refs_1_, ...), custom_call_target="tpu_custom_call" | custom-call | flops 1073741824 | bytes 4325376 | tf_op jit(solution)/shard_map/pair/pallas_call | solution.py:144
  48.2 0.1 collective-permute-start.14
  48.3 1.5 %collective-permute-done.16 = bf16[256,512]{1,0:T(8,128)(2,1)S(1)} collective-permute-done((bf16[256,512]{1,0:T(8,128)(2,1)S(1)}, bf16[256,512]{1,0:T(8,128)(2,1)S(1)}, u32[]{:S(2)}, u32[]{:S(2)}) %collective-permute-start.16) | collective-permute-done | bytes 262176 | tf_op jit(solution)/shard_map/ppermute | solution.py:45
  49.8 0.1 add_convert_fusion
  49.9 0.2 collective-permute-start.17
  50.0 0.0 copy-start.1
  50.0 3.8 %collective-permute-start.18 = (bf16[128,512]{1,0:T(8,128)(2,1)S(1)}, bf16[128,512]{1,0:T(8,128)(2,1)S(1)}, u32[]{:S(2)}, u32[]{:S(2)}) collective-permute-start(bf16[128,512]{1,0:T(8,128)(2,1)S(1)} %get-tuple-element.17), channel_id=1, source_target_pairs={{0,200},{1,9},{8,64},{9,1},{64,8},{65,73},{72,128},{73,65},{128,72... | collective-permute-start | bytes 393224 | tf_op jit(solution)/shard_map/ppermute | solution.py:45
  53.8 2.1 %pair.7.own = f32[128,512]{1,0:T(8,128)S(1)} custom-call(bf16[528,128]{1,0:T(8,128)(2,1)S(1)} %pack.1.refs_3_.refs_0_, bf16[2064,128]{1,0:T(8,128)(2,1)S(1)} %join.2.refs_1_.refs_2_, bf16[2064,128]{1,0:T(8,128)(2,1)S(1)} %collective-permute-done.3.refs_2_.refs_3_, bf16[2064,128]{1,0:T(8,128)(2,1)S(1)} %collective-permute-done.4.refs_3_.refs_4_.refs_1_, ...), custom_call_target="tpu_custom_call" | custom-call | flops 1073741824 | bytes 4325376 | tf_op jit(solution)/shard_map/pair/pallas_call | solution.py:144
  56.0 0.0 collective-permute-done.14.refs_0_
  56.0 0.7 %collective-permute-done.17.refs_1_ = bf16[128,512]{1,0:T(8,128)(2,1)S(1)} collective-permute-done((bf16[128,512]{1,0:T(8,128)(2,1)S(1)}, bf16[128,512]{1,0:T(8,128)(2,1)S(1)}, u32[]{:S(2)}, u32[]{:S(2)}) %collective-permute-start.17) | collective-permute-done | bytes 131104 | tf_op jit(solution)/shard_map/ppermute | solution.py:53
  56.7 2.5 %collective-permute-done.18.refs_2_ = bf16[128,512]{1,0:T(8,128)(2,1)S(1)} collective-permute-done((bf16[128,512]{1,0:T(8,128)(2,1)S(1)}, bf16[128,512]{1,0:T(8,128)(2,1)S(1)}, u32[]{:S(2)}, u32[]{:S(2)}) %collective-permute-start.18) | collective-permute-done | bytes 131104 | tf_op jit(solution)/shard_map/ppermute | solution.py:45
  59.3 0.0 copy-done.1
  59.3 0.9 %final.1 = f32[128,512]{1,0:T(8,128)} custom-call(f32[128,512]{1,0:T(8,128)S(1)} %copy-done.1, f32[128,512]{1,0:T(8,128)S(1)} %pair.7.own, bf16[128,512]{1,0:T(8,128)(2,1)S(1)} %collective-permute-done.14.refs_0_, bf16[128,512]{1,0:T(8,128)(2,1)S(1)} %collective-permute-done.17.refs_1_, bf16[128,512]{1,0:T(8,128)(2,1)S(1)} %collective-permute-done.18.refs_2_), custom_call_target="tpu_custom_call" | custom-call | tf_op jit(solution)/shard_map/final/pallas_call | solution.py:217
  (4 shorter events, 0.1 us)
Async XLA Ops:
  0.0 0.9 %copy-start = (f32[128,512]{1,0:T(8,128)S(1)}, f32[128,512]{1,0:T(8,128)}, u32[]{:S(2)}) copy-start(f32[128,512]{1,0:T(8,128)} %emb.3) | copy-start | bytes 786436
  1.1 0.7 %copy-start.2 = (s32[128]{0:T(128)S(1)}, s32[128]{0:T(128)}, u32[]{:S(2)}) copy-start(s32[128]{0:T(128)} %param.4) | copy-start | bytes 1540
  1.1 0.7 %copy-start.3 = (s32[128]{0:T(128)S(1)}, s32[128]{0:T(128)}, u32[]{:S(2)}) copy-start(s32[128]{0:T(128)} %param.5) | copy-start | bytes 1540
  1.8 11.7 %collective-permute-start.6 = (bf16[528,128]{1,0:T(8,128)(2,1)S(1)}, bf16[528,128]{1,0:T(8,128)(2,1)S(1)}, u32[]{:S(2)}, u32[]{:S(2)}) collective-permute-start(bf16[528,128]{1,0:T(8,128)(2,1)S(1)} %pack.1.refs_3_.refs_0_), channel_id=1, source_target_pairs={{0,8},{1,201},{8,0},{9,65},{64,72},{65,9},{72,64},{73,129},{128,13... | collective-permute-start | bytes 405512 | tf_op jit(solution)/shard_map/ppermute | solution.py:45
  8.3 7.3 %collective-permute-start = (bf16[528,128]{1,0:T(8,128)(2,1)S(1)}, bf16[528,128]{1,0:T(8,128)(2,1)S(1)}, u32[]{:S(2)}, u32[]{:S(2)}) collective-permute-start(bf16[528,128]{1,0:T(8,128)(2,1)S(1)} %pack.1.refs_3_.refs_0_), channel_id=1, source_target_pairs={{0,18},{1,55},{8,26},{9,63},{64,82},{65,119},{72,90},{73,127},{128... | collective-permute-start | bytes 405512 | tf_op jit(solution)/shard_map/ppermute | solution.py:45
  13.2 5.2 %collective-permute-start.1 = (bf16[528,128]{1,0:T(8,128)(2,1)S(1)}, bf16[528,128]{1,0:T(8,128)(2,1)S(1)}, u32[]{:S(2)}, u32[]{:S(2)}) collective-permute-start(bf16[528,128]{1,0:T(8,128)(2,1)S(1)} %pack.1.refs_3_.refs_0_), channel_id=1, source_target_pairs={{0,16},{1,49},{8,24},{9,57},{64,80},{65,113},{72,88},{73,121},{128... | collective-permute-start | bytes 405512 | tf_op jit(solution)/shard_map/ppermute | solution.py:45
  13.4 5.1 %collective-permute-start.2 = (bf16[528,128]{1,0:T(8,128)(2,1)S(1)}, bf16[528,128]{1,0:T(8,128)(2,1)S(1)}, u32[]{:S(2)}, u32[]{:S(2)}) collective-permute-start(bf16[528,128]{1,0:T(8,128)(2,1)S(1)} %pack.1.refs_3_.refs_0_), channel_id=1, source_target_pairs={{0,2},{1,7},{8,10},{9,15},{64,66},{65,71},{72,74},{73,79},{128,130... | collective-permute-start | bytes 405512 | tf_op jit(solution)/shard_map/ppermute | solution.py:45
  13.5 7.7 %collective-permute-start.7 = (bf16[1040,128]{1,0:T(8,128)(2,1)S(1)}, bf16[1040,128]{1,0:T(8,128)(2,1)S(1)}, u32[]{:S(2)}, u32[]{:S(2)}) collective-permute-start(bf16[1040,128]{1,0:T(8,128)(2,1)S(1)} %join.3), channel_id=1, source_target_pairs={{0,200},{1,9},{8,64},{9,1},{64,8},{65,73},{72,128},{73,65},{128,72... | collective-permute-start | bytes 798728 | tf_op jit(solution)/shard_map/ppermute | solution.py:45
  18.5 8.5 %collective-permute-start.3 = (bf16[2064,128]{1,0:T(8,128)(2,1)S(1)}, bf16[2064,128]{1,0:T(8,128)(2,1)S(1)}, u32[]{:S(2)}, u32[]{:S(2)}) collective-permute-start(bf16[2064,128]{1,0:T(8,128)(2,1)S(1)} %join.2.refs_1_.refs_2_), channel_id=1, source_target_pairs={{0,48},{1,17},{8,56},{9,25},{64,112},{65,81},{72,120},{73,89},{128... | collective-permute-start | bytes 1585160 | tf_op jit(solution)/shard_map/ppermute | solution.py:45
  18.9 14.0 %collective-permute-start.4 = (bf16[2064,128]{1,0:T(8,128)(2,1)S(1)}, bf16[2064,128]{1,0:T(8,128)(2,1)S(1)}, u32[]{:S(2)}, u32[]{:S(2)}) collective-permute-start(bf16[2064,128]{1,0:T(8,128)(2,1)S(1)} %join.2.refs_1_.refs_2_), channel_id=1, source_target_pairs={{0,6},{1,3},{8,14},{9,11},{64,70},{65,67},{72,78},{73,75},{128,134... | collective-permute-start | bytes 1585160 | tf_op jit(solution)/shard_map/ppermute | solution.py:45
  18.9 14.0 %collective-permute-start.5 = (bf16[2064,128]{1,0:T(8,128)(2,1)S(1)}, bf16[2064,128]{1,0:T(8,128)(2,1)S(1)}, u32[]{:S(2)}, u32[]{:S(2)}) collective-permute-start(bf16[2064,128]{1,0:T(8,128)(2,1)S(1)} %join.2.refs_1_.refs_2_), channel_id=1, source_target_pairs={{0,54},{1,19},{8,62},{9,27},{64,118},{65,83},{72,126},{73,91},{128... | collective-permute-start | bytes 1585160 | tf_op jit(solution)/shard_map/ppermute | solution.py:45
  21.2 9.0 %collective-permute-start.9 = (bf16[1040,128]{1,0:T(8,128)(2,1)S(1)}, bf16[1040,128]{1,0:T(8,128)(2,1)S(1)}, u32[]{:S(2)}, u32[]{:S(2)}) collective-permute-start(bf16[1040,128]{1,0:T(8,128)(2,1)S(1)} %collective-permute-done.7.refs_1_), channel_id=1, source_target_pairs={{0,64},{1,193},{8,200},{9,73},{64,128},{65,1},{72,8},{73,137},{128... | collective-permute-start | bytes 798728 | tf_op jit(solution)/shard_map/ppermute | solution.py:53
  22.4 10.5 %collective-permute-start.8 = (bf16[1040,128]{1,0:T(8,128)(2,1)S(1)}, bf16[1040,128]{1,0:T(8,128)(2,1)S(1)}, u32[]{:S(2)}, u32[]{:S(2)}) collective-permute-start(bf16[1040,128]{1,0:T(8,128)(2,1)S(1)} %collective-permute-done.7.refs_1_), channel_id=1, source_target_pairs={{0,8},{1,201},{8,0},{9,65},{64,72},{65,9},{72,64},{73,129},{128,13... | collective-permute-start | bytes 798728 | tf_op jit(solution)/shard_map/ppermute | solution.py:45
  27.0 6.9 %collective-permute-start.10 = (bf16[2064,128]{1,0:T(8,128)(2,1)S(1)}, bf16[2064,128]{1,0:T(8,128)(2,1)S(1)}, u32[]{:S(2)}, u32[]{:S(2)}) collective-permute-start(bf16[2064,128]{1,0:T(8,128)(2,1)S(1)} %join.2.refs_1_.refs_2_), channel_id=1, source_target_pairs={{0,1},{1,0},{2,3},{3,2},{4,5},{5,4},{6,7},{7,6},{8,9},{9,8},{10,11... | collective-permute-start | bytes 1585160 | tf_op jit(solution)/shard_map/ppermute | solution.py:57
  30.3 3.6 %collective-permute-start.11 = (bf16[2064,128]{1,0:T(8,128)(2,1)S(1)}, bf16[2064,128]{1,0:T(8,128)(2,1)S(1)}, u32[]{:S(2)}, u32[]{:S(2)}) collective-permute-start(bf16[2064,128]{1,0:T(8,128)(2,1)S(1)} %collective-permute-done.3.refs_2_.refs_3_), channel_id=1, source_target_pairs={{0,1},{1,0},{2,3},{3,2},{4,5},{5,4},{6,7},{7,6},{8,9},{9,8},{10,11... | collective-permute-start | bytes 1585160 | tf_op jit(solution)/shard_map/ppermute | solution.py:57
  32.9 2.5 %collective-permute-start.12 = (bf16[2064,128]{1,0:T(8,128)(2,1)S(1)}, bf16[2064,128]{1,0:T(8,128)(2,1)S(1)}, u32[]{:S(2)}, u32[]{:S(2)}) collective-permute-start(bf16[2064,128]{1,0:T(8,128)(2,1)S(1)} %collective-permute-done.4.refs_3_.refs_4_.refs_1_), channel_id=1, source_target_pairs={{0,1},{1,0},{2,3},{3,2},{4,5},{5,4},{6,7},{7,6},{8,9},{9,8},{10,11... | collective-permute-start | bytes 1585160 | tf_op jit(solution)/shard_map/ppermute | solution.py:57
  33.9 2.3 %collective-permute-start.13 = (bf16[2064,128]{1,0:T(8,128)(2,1)S(1)}, bf16[2064,128]{1,0:T(8,128)(2,1)S(1)}, u32[]{:S(2)}, u32[]{:S(2)}) collective-permute-start(bf16[2064,128]{1,0:T(8,128)(2,1)S(1)} %collective-permute-done.5.refs_4_.refs_5_.refs_2_), channel_id=1, source_target_pairs={{0,1},{1,0},{2,3},{3,2},{4,5},{5,4},{6,7},{7,6},{8,9},{9,8},{10,11... | collective-permute-start | bytes 1585160 | tf_op jit(solution)/shard_map/ppermute | solution.py:57
  36.9 5.8 %collective-permute-start.15 = (bf16[256,512]{1,0:T(8,128)(2,1)S(1)}, bf16[256,512]{1,0:T(8,128)(2,1)S(1)}, u32[]{:S(2)}, u32[]{:S(2)}) collective-permute-start(bf16[256,512]{1,0:T(8,128)(2,1)S(1)} %pair.11), channel_id=1, source_target_pairs={{0,200},{1,9},{8,64},{9,1},{64,8},{65,73},{72,128},{73,65},{128,72... | collective-permute-start | bytes 786440 | tf_op jit(solution)/shard_map/ppermute | solution.py:45
  42.8 7.0 %collective-permute-start.16 = (bf16[256,512]{1,0:T(8,128)(2,1)S(1)}, bf16[256,512]{1,0:T(8,128)(2,1)S(1)}, u32[]{:S(2)}, u32[]{:S(2)}) collective-permute-start(bf16[256,512]{1,0:T(8,128)(2,1)S(1)} %add_convert_fusion.1), channel_id=1, source_target_pairs={{0,8},{1,201},{8,0},{9,65},{64,72},{65,9},{72,64},{73,129},{128,13... | collective-permute-start | bytes 786440 | tf_op jit(solution)/shard_map/ppermute | solution.py:45
  48.2 7.8 %collective-permute-start.14 = (bf16[128,512]{1,0:T(8,128)(2,1)S(1)}, bf16[128,512]{1,0:T(8,128)(2,1)S(1)}, u32[]{:S(2)}, u32[]{:S(2)}) collective-permute-start(bf16[128,512]{1,0:T(8,128)(2,1)S(1)} %pair.8), channel_id=1, source_target_pairs={{0,8},{1,201},{8,0},{9,65},{64,72},{65,9},{72,64},{73,129},{128,13... | collective-permute-start | bytes 393224 | tf_op jit(solution)/shard_map/ppermute | solution.py:45
  49.9 6.8 %collective-permute-start.17 = (bf16[128,512]{1,0:T(8,128)(2,1)S(1)}, bf16[128,512]{1,0:T(8,128)(2,1)S(1)}, u32[]{:S(2)}, u32[]{:S(2)}) collective-permute-start(bf16[128,512]{1,0:T(8,128)(2,1)S(1)} %get-tuple-element.18), channel_id=1, source_target_pairs={{0,192},{1,65},{8,72},{9,201},{64,0},{65,129},{72,136},{73,9},{128... | collective-permute-start | bytes 393224 | tf_op jit(solution)/shard_map/ppermute | solution.py:53
  50.0 9.2 %copy-start.1 = (f32[128,512]{1,0:T(8,128)S(1)}, f32[128,512]{1,0:T(8,128)}, u32[]{:S(2)}) copy-start(f32[128,512]{1,0:T(8,128)} %emb.3) | copy-start | bytes 786436
  50.0 9.2 %collective-permute-start.18 = (bf16[128,512]{1,0:T(8,128)(2,1)S(1)}, bf16[128,512]{1,0:T(8,128)(2,1)S(1)}, u32[]{:S(2)}, u32[]{:S(2)}) collective-permute-start(bf16[128,512]{1,0:T(8,128)(2,1)S(1)} %get-tuple-element.17), channel_id=1, source_target_pairs={{0,200},{1,9},{8,64},{9,1},{64,8},{65,73},{72,128},{73,65},{128,72... | collective-permute-start | bytes 393224 | tf_op jit(solution)/shard_map/ppermute | solution.py:45
